TPU v7x, 32 devices: a whole 2x2x4 slice. The times are simulated.
32 devices in a mesh: ctx: 8 (over z, x), grp: 4 (over y, core).
Axes of the slice: x: 2, y: 2, z: 4, core: 2. Of those that a mesh axis runs over, the one named last changes fastest.
Arguments:
- queries: bfloat16 [32768, 512], P(('grp', 'ctx')), parts along dimension 0, may hold values from -6 to 6
- key_vectors: bfloat16 [32768, 512], P(('grp', 'ctx')), parts along dimension 0, may hold values from -6 to 6
- value_rows: bfloat16 [32768, 512], P(('grp', 'ctx')), parts along dimension 0, may hold values from -6 to 6
- cotangent: bfloat16 [32768, 512], P(('grp', 'ctx')), parts along dimension 0, may hold values from -6 to 6
Outputs:
- attended: bfloat16 [32768, 512], P(('grp', 'ctx')), parts along dimension 0
- grad_queries: bfloat16 [32768, 512], P(('grp', 'ctx')), parts along dimension 0
- grad_keys: bfloat16 [32768, 512], P(('grp', 'ctx')), parts along dimension 0
- grad_values: bfloat16 [32768, 512], P(('grp', 'ctx')), parts along dimension 0
There are 4 independent parts, one for each index of `grp`. A program takes and returns all parts, laid end to end along the dimension named above; each array names one. Nothing has to cross between parts.
All inputs are finite; a program needn't handle non-finite values.
Results may differ from a plain program's by a relative error of at most 0.0025.
Values sent between devices are 32-bit elements; how exact they have to be, the bound alone decides.
No kernel may reach another device: no remote copies, remote signals or barrier semaphores. Data moves between devices by JAX's collectives and lax.ppermute only.
A program may use at most 128 MiB of HBM per device.

v0:
```python
import math

import jax
import jax.numpy as jnp
from jax import lax
from jax.sharding import PartitionSpec as P

DH = 128
HEADS = 4


def entering(value, axis, combine, identity, reverse):
    devices, position = (lax.axis_size(axis), lax.axis_index(axis))
    everything = lax.all_gather(value, axis)
    start = jnp.broadcast_to(jnp.asarray(identity, value.dtype), value.shape)

    def lap(k, before):
        at = devices - 1 - k if reverse else k
        reached = at > position if reverse else at < position
        new = combine(before, everything[at])
        return jnp.where(reached, new, before)

    return lax.fori_loop(0, devices, lap, start)


def inner_first(left, right):
    return lax.dot_general(
        left, right, (((0,), (0,)), ((), ())), preferred_element_type=jnp.float32
    )


def inner_last(left, right):
    return lax.dot_general(
        left, right, (((1,), (1,)), ((), ())), preferred_element_type=jnp.float32
    )


def split_state(state):
    upper = lax.optimization_barrier(state.astype(jnp.bfloat16))
    lower = (state - upper.astype(jnp.float32)).astype(jnp.bfloat16)
    return (upper, lower)


def block_states(queries, key_vectors, value_rows, cotangent):
    width = DH
    states = []
    grads = []
    for head_index in range(HEADS):
        cols = slice(head_index * width, (head_index + 1) * width)
        states.append(inner_first(key_vectors[:, cols], value_rows[:, cols]))
        grads.append(inner_first(queries[:, cols], cotangent[:, cols]))
    return (jnp.stack(states), jnp.stack(grads))


def block_outputs(queries, key_vectors, value_rows, cotangent, prefix_state, suffix_grad, factor):
    width = DH
    length = queries.shape[0]
    causal = lax.broadcasted_iota(jnp.int32, (length, length), 0) >= lax.broadcasted_iota(
        jnp.int32, (length, length), 1
    )
    results = ([], [], [], [])
    prefix_hi, prefix_lo = split_state(prefix_state)
    suffix_hi, suffix_lo = split_state(suffix_grad)
    for head_index in range(HEADS):
        cols = slice(head_index * width, (head_index + 1) * width)
        query_head = queries[:, cols]
        key_head = key_vectors[:, cols]
        value_head = value_rows[:, cols]
        cot_head = cotangent[:, cols]
        state_hi = prefix_hi[head_index]
        state_lo = prefix_lo[head_index]
        grad_hi = suffix_hi[head_index]
        grad_lo = suffix_lo[head_index]
        weights = jnp.where(causal, inner_last(query_head, key_head), 0.0).astype(jnp.bfloat16)
        back_weights = jnp.where(causal, inner_last(cot_head, value_head), 0.0).astype(jnp.bfloat16)
        attended = (
            jnp.dot(weights, value_head, preferred_element_type=jnp.float32)
            + jnp.dot(query_head, state_hi, preferred_element_type=jnp.float32)
            + jnp.dot(query_head, state_lo, preferred_element_type=jnp.float32)
        )
        grad_q = (
            jnp.dot(back_weights, key_head, preferred_element_type=jnp.float32)
            + inner_last(cot_head, state_hi)
            + inner_last(cot_head, state_lo)
        )
        grad_k = (
            inner_first(back_weights, query_head)
            + inner_last(value_head, grad_hi)
            + inner_last(value_head, grad_lo)
        )
        grad_v = (
            inner_first(weights, cot_head)
            + jnp.dot(key_head, grad_hi, preferred_element_type=jnp.float32)
            + jnp.dot(key_head, grad_lo, preferred_element_type=jnp.float32)
        )
        for target, source in zip(results, (attended, grad_q, grad_k, grad_v)):
            target.append((factor * source).astype(jnp.bfloat16))
    return tuple((jnp.concatenate(parts, axis=1) for parts in results))


def combine_sum(earlier, later):
    return jax.tree.map(jnp.add, earlier, later)


def on_device(queries, key_vectors, value_rows, cotangent):
    devices_ctx = lax.axis_size("ctx")
    length = queries.shape[0]
    factor = 1.0 / math.sqrt(DH * length * devices_ctx)
    states_local, grads_local = block_states(queries, key_vectors, value_rows, cotangent)
    zeros_state = jnp.zeros_like(states_local)
    prefix_state = entering(states_local, "ctx", combine_sum, zeros_state, False)
    suffix_grad = entering(grads_local, "ctx", combine_sum, zeros_state, True)
    return block_outputs(
        queries, key_vectors, value_rows, cotangent, prefix_state, suffix_grad, factor
    )


def solution(mesh):
    in_specs = (
        P(("grp", "ctx"), None),
        P(("grp", "ctx"), None),
        P(("grp", "ctx"), None),
        P(("grp", "ctx"), None),
    )
    out_specs = (
        P(("grp", "ctx"), None),
        P(("grp", "ctx"), None),
        P(("grp", "ctx"), None),
        P(("grp", "ctx"), None),
    )
    return jax.shard_map(
        on_device, mesh=mesh, in_specs=in_specs, out_specs=out_specs, check_vma=False
    )
```

profile of v0, /device:TPU:0, one launch (start us, length us, event | category | flops | bytes accessed | tf_op | source)
XLA Modules:
  0.0 151.7 jit_solution(14088489888357031054)
XLA Ops:
  7.2 1.4 convolution_bitcast_fusion.35
  17.8 1.6 %fusion.133 = f32[1024,128]{0,1:T(8,128)} fusion(bf16[1024,1024]{1,0:T(8,128)(2,1)S(1)} %select_convert_fusion.6, bf16[1024,512]{1,0:T(8,128)(2,1)S(1)} %copy-done.10), kind=kOutput, calls=%fused_computation.192 | convolution fusion | flops 268435456 | bytes 2883584 | tf_op jit(solution)/shard_map/dot_general | solution.py:77
  21.5 1.6 %fusion.146 = f32[1024,128]{0,1:T(8,128)} fusion(bf16[1024,1024]{1,0:T(8,128)(2,1)S(1)} %select_convert_fusion.7, bf16[1024,512]{1,0:T(8,128)(2,1)S(1)} %copy-done.10), kind=kOutput, calls=%fused_computation.205 | convolution fusion | flops 268435456 | bytes 2883584 | tf_op jit(solution)/shard_map/dot_general | solution.py:77
  25.2 1.6 %fusion.109 = f32[1024,128]{0,1:T(8,128)} fusion(bf16[1024,1024]{1,0:T(8,128)(2,1)S(1)} %select_convert_fusion.4, bf16[1024,512]{1,0:T(8,128)(2,1)S(1)} %copy-done.10), kind=kOutput, calls=%fused_computation.168 | convolution fusion | flops 268435456 | bytes 2883584 | tf_op jit(solution)/shard_map/dot_general | solution.py:77
  28.8 1.6 %fusion.121 = f32[1024,128]{0,1:T(8,128)} fusion(bf16[1024,1024]{1,0:T(8,128)(2,1)S(1)} %select_convert_fusion.5, bf16[1024,512]{1,0:T(8,128)(2,1)S(1)} %copy-done.10), kind=kOutput, calls=%fused_computation.180 | convolution fusion | flops 268435456 | bytes 2883584 | tf_op jit(solution)/shard_map/dot_general | solution.py:77
  31.2 1.3 fusion.155
  32.5 1.6 %fusion.150 = f32[1024,128]{0,1:T(8,128)} fusion(bf16[1024,1024]{1,0:T(8,128)(2,1)S(1)} %select_convert_fusion.3, bf16[1024,512]{1,0:T(8,128)(2,1)S(1)} %copy-done.6), kind=kOutput, calls=%fused_computation.209 | convolution fusion | flops 268435456 | bytes 2883584 | tf_op jit(solution)/shard_map/dot_general | solution.py:82
  34.9 2.1 %select_convert_fusion.1 = bf16[1024,1024]{1,0:T(8,128)(2,1)} fusion(bf16[1024,512]{1,0:T(8,128)(2,1)S(1)} %copy-done.4, bf16[1024,512]{1,0:T(8,128)(2,1)S(1)} %copy-done.10), kind=kOutput, calls=%fused_computation.3 | convolution fusion | flops 271581184 | bytes 2621440 | tf_op jit(solution)/shard_map/dot_general | solution.py:33
  37.1 1.3 fusion.100
  38.4 1.7 %select_convert_fusion = bf16[1024,1024]{1,0:T(8,128)(2,1)S(1)} fusion(bf16[1024,512]{1,0:T(8,128)(2,1)} %param.11, bf16[1024,512]{1,0:T(8,128)(2,1)S(1)} %copy-done.10), kind=kOutput, calls=%fused_computation.2 | convolution fusion | flops 271581184 | bytes 2621440 | tf_op jit(solution)/shard_map/dot_general | solution.py:33
  40.2 3.4 %fusion.138 = f32[1024,128]{0,1:T(8,128)} fusion(bf16[1024,1024]{1,0:T(8,128)(2,1)} %copy-done.1, bf16[1024,512]{1,0:T(8,128)(2,1)} %param.9), kind=kOutput, calls=%fused_computation.197 | convolution fusion | flops 268435456 | bytes 2883584 | tf_op jit(solution)/shard_map/dot_general | solution.py:82
  43.6 2.6 %fusion.94 = f32[1024,128]{0,1:T(8,128)} fusion(bf16[1024,1024]{1,0:T(8,128)(2,1)S(1)} %copy-done, bf16[1024,512]{1,0:T(8,128)(2,1)} %param.8), kind=kOutput, calls=%fused_computation.153 | convolution fusion | flops 268435456 | bytes 2883584 | tf_op jit(solution)/shard_map/dot_general | solution.py:27
  46.1 1.6 %fusion.126 = f32[1024,128]{0,1:T(8,128)} fusion(bf16[1024,1024]{1,0:T(8,128)(2,1)S(1)} %copy-done, bf16[1024,512]{1,0:T(8,128)(2,1)S(1)} %copy-done.7), kind=kOutput, calls=%fused_computation.185 | convolution fusion | flops 268435456 | bytes 2883584 | tf_op jit(solution)/shard_map/dot_general | solution.py:82
  47.8 2.2 %fusion.88 = f32[1024,128]{0,1:T(8,128)} fusion(bf16[1024,1024]{1,0:T(8,128)(2,1)S(1)} %select_convert_fusion, bf16[1024,512]{1,0:T(8,128)(2,1)} %param.8), kind=kOutput, calls=%fused_computation.147 | convolution fusion | flops 268435456 | bytes 2883584 | tf_op jit(solution)/shard_map/dot_general | solution.py:27
  50.0 1.6 %fusion.114 = f32[1024,128]{0,1:T(8,128)} fusion(bf16[1024,1024]{1,0:T(8,128)(2,1)S(1)} %select_convert_fusion, bf16[1024,512]{1,0:T(8,128)(2,1)S(1)} %copy-done.7), kind=kOutput, calls=%fused_computation.173 | convolution fusion | flops 268435456 | bytes 2883584 | tf_op jit(solution)/shard_map/dot_general | solution.py:82
  51.7 14.0 %all-gather.7.cloned.1.call-done = f32[32,128,128]{2,1,0:T(8,128)} async-done(((f32[4,128,128]{2,1,0:T(8,128)}), f32[32,128,128]{2,1,0:T(8,128)}) %all-gather.7.cloned.1.call-update) | async-done | bytes 2097168 | tf_op jit(solution)/shard_map/all_gather | solution.py:14
  65.6 8.6 %while.31 = (s32[]{:T(128)}, f32[4,128,128]{2,1,0:T(8,128)S(1)}, s32[]{:T(128)}, f32[8,4,128,128]{3,2,1,0:T(8,128)}, s32[]{:T(128)}, /*index=5*/s32[]{:T(128)}, s32[]{:T(128)}, s32[]{:T(128)}) while((s32[]{:T(128)}, f32[4,128,128]{2,1,0:T(8,128)S(1)}, s32[]{:T(128)}, f32[8,4,128,128]{3,2,1,0:T(8,128)}, s32[]{:T(128)}, ...), condition=%wide.region_3.4_spmd.clone, body=%wide.region_2.3_spmd.clone.sunk | while | flops 196616 | bytes 786595 | solution.py:23
  74.3 41.3 %all-gather.5.cloned.1.call-done = f32[32,128,128]{2,1,0:T(8,128)} async-done(((f32[4,128,128]{2,1,0:T(8,128)}), f32[32,128,128]{2,1,0:T(8,128)}) %all-gather.5.cloned.1.call-update) | async-done | bytes 2097168 | tf_op jit(solution)/shard_map/all_gather | solution.py:14
  115.6 8.6 %while.30 = (s32[]{:T(128)}, f32[4,128,128]{2,1,0:T(8,128)S(1)}, s32[]{:T(128)}, f32[8,4,128,128]{3,2,1,0:T(8,128)}, s32[]{:T(128)}, /*index=5*/s32[]{:T(128)}) while((s32[]{:T(128)}, f32[4,128,128]{2,1,0:T(8,128)S(1)}, s32[]{:T(128)}, f32[8,4,128,128]{3,2,1,0:T(8,128)}, s32[]{:T(128)}, /*index=5*/s32[]{:T(128)}) %tuple.83), condition=%wide.region_1.2_spmd.clone, body=%wide.region_0.1_spmd.clone.sunk | while | flops 196612 | bytes 786533 | solution.py:23
  131.2 1.3 copy.12
  134.0 1.3 copy.15
  135.3 1.4 fusion.23
  142.1 1.3 copy.14
  143.5 1.3 copy.13
  (154 shorter events, 47.1 us)
Async XLA Ops:
  7.2 6.3 %copy-start.9 = (bf16[1024,512]{1,0:T(8,128)(2,1)S(1)}, bf16[1024,512]{1,0:T(8,128)(2,1)}, u32[]{:S(2)}) copy-start(bf16[1024,512]{1,0:T(8,128)(2,1)} %param.10) | copy-start | bytes 3145732
  7.2 6.3 %copy-start.6 = (bf16[1024,512]{1,0:T(8,128)(2,1)S(1)}, bf16[1024,512]{1,0:T(8,128)(2,1)}, u32[]{:S(2)}) copy-start(bf16[1024,512]{1,0:T(8,128)(2,1)} %param.9) | copy-start | bytes 3145732
  7.2 58.4 %all-gather.7.cloned.1.call-start = ((), (), s32[]{:S(2)}) async-start(), calls=%async_computation.1 | async-start | bytes 2359296 | tf_op jit(solution)/shard_map/all_gather | solution.py:14
  12.6 2.7 %copy-start.2 = (bf16[1024,512]{1,0:T(8,128)(2,1)S(1)}, bf16[1024,512]{1,0:T(8,128)(2,1)}, u32[]{:S(2)}) copy-start(bf16[1024,512]{1,0:T(8,128)(2,1)} %param.8) | copy-start | bytes 3145732
  13.4 102.2 %all-gather.5.cloned.1.call-start = ((), (), s32[]{:S(2)}) async-start(), calls=%async_computation | async-start | bytes 2359296 | tf_op jit(solution)/shard_map/all_gather | solution.py:14
  34.9 3.5 %copy-start.1 = (bf16[1024,1024]{1,0:T(8,128)(2,1)}, bf16[1024,1024]{1,0:T(8,128)(2,1)S(1)}, u32[]{:S(2)}) copy-start(bf16[1024,1024]{1,0:T(8,128)(2,1)S(1)} %select_convert_fusion.2) | copy-start | bytes 6291460
  40.2 3.4 %copy-start = (bf16[1024,1024]{1,0:T(8,128)(2,1)S(1)}, bf16[1024,1024]{1,0:T(8,128)(2,1)}, u32[]{:S(2)}) copy-start(bf16[1024,1024]{1,0:T(8,128)(2,1)} %select_convert_fusion.1) | copy-start | bytes 6291460
  43.6 2.6 %copy-start.7 = (bf16[1024,512]{1,0:T(8,128)(2,1)S(1)}, bf16[1024,512]{1,0:T(8,128)(2,1)}, u32[]{:S(2)}) copy-start(bf16[1024,512]{1,0:T(8,128)(2,1)} %param.9) | copy-start | bytes 3145732
  65.6 58.6 %copy-start.25 = (f32[1024,128]{0,1:T(8,128)S(1)}, f32[1024,128]{0,1:T(8,128)}, u32[]{:S(2)}) copy-start(f32[1024,128]{0,1:T(8,128)} %fusion.133) | copy-start | bytes 1572868
  74.3 55.3 %copy-start.29 = (bf16[4,128,128]{2,1,0:T(8,128)(2,1)}, bf16[4,128,128]{2,1,0:T(8,128)(2,1)S(1)}, u32[]{:S(2)}) copy-start(bf16[4,128,128]{2,1,0:T(8,128)(2,1)S(1)} %subtract_convert_fusion) | copy-start | bytes 393220
  115.6 8.7 %copy-start.3 = (bf16[1024,512]{1,0:T(8,128)(2,1)S(1)}, bf16[1024,512]{1,0:T(8,128)(2,1)}, u32[]{:S(2)}) copy-start(bf16[1024,512]{1,0:T(8,128)(2,1)} %param.8) | copy-start | bytes 3145732
  124.2 1.4 copy-start.19
  124.2 1.7 %copy-start.26 = (f32[1024,128]{0,1:T(8,128)S(1)}, f32[1024,128]{0,1:T(8,128)}, u32[]{:S(2)}) copy-start(f32[1024,128]{0,1:T(8,128)} %fusion.146) | copy-start | bytes 1572868
  124.2 6.4 %copy-start.27 = (bf16[4,128,128]{2,1,0:T(8,128)(2,1)}, bf16[4,128,128]{2,1,0:T(8,128)(2,1)S(1)}, u32[]{:S(2)}) copy-start(bf16[4,128,128]{2,1,0:T(8,128)(2,1)S(1)} %convert_element_type.91) | copy-start | bytes 393220
  124.3 6.6 %copy-start.31 = (bf16[4,128,128]{2,1,0:T(8,128)(2,1)}, bf16[4,128,128]{2,1,0:T(8,128)(2,1)S(1)}, u32[]{:S(2)}) copy-start(bf16[4,128,128]{2,1,0:T(8,128)(2,1)S(1)} %subtract_convert_fusion.1) | copy-start | bytes 393220
  126.4 2.5 %copy-start.24 = (f32[1024,128]{0,1:T(8,128)S(1)}, f32[1024,128]{0,1:T(8,128)}, u32[]{:S(2)}) copy-start(f32[1024,128]{0,1:T(8,128)} %fusion.109) | copy-start | bytes 1572868
  126.9 2.4 %copy-start.17 = (f32[1024,128]{0,1:T(8,128)S(1)}, f32[1024,128]{0,1:T(8,128)}, u32[]{:S(2)}) copy-start(f32[1024,128]{0,1:T(8,128)} %fusion.64) | copy-start | bytes 1572868
  128.8 1.7 %copy-start.23 = (f32[1024,128]{0,1:T(8,128)S(1)}, f32[1024,128]{0,1:T(8,128)}, u32[]{:S(2)}) copy-start(f32[1024,128]{0,1:T(8,128)} %fusion.121) | copy-start | bytes 1572868
  133.9 3.7 %copy-start.11 = (bf16[1024,512]{1,0:T(8,128)(2,1)S(1)}, bf16[1024,512]{1,0:T(8,128)(2,1)}, u32[]{:S(2)}) copy-start(bf16[1024,512]{1,0:T(8,128)(2,1)} %param.10) | copy-start | bytes 3145732
  135.3 2.4 %copy-start.14 = (f32[1024,128]{0,1:T(8,128)S(1)}, f32[1024,128]{0,1:T(8,128)}, u32[]{:S(2)}) copy-start(f32[1024,128]{0,1:T(8,128)} %fusion.155) | copy-start | bytes 1572868
  135.3 2.7 %copy-start.30 = (bf16[4,128,128]{2,1,0:T(8,128)(2,1)S(1)}, bf16[4,128,128]{2,1,0:T(8,128)(2,1)}, u32[]{:S(2)}) copy-start(bf16[4,128,128]{2,1,0:T(8,128)(2,1)} %copy-done.29) | copy-start | bytes 393220
  135.3 2.9 %copy-start.22 = (f32[1024,128]{0,1:T(8,128)S(1)}, f32[1024,128]{0,1:T(8,128)}, u32[]{:S(2)}) copy-start(f32[1024,128]{0,1:T(8,128)} %fusion.138) | copy-start | bytes 1572868
  138.8 1.7 %copy-start.15 = (f32[1024,128]{0,1:T(8,128)S(1)}, f32[1024,128]{0,1:T(8,128)}, u32[]{:S(2)}) copy-start(f32[1024,128]{0,1:T(8,128)} %fusion.94) | copy-start | bytes 1572868
  139.3 1.7 %copy-start.20 = (f32[1024,128]{0,1:T(8,128)S(1)}, f32[1024,128]{0,1:T(8,128)}, u32[]{:S(2)}) copy-start(f32[1024,128]{0,1:T(8,128)} %fusion.114) | copy-start | bytes 1572868
  (15 other events, 18.7 us)
Sparse Core Ops, SparseCore 0:
  13.5 52.0 all-gather.6
  67.7 47.7 all-gather.4
where the time goes:
time: 153 us; the launch traced here: 152 us
  matrix products  55.3 us (36%)
  waiting for transfers between devices  55.3 us (36%)
  other arithmetic  18.6 us (12%)
  between operations  14.8 us (10%)
  local copies, waits for them, and re-layouts  7.19 us (5%)
    all_gather x2, waiting for transfers between devices, entering(): everything = lax.all_gather(value, axis)  55.2 us
    dot_general x16, matrix products, inner_first(): lax.dot_general(left, right, (((0,), (0,)), ((), ())), preferred_element_...  19.1 us
    select_n x16, other arithmetic, lap(): return jnp.where(reached, new, before)  16.8 us
    dot_general x24, matrix products, inner_last(): lax.dot_general(left, right, (((1,), (1,)), ((), ())), preferred_element_...  14.6 us
    dot_general x4, matrix products, block_outputs(): jnp.dot(back_weights, key_head, preferred_element_type=jnp.float32)  8.3 us
    unnamed x78, local copies, waits for them, and re-layouts  7.19 us
    dot_general x4, matrix products, block_outputs(): jnp.dot(weights, value_head, preferred_element_type=jnp.float32)  6.48 us
    dot_general x4, matrix products, block_outputs(): jnp.dot(key_head, grad_lo, preferred_element_type=jnp.float32)  3.86 us
  transfers between devices with their start and end apart: 2, of which 2 were waited for; matrix products, arithmetic and copies ran while one was open for 30% of the time, Pallas kernels for 0%

commit v1 on v0

v1 whole, which is shorter than its diff:
```python
import functools
import math

import jax
import jax.numpy as jnp
from jax import lax
from jax.experimental import pallas as pl
from jax.experimental.pallas import tpu as pltpu
from jax.sharding import PartitionSpec as P

DH = 128
HEADS = 4
CHUNK = 256
F32 = jnp.float32
BF16 = jnp.bfloat16


def mm(left, right):
    return lax.dot_general(left, right, (((1,), (0,)), ((), ())), preferred_element_type=F32)


def mm_first(left, right):
    return lax.dot_general(left, right, (((0,), (0,)), ((), ())), preferred_element_type=F32)


def mm_last(left, right):
    return lax.dot_general(left, right, (((1,), (1,)), ((), ())), preferred_element_type=F32)


def split(state):
    hi = state.astype(BF16)
    return hi, (state - hi.astype(F32)).astype(BF16)


def states_kernel(half_ref, q_ref, k_ref, v_ref, d_ref, out_ref):
    per = q_ref.shape[1] // DH
    for head in range(per):
        cols = slice(head * DH, (head + 1) * DH)
        out_ref[head] = mm_first(k_ref[:, cols], v_ref[:, cols])
        out_ref[per + head] = mm_first(q_ref[:, cols], d_ref[:, cols])


def half_states(half, queries, key_vectors, value_rows, cotangent):
    length, columns = queries.shape
    spec = pl.BlockSpec((length, columns // 2), lambda i, half_ref: (0, half_ref[0]))
    return pl.pallas_call(
        states_kernel,
        out_shape=jax.ShapeDtypeStruct((HEADS, DH, DH), F32),
        grid_spec=pltpu.PrefetchScalarGridSpec(
            num_scalar_prefetch=1,
            grid=(1,),
            in_specs=[spec] * 4,
            out_specs=pl.BlockSpec((HEADS, DH, DH), lambda i, half_ref: (0, 0, 0)),
        ),
        compiler_params=pltpu.CompilerParams(vmem_limit_bytes=40 * 2**20),
        cost_estimate=pl.CostEstimate(flops=2 * 2 * 2 * length * DH * DH, bytes_accessed=4 * length * columns, transcendentals=0),
        name="half_states",
    )(half, queries, key_vectors, value_rows, cotangent)


def final_kernel(factor, half_ref, q_ref, k_ref, v_ref, d_ref, pre_ref, suf_ref, *refs):
    att_ref, gq_ref, gk_ref, gv_ref = refs[-4:]
    length = q_ref.shape[0]
    chunks = length // CHUNK
    rows = lax.broadcasted_iota(jnp.int32, (CHUNK, CHUNK), 0)
    cols = lax.broadcasted_iota(jnp.int32, (CHUNK, CHUNK), 1)
    lower = rows >= cols
    upper = rows <= cols
    state = pre_ref[0]
    for c in range(chunks):
        at = slice(c * CHUNK, (c + 1) * CHUNK)
        q, k, v, d = q_ref[at, :], k_ref[at, :], v_ref[at, :], d_ref[at, :]
        hi, lo = split(state)
        weights = jnp.where(lower, mm_last(q, k), 0.0).astype(BF16)
        back = jnp.where(lower, mm_last(d, v), 0.0).astype(BF16)
        att = mm(weights, v) + mm(jnp.concatenate([q, q], 1), jnp.concatenate([hi, lo], 0))
        gq = mm(back, k) + mm_last(jnp.concatenate([d, d], 1), jnp.concatenate([hi, lo], 1))
        att_ref[at, :] = (factor * att).astype(BF16)
        gq_ref[at, :] = (factor * gq).astype(BF16)
        if c < chunks - 1:
            state = state + mm_first(k, v)
    state = suf_ref[0]
    for c in reversed(range(chunks)):
        at = slice(c * CHUNK, (c + 1) * CHUNK)
        q, k, v, d = q_ref[at, :], k_ref[at, :], v_ref[at, :], d_ref[at, :]
        hi, lo = split(state)
        weights = jnp.where(upper, mm_last(k, q), 0.0).astype(BF16)
        back = jnp.where(upper, mm_last(v, d), 0.0).astype(BF16)
        gk = mm(back, q) + mm_last(jnp.concatenate([v, v], 1), jnp.concatenate([hi, lo], 1))
        gv = mm(weights, d) + mm(jnp.concatenate([k, k], 1), jnp.concatenate([hi, lo], 0))
        gk_ref[at, :] = (factor * gk).astype(BF16)
        gv_ref[at, :] = (factor * gv).astype(BF16)
        if c > 0:
            state = state + mm_first(q, d)


def half_outputs(factor, half, arrays, prefix, suffix, previous=()):
    length, columns = arrays[0].shape
    per = HEADS // 2
    wide = pl.BlockSpec((length, DH), lambda i, half_ref: (0, half_ref[0] * per + i))
    state = pl.BlockSpec((1, DH, DH), lambda i, half_ref: (i, 0, 0))
    out = jax.ShapeDtypeStruct((length, columns), BF16)
    return pl.pallas_call(
        functools.partial(final_kernel, factor),
        out_shape=[out] * 4,
        grid_spec=pltpu.PrefetchScalarGridSpec(
            num_scalar_prefetch=1,
            grid=(per,),
            in_specs=[wide] * 4 + [state] * 2 + [pl.BlockSpec(memory_space=pl.ANY)] * len(previous),
            out_specs=[wide] * 4,
        ),
        input_output_aliases={7 + i: i for i in range(len(previous))},
        compiler_params=pltpu.CompilerParams(vmem_limit_bytes=40 * 2**20),
        cost_estimate=pl.CostEstimate(flops=per * 2 * 1024 * 128 * 128 * 16, bytes_accessed=8 * length * columns, transcendentals=0),
        name="half_outputs",
    )(half, *arrays, prefix, suffix, *previous)


def swap(value, bit, devices):
    return lax.ppermute(value, "ctx", [(i, i ^ bit) for i in range(devices)])


def on_device(queries, key_vectors, value_rows, cotangent):
    devices = lax.axis_size("ctx")
    length = queries.shape[0]
    factor = 1.0 / math.sqrt(DH * length * devices)
    per = HEADS // 2
    arrays = (queries, key_vectors, value_rows, cotangent)
    me = lax.axis_index("ctx")
    last = lax.rem(me, 2)
    own = jnp.reshape(last, (1,))
    other = 1 - own
    send = half_states(other, *arrays)
    got = swap(send, 1, devices)
    keep = half_states(own, *arrays)
    total = keep + got
    prefix = jnp.zeros((per, DH, DH), F32)
    suffix = prefix
    bit = 2
    while bit < devices:
        high = (me & bit) != 0
        if bit * 2 < devices:
            part = swap(total, bit, devices)
            total = total + part
            prefix = prefix + jnp.where(high, part[:per], 0.0)
            suffix = suffix + jnp.where(high, 0.0, part[per:])
        else:
            part = swap(jnp.where(high, total[per:], total[:per]), bit, devices)
            prefix = prefix + jnp.where(high, part, 0.0)
            suffix = suffix + jnp.where(high, 0.0, part)
        bit *= 2
    first = last == 0
    give_prefix = prefix + jnp.where(first, keep[:per], 0.0)
    give_suffix = suffix + jnp.where(first, 0.0, keep[per:])
    taken = swap(jnp.concatenate([give_prefix, give_suffix]), 1, devices)
    own_prefix = prefix + jnp.where(first, 0.0, got[:per])
    own_suffix = suffix + jnp.where(first, got[per:], 0.0)
    outs = half_outputs(factor, own, arrays, own_prefix, own_suffix)
    return tuple(half_outputs(factor, other, arrays, taken[:per], taken[per:], tuple(outs)))


def solution(mesh):
    spec = P(("grp", "ctx"), None)
    return jax.shard_map(
        on_device, mesh=mesh, in_specs=(spec,) * 4, out_specs=(spec,) * 4, check_vma=False
    )
```

time: 153 us -> 48.8 us (0.32)
  matrix products: 55.3 us -> 0 us
  waiting for transfers between devices: 55.3 us -> 16.8 us
  other arithmetic: 18.6 us -> 3.69 us
  between operations: 14.8 us -> 0.7 us
  Pallas kernels: 0 us -> 13.7 us
  starting transfers between devices: 0.08 us -> 8.61 us
  local copies, waits for them, and re-layouts: 7.19 us -> 4.93 us
    dot_general x64 -> x0, matrix products: 55.3 us -> none  [the longest x16 19.1 us: inner_first(): lax.dot_general(left, right, (((0,), (0,)), ((), ())), preferred_element_...]
    all_gather x2 -> x0, waiting for transfers between devices: 55.2 us -> none  [entering(): everything = lax.all_gather(value, axis)]
    ppermute x0 -> x4, waiting for transfers between devices: none -> 16.8 us  [swap(): return lax.ppermute(value, 'ctx', [(i, i ^ bit) for i in range(devices)])]
    select_n x16 -> x1, other arithmetic: 16.8 us -> 0.67 us  [on_device(): part = swap(jnp.where(high, total[per:], total[:per]), bit, devices)]
    pallas_call x0 -> x4, Pallas kernels: none -> 13.7 us  [the longest x2 12.5 us: half_outputs(): pl.pallas_call(functools.partial(final_kernel, factor), out_shape=[out] *...]
    ppermute x0 -> x4, starting transfers between devices: none -> 8.61 us  [swap(): return lax.ppermute(value, 'ctx', [(i, i ^ bit) for i in range(devices)])]
    add x0 -> x3, other arithmetic: none -> 3 us  [the longest x1 1.16 us: on_device(): own_suffix = suffix + jnp.where(first, got[per:], 0.0)]
    unnamed x78 -> x20, local copies, waits for them, and re-layouts: 7.19 us -> 4.91 us
  transfers between devices with their start and end apart: 2 -> 4, of which waited for: 2 -> 3; matrix products, arithmetic and copies ran while one was open for 30% -> 0% of each run, Pallas kernels for 0% -> 14%
where the time goes in v1:
time: 48.8 us; the launch traced here: 48.5 us
  waiting for transfers between devices  16.8 us (34%)
  Pallas kernels  13.7 us (28%)
  starting transfers between devices  8.61 us (18%)
  local copies, waits for them, and re-layouts  4.93 us (10%)
  other arithmetic  3.69 us (8%)
  between operations  0.7 us (1%)
    ppermute x4, waiting for transfers between devices, swap(): return lax.ppermute(value, 'ctx', [(i, i ^ bit) for i in range(devices)])  16.8 us
    pallas_call x2, Pallas kernels, half_outputs(): pl.pallas_call(functools.partial(final_kernel, factor), out_shape=[out] *...  12.5 us
    ppermute x4, starting transfers between devices, swap(): return lax.ppermute(value, 'ctx', [(i, i ^ bit) for i in range(devices)])  8.61 us
    unnamed x20, local copies, waits for them, and re-layouts  4.91 us
    pallas_call x2, Pallas kernels, half_states(): pl.pallas_call(states_kernel, out_shape=jax.ShapeDtypeStruct((HEADS, DH,...  1.21 us
    add x1, other arithmetic, on_device(): own_suffix = suffix + jnp.where(first, got[per:], 0.0)  1.16 us
    add x1, other arithmetic, on_device(): total = total + part  1.06 us
  transfers between devices with their start and end apart: 4, of which 3 were waited for; matrix products, arithmetic and copies ran while one was open for 0% of the time, Pallas kernels for 14%

profile of v1, /device:TPU:0, one launch (start us, length us, event | category | flops | bytes accessed | tf_op | source)
XLA Modules:
  0.0 48.5 jit_solution(11671754111006171449)
XLA Ops:
  0.6 0.0 copy-start
  0.6 1.2 %copy-done = bf16[1024,512]{1,0:T(8,128)(2,1)S(1)} copy-done((bf16[1024,512]{1,0:T(8,128)(2,1)S(1)}, bf16[1024,512]{1,0:T(8,128)(2,1)}, u32[]{:S(2)}) %copy-start) | copy-done | bytes 1048600
  1.9 1.2 %copy-done.2 = bf16[1024,512]{1,0:T(8,128)(2,1)S(1)} copy-done((bf16[1024,512]{1,0:T(8,128)(2,1)S(1)}, bf16[1024,512]{1,0:T(8,128)(2,1)}, u32[]{:S(2)}) %copy-start.2) | copy-done | bytes 1048600
  3.1 1.2 %copy-done.4 = bf16[1024,512]{1,0:T(8,128)(2,1)S(1)} copy-done((bf16[1024,512]{1,0:T(8,128)(2,1)S(1)}, bf16[1024,512]{1,0:T(8,128)(2,1)}, u32[]{:S(2)}) %copy-start.4) | copy-done | bytes 1048600
  4.3 1.2 %copy-done.6 = bf16[1024,512]{1,0:T(8,128)(2,1)S(1)} copy-done((bf16[1024,512]{1,0:T(8,128)(2,1)S(1)}, bf16[1024,512]{1,0:T(8,128)(2,1)}, u32[]{:S(2)}) %copy-start.6) | copy-done | bytes 1048600
  5.5 0.6 %half_states.3 = f32[4,128,128]{2,1,0:T(8,128)S(1)} custom-call(s32[1]{0:T(128)S(6)} %sub.3.half_ref, bf16[1024,512]{1,0:T(8,128)(2,1)S(1)} %copy-done, bf16[1024,512]{1,0:T(8,128)(2,1)S(1)} %copy-done.2, bf16[1024,512]{1,0:T(8,128)(2,1)S(1)} %copy-done.4, bf16[1024,512]{1,0:T(8,128)(2,1)S(1)} %copy-done.6), custom_call_target="tpu_custom_call" | custom-call | flops 134217728 | bytes 2097152 | tf_op jit(solution)/shard_map/half_states/pallas_call | solution.py:46
  6.2 3.0 %collective-permute-start = (f32[4,128,128]{2,1,0:T(8,128)S(1)}, f32[4,128,128]{2,1,0:T(8,128)S(1)}, u32[]{:S(2)}, u32[]{:S(2)}) collective-permute-start(f32[4,128,128]{2,1,0:T(8,128)S(1)} %half_states.3), channel_id=1, source_target_pairs={{0,4},{4,0},{8,12},{12,8},{16,20},{20,16},{24,28},{28,24},{1,5},{5... | collective-permute-start | bytes 786440 | tf_op jit(solution)/shard_map/ppermute | solution.py:120
  9.2 0.0 copy-done.1
  9.2 0.0 copy-done.3
  9.2 0.0 copy-done.5
  9.2 0.6 %half_states.2 = f32[4,128,128]{2,1,0:T(8,128)S(1)} custom-call(s32[1]{0:T(128)} %bitcast.half_ref, bf16[1024,512]{1,0:T(8,128)(2,1)S(1)} %copy-done.1, bf16[1024,512]{1,0:T(8,128)(2,1)S(1)} %copy-done.3, bf16[1024,512]{1,0:T(8,128)(2,1)S(1)} %copy-done.5, bf16[1024,512]{1,0:T(8,128)(2,1)S(1)} %copy-done.7), custom_call_target="tpu_custom_call" | custom-call | flops 134217728 | bytes 2097152 | tf_op jit(solution)/shard_map/half_states/pallas_call | solution.py:46
  9.8 5.7 %collective-permute-done = f32[4,128,128]{2,1,0:T(8,128)S(1)} collective-permute-done((f32[4,128,128]{2,1,0:T(8,128)S(1)}, f32[4,128,128]{2,1,0:T(8,128)S(1)}, u32[]{:S(2)}, u32[]{:S(2)}) %collective-permute-start) | collective-permute-done | bytes 262176 | tf_op jit(solution)/shard_map/ppermute | solution.py:120
  15.5 0.8 %add.24 = f32[4,128,128]{2,1,0:T(8,128)} add(f32[4,128,128]{2,1,0:T(8,128)S(1)} %half_states.2, f32[4,128,128]{2,1,0:T(8,128)S(1)} %collective-permute-done) | non-fusion elementwise | flops 65536 | bytes 786432 | tf_op jit(solution)/shard_map/add | solution.py:136
  16.3 1.8 %collective-permute-start.1 = (f32[4,128,128]{2,1,0:T(8,128)}, f32[4,128,128]{2,1,0:T(8,128)}, u32[]{:S(2)}, u32[]{:S(2)}) collective-permute-start(f32[4,128,128]{2,1,0:T(8,128)} %add.24), channel_id=1, source_target_pairs={{0,8},{4,12},{8,0},{12,4},{16,24},{20,28},{24,16},{28,20},{1,9},{5... | collective-permute-start | bytes 786440 | tf_op jit(solution)/shard_map/ppermute | solution.py:120
  18.1 6.0 %collective-permute-done.1 = f32[4,128,128]{2,1,0:T(8,128)} collective-permute-done((f32[4,128,128]{2,1,0:T(8,128)}, f32[4,128,128]{2,1,0:T(8,128)}, u32[]{:S(2)}, u32[]{:S(2)}) %collective-permute-start.1) | collective-permute-done | bytes 262176 | tf_op jit(solution)/shard_map/ppermute | solution.py:120
  24.1 1.1 %add.25 = f32[4,128,128]{2,1,0:T(8,128)S(1)} add(f32[4,128,128]{2,1,0:T(8,128)} %add.24, f32[4,128,128]{2,1,0:T(8,128)} %collective-permute-done.1) | non-fusion elementwise | flops 65536 | bytes 786432 | tf_op jit(solution)/shard_map/add | solution.py:144
  25.1 0.7 %slice_select_fusion.5 = f32[2,128,128]{2,1,0:T(8,128)} fusion(f32[4,128,128]{2,1,0:T(8,128)S(1)} %add.25, pred[]{:T(512)S(6)} %ne.7), kind=kLoop, calls=%fused_computation.11 | loop fusion | flops 32768 | bytes 393217 | tf_op jit(solution)/shard_map/jit(_where)/select_n | solution.py:148
  25.8 2.5 %collective-permute-start.2 = (f32[2,128,128]{2,1,0:T(8,128)}, f32[2,128,128]{2,1,0:T(8,128)S(1)}, u32[]{:S(2)}, u32[]{:S(2)}) collective-permute-start(f32[2,128,128]{2,1,0:T(8,128)} %slice_select_fusion.5), channel_id=1, source_target_pairs={{0,16},{4,20},{8,24},{12,28},{16,0},{20,4},{24,8},{28,12},{1,17},{... | collective-permute-start | bytes 393224 | tf_op jit(solution)/shard_map/ppermute | solution.py:120
  28.3 5.2 %collective-permute-done.2 = f32[2,128,128]{2,1,0:T(8,128)S(1)} collective-permute-done((f32[2,128,128]{2,1,0:T(8,128)}, f32[2,128,128]{2,1,0:T(8,128)S(1)}, u32[]{:S(2)}, u32[]{:S(2)}) %collective-permute-start.2) | collective-permute-done | bytes 131104 | tf_op jit(solution)/shard_map/ppermute | solution.py:120
  33.5 1.2 %fusion = (f32[2,128,128]{2,1,0:T(8,128)S(1)}, f32[2,128,128]{2,1,0:T(8,128)S(1)}, f32[2,128,128]{2,1,0:T(8,128)S(1)}, f32[2,128,128]{2,1,0:T(8,128)S(1)}) fusion(f32[4,128,128]{2,1,0:T(8,128)} %copy-done.9, pred[]{:T(512)S(6)} %eq.3, f32[2,128,128]{2,1,0:T(8,128)S(1)} %collective-permute-done.2, pred[]{:T(512)S(6)} %ne.7, ...), kind=kLoop, calls=%fused_computation.2 | loop fusion | flops 458752 | bytes 1441795 | tf_op jit(solution)/shard_map/add | solution.py:157
  34.7 1.3 %collective-permute-start.3 = (f32[4,128,128]{2,1,0:T(8,128)S(1)}, f32[4,128,128]{2,1,0:T(8,128)S(1)}, u32[]{:S(2)}, u32[]{:S(2)}) collective-permute-start(f32[4,128,128]{2,1,0:T(8,128)S(1)} %pad_maximum_fusion), channel_id=1, source_target_pairs={{0,4},{4,0},{8,12},{12,8},{16,20},{20,16},{24,28},{28,24},{1,5},{5... | collective-permute-start | bytes 786440 | tf_op jit(solution)/shard_map/ppermute | solution.py:120
  36.0 6.2 %half_outputs.2 = (bf16[1024,512]{1,0:T(8,128)(2,1)}, bf16[1024,512]{1,0:T(8,128)(2,1)}, bf16[1024,512]{1,0:T(8,128)(2,1)}, bf16[1024,512]{1,0:T(8,128)(2,1)}) custom-call(s32[1]{0:T(128)} %bitcast.half_ref, bf16[1024,512]{1,0:T(8,128)(2,1)S(1)} %copy-done.1, bf16[1024,512]{1,0:T(8,128)(2,1)S(1)} %copy-done.3, bf16[1024,512]{1,0:T(8,128)(2,1)S(1)} %copy-done.5, ...), custom_call_target="tpu_custom_call" | custom-call | flops 1073741824 | bytes 4194304 | tf_op jit(solution)/shard_map/half_outputs/pallas_call | solution.py:103
  42.2 0.0 collective-permute-done.3
  42.2 6.3 %half_outputs.3 = (bf16[1024,512]{1,0:T(8,128)(2,1)}, bf16[1024,512]{1,0:T(8,128)(2,1)}, bf16[1024,512]{1,0:T(8,128)(2,1)}, bf16[1024,512]{1,0:T(8,128)(2,1)}) custom-call(s32[1]{0:T(128)S(6)} %sub.3.half_ref, bf16[1024,512]{1,0:T(8,128)(2,1)S(1)} %copy-done.1, ...), custom_call_target="tpu_custom_call", output_to_operand_aliasing={{0}: (7, {}), {1}: (8, {}), {2}: (9, {}), {3}: (10, {})} | custom-call | flops 1073741824 | bytes 4194304 | tf_op jit(solution)/shard_map/half_outputs/pallas_call | solution.py:103
  (14 shorter events, 0.1 us)
Async XLA Ops:
  0.6 1.2 %copy-start = (bf16[1024,512]{1,0:T(8,128)(2,1)S(1)}, bf16[1024,512]{1,0:T(8,128)(2,1)}, u32[]{:S(2)}) copy-start(bf16[1024,512]{1,0:T(8,128)(2,1)} %q_ref.7) | copy-start | bytes 3145732
  1.9 1.2 %copy-start.2 = (bf16[1024,512]{1,0:T(8,128)(2,1)S(1)}, bf16[1024,512]{1,0:T(8,128)(2,1)}, u32[]{:S(2)}) copy-start(bf16[1024,512]{1,0:T(8,128)(2,1)} %k_ref.7) | copy-start | bytes 3145732
  3.1 1.2 %copy-start.4 = (bf16[1024,512]{1,0:T(8,128)(2,1)S(1)}, bf16[1024,512]{1,0:T(8,128)(2,1)}, u32[]{:S(2)}) copy-start(bf16[1024,512]{1,0:T(8,128)(2,1)} %v_ref.7) | copy-start | bytes 3145732
  4.3 1.2 %copy-start.6 = (bf16[1024,512]{1,0:T(8,128)(2,1)S(1)}, bf16[1024,512]{1,0:T(8,128)(2,1)}, u32[]{:S(2)}) copy-start(bf16[1024,512]{1,0:T(8,128)(2,1)} %d_ref.7) | copy-start | bytes 3145732
  5.5 3.6 %copy-start.1 = (bf16[1024,512]{1,0:T(8,128)(2,1)S(1)}, bf16[1024,512]{1,0:T(8,128)(2,1)}, u32[]{:S(2)}) copy-start(bf16[1024,512]{1,0:T(8,128)(2,1)} %q_ref.7) | copy-start | bytes 3145732
  5.5 3.6 %copy-start.3 = (bf16[1024,512]{1,0:T(8,128)(2,1)S(1)}, bf16[1024,512]{1,0:T(8,128)(2,1)}, u32[]{:S(2)}) copy-start(bf16[1024,512]{1,0:T(8,128)(2,1)} %k_ref.7) | copy-start | bytes 3145732
  5.5 3.6 %copy-start.5 = (bf16[1024,512]{1,0:T(8,128)(2,1)S(1)}, bf16[1024,512]{1,0:T(8,128)(2,1)}, u32[]{:S(2)}) copy-start(bf16[1024,512]{1,0:T(8,128)(2,1)} %v_ref.7) | copy-start | bytes 3145732
  5.5 3.6 %copy-start.7 = (bf16[1024,512]{1,0:T(8,128)(2,1)S(1)}, bf16[1024,512]{1,0:T(8,128)(2,1)}, u32[]{:S(2)}) copy-start(bf16[1024,512]{1,0:T(8,128)(2,1)} %d_ref.7) | copy-start | bytes 3145732
  6.2 9.3 %collective-permute-start = (f32[4,128,128]{2,1,0:T(8,128)S(1)}, f32[4,128,128]{2,1,0:T(8,128)S(1)}, u32[]{:S(2)}, u32[]{:S(2)}) collective-permute-start(f32[4,128,128]{2,1,0:T(8,128)S(1)} %half_states.3), channel_id=1, source_target_pairs={{0,4},{4,0},{8,12},{12,8},{16,20},{20,16},{24,28},{28,24},{1,5},{5... | collective-permute-start | bytes 786440 | tf_op jit(solution)/shard_map/ppermute | solution.py:120
  15.5 0.8 %copy-start.9 = (f32[4,128,128]{2,1,0:T(8,128)}, f32[4,128,128]{2,1,0:T(8,128)S(1)}, u32[]{:S(2)}) copy-start(f32[4,128,128]{2,1,0:T(8,128)S(1)} %collective-permute-done) | copy-start | bytes 786436
  16.3 7.8 %collective-permute-start.1 = (f32[4,128,128]{2,1,0:T(8,128)}, f32[4,128,128]{2,1,0:T(8,128)}, u32[]{:S(2)}, u32[]{:S(2)}) collective-permute-start(f32[4,128,128]{2,1,0:T(8,128)} %add.24), channel_id=1, source_target_pairs={{0,8},{4,12},{8,0},{12,4},{16,24},{20,28},{24,16},{28,20},{1,9},{5... | collective-permute-start | bytes 786440 | tf_op jit(solution)/shard_map/ppermute | solution.py:120
  25.8 7.7 %collective-permute-start.2 = (f32[2,128,128]{2,1,0:T(8,128)}, f32[2,128,128]{2,1,0:T(8,128)S(1)}, u32[]{:S(2)}, u32[]{:S(2)}) collective-permute-start(f32[2,128,128]{2,1,0:T(8,128)} %slice_select_fusion.5), channel_id=1, source_target_pairs={{0,16},{4,20},{8,24},{12,28},{16,0},{20,4},{24,8},{28,12},{1,17},{... | collective-permute-start | bytes 393224 | tf_op jit(solution)/shard_map/ppermute | solution.py:120
  28.3 7.7 %copy-start.8 = (bf16[1024,512]{1,0:T(8,128)(2,1)S(1)}, bf16[1024,512]{1,0:T(8,128)(2,1)}, u32[]{:S(2)}) copy-start(bf16[1024,512]{1,0:T(8,128)(2,1)} %d_ref.7) | copy-start | bytes 3145732
  34.7 7.5 %collective-permute-start.3 = (f32[4,128,128]{2,1,0:T(8,128)S(1)}, f32[4,128,128]{2,1,0:T(8,128)S(1)}, u32[]{:S(2)}, u32[]{:S(2)}) collective-permute-start(f32[4,128,128]{2,1,0:T(8,128)S(1)} %pad_maximum_fusion), channel_id=1, source_target_pairs={{0,4},{4,0},{8,12},{12,8},{16,20},{20,16},{24,28},{28,24},{1,5},{5... | collective-permute-start | bytes 786440 | tf_op jit(solution)/shard_map/ppermute | solution.py:120

commit v2 on v1

v2 whole, which is shorter than its diff:
```python
import functools
import math

import jax
import jax.numpy as jnp
from jax import lax
from jax.experimental import pallas as pl
from jax.experimental.pallas import tpu as pltpu
from jax.sharding import PartitionSpec as P

DH = 128
HEADS = 4
PER = HEADS // 2
CHUNK = 256
F32 = jnp.float32
BF16 = jnp.bfloat16
MIB = 2**20
VMEM = pl.BlockSpec(memory_space=pltpu.VMEM)
SMEM = pl.BlockSpec(memory_space=pltpu.SMEM)
HBM = pl.BlockSpec(memory_space=pltpu.HBM)


def mm(left, right):
    return lax.dot_general(left, right, (((1,), (0,)), ((), ())), preferred_element_type=F32)


def mm_first(left, right):
    return lax.dot_general(left, right, (((0,), (0,)), ((), ())), preferred_element_type=F32)


def mm_last(left, right):
    return lax.dot_general(left, right, (((1,), (1,)), ((), ())), preferred_element_type=F32)


def split(state):
    hi = state.astype(BF16)
    return hi, (state - hi.astype(F32)).astype(BF16)


def half_columns(half_ref):
    return pl.ds(pl.multiple_of(half_ref[0] * (PER * DH), PER * DH), PER * DH)


def states_kernel(half_ref, q_hbm, k_hbm, v_hbm, d_hbm, out_ref, q_ref, k_ref, v_ref, d_ref, sems):
    at = half_columns(half_ref)
    pairs = ((k_hbm, k_ref), (v_hbm, v_ref), (q_hbm, q_ref), (d_hbm, d_ref))
    copies = [
        pltpu.make_async_copy(source.at[:, at], target, sems.at[i])
        for i, (source, target) in enumerate(pairs)
    ]
    for copy in copies:
        copy.start()
    for pair, (left, right) in enumerate(((k_ref, v_ref), (q_ref, d_ref))):
        copies[2 * pair].wait()
        copies[2 * pair + 1].wait()
        for head in range(PER):
            cols = slice(head * DH, (head + 1) * DH)
            out_ref[pair * PER + head] = mm_first(left[:, cols], right[:, cols])


def half_states(half, arrays):
    length = arrays[0].shape[0]
    return pl.pallas_call(
        states_kernel,
        out_shape=jax.ShapeDtypeStruct((HEADS, DH, DH), F32),
        in_specs=[SMEM] + [HBM] * 4,
        out_specs=VMEM,
        scratch_shapes=[pltpu.VMEM((length, PER * DH), BF16)] * 4 + [pltpu.SemaphoreType.DMA((4,))],
        compiler_params=pltpu.CompilerParams(vmem_limit_bytes=16 * MIB),
        cost_estimate=pl.CostEstimate(flops=8 * length * DH * DH, bytes_accessed=8 * length * PER * DH, transcendentals=0),
        name="half_states",
    )(half, *arrays)


def local_kernel(half_ref, after_ref, q_ref, k_ref, v_ref, d_ref, att_ref, gq_ref, gk_ref, gv_ref, keep_ref):
    length = q_ref.shape[0]
    chunks = length // CHUNK
    rows = lax.broadcasted_iota(jnp.int32, (CHUNK, CHUNK), 0)
    cols = lax.broadcasted_iota(jnp.int32, (CHUNK, CHUNK), 1)
    lower = rows >= cols
    upper = rows <= cols
    for head in range(PER):
        columns = pl.ds(pl.multiple_of((half_ref[0] * PER + head) * DH, DH), DH)
        state = None
        for c in range(chunks):
            at = slice(c * CHUNK, (c + 1) * CHUNK)
            q, k, v, d = q_ref[at, columns], k_ref[at, columns], v_ref[at, columns], d_ref[at, columns]
            weights = jnp.where(lower, mm_last(q, k), 0.0).astype(BF16)
            back = jnp.where(lower, mm_last(d, v), 0.0).astype(BF16)
            att = mm(weights, v)
            gq = mm(back, k)
            if c:
                hi, lo = split(state)
                att += mm(jnp.concatenate([q, q], 1), jnp.concatenate([hi, lo], 0))
                gq += mm_last(jnp.concatenate([d, d], 1), jnp.concatenate([hi, lo], 1))
            att_ref[head, at, :] = att
            gq_ref[head, at, :] = gq
            new = mm_first(k, v)
            state = new if state is None else state + new
        keep_ref[head] = state
        state = None
        for c in reversed(range(chunks)):
            at = slice(c * CHUNK, (c + 1) * CHUNK)
            q, k, v, d = q_ref[at, columns], k_ref[at, columns], v_ref[at, columns], d_ref[at, columns]
            weights = jnp.where(upper, mm_last(k, q), 0.0).astype(BF16)
            back = jnp.where(upper, mm_last(v, d), 0.0).astype(BF16)
            gk = mm(back, q)
            gv = mm(weights, d)
            if c < chunks - 1:
                hi, lo = split(state)
                gk += mm_last(jnp.concatenate([v, v], 1), jnp.concatenate([hi, lo], 1))
                gv += mm(jnp.concatenate([k, k], 1), jnp.concatenate([hi, lo], 0))
            gk_ref[head, at, :] = gk
            gv_ref[head, at, :] = gv
            new = mm_first(q, d)
            state = new if state is None else state + new
        keep_ref[PER + head] = state


def local_products(half, arrays, after):
    length, columns = arrays[0].shape
    return pl.pallas_call(
        local_kernel,
        out_shape=[jax.ShapeDtypeStruct((PER, length, DH), F32)] * 4 + [jax.ShapeDtypeStruct((HEADS, DH, DH), F32)],
        in_specs=[SMEM] + [VMEM] * 5,
        out_specs=[VMEM] * 5,
        compiler_params=pltpu.CompilerParams(vmem_limit_bytes=16 * MIB),
        cost_estimate=pl.CostEstimate(
            flops=PER * 16 * length * CHUNK * DH, bytes_accessed=8 * length * columns, transcendentals=0
        ),
        name="local_products",
    )(half, after, *arrays)


def final_kernel(factor, half_ref, q_ref, k_ref, v_ref, d_ref, pre_ref, suf_ref, att_ref, gq_ref, gk_ref, gv_ref, *refs):
    outs, stage, sems = refs[-6:-2], refs[-2], refs[-1]
    copies = []
    for head in range(PER):
        columns = pl.ds(pl.multiple_of((half_ref[0] * PER + head) * DH, DH), DH)
        hi, lo = split(pre_ref[head])
        suf_hi, suf_lo = split(suf_ref[head])
        down = jnp.concatenate([hi, lo], 0)
        along = jnp.concatenate([hi, lo], 1)
        suf_down = jnp.concatenate([suf_hi, suf_lo], 0)
        suf_along = jnp.concatenate([suf_hi, suf_lo], 1)
        work = (
            (q_ref, down, mm, att_ref),
            (d_ref, along, mm_last, gq_ref),
            (v_ref, suf_along, mm_last, gk_ref),
            (k_ref, suf_down, mm, gv_ref),
        )
        for i, (source, state, product, local) in enumerate(work):
            rows = source[:, columns]
            value = product(jnp.concatenate([rows, rows], 1), state) + local[head]
            stage[i, head] = (factor * value).astype(BF16)
            copy = pltpu.make_async_copy(stage.at[i, head], outs[i].at[:, columns], sems.at[i, head])
            copy.start()
            copies.append(copy)
    for copy in copies:
        copy.wait()


def half_outputs(factor, half, arrays, prefix, suffix, local, previous=()):
    length, columns = arrays[0].shape
    out = jax.ShapeDtypeStruct((length, columns), BF16)
    return pl.pallas_call(
        functools.partial(final_kernel, factor),
        out_shape=[out] * 4,
        in_specs=[SMEM] + [VMEM] * 10 + [HBM] * len(previous),
        out_specs=[HBM] * 4,
        scratch_shapes=[pltpu.VMEM((4, PER, length, DH), BF16), pltpu.SemaphoreType.DMA((4, PER))],
        input_output_aliases={11 + i: i for i in range(len(previous))},
        compiler_params=pltpu.CompilerParams(vmem_limit_bytes=16 * MIB),
        cost_estimate=pl.CostEstimate(
            flops=PER * 16 * length * DH * DH, bytes_accessed=8 * length * columns, transcendentals=0
        ),
        name="half_outputs",
    )(half, *arrays, prefix, suffix, *local, *previous)


def add_kernel(left_ref, right_ref, out_ref):
    out_ref[...] = left_ref[...] + right_ref[...]


SMALL = pltpu.CompilerParams(vmem_limit_bytes=4 * MIB)


def add_states(left, right):
    return pl.pallas_call(
        add_kernel,
        out_shape=jax.ShapeDtypeStruct(left.shape, F32),
        in_specs=[VMEM] * 2,
        out_specs=VMEM,
        compiler_params=SMALL,
        name="add_states",
    )(left, right)


def part_kernel(high_ref, left_ref, right_ref, after_ref, out_ref):
    at = pl.ds(high_ref[0] * PER, PER)
    out_ref[...] = left_ref[at] + right_ref[at]


def add_part(high, left, right, after):
    return pl.pallas_call(
        part_kernel,
        out_shape=jax.ShapeDtypeStruct((PER, DH, DH), F32),
        in_specs=[SMEM] + [VMEM] * 3,
        out_specs=VMEM,
        compiler_params=SMALL,
        name="add_part",
    )(high, left, right, after)


def join_kernel(bits, me_ref, after_ref, keep_ref, got_ref, last_ref, *refs):
    parts, (give_ref, pre_ref, suf_ref) = refs[:-3], refs[-3:]
    me = me_ref[0]
    high = [(lax.rem(lax.div(me, bit), 2) == 1) for bit in bits]
    first = lax.rem(me, 2) == 0
    last = last_ref[...]
    zero = jnp.zeros_like(last)
    prefix = jnp.where(high[-1], last, zero)
    suffix = jnp.where(high[-1], zero, last)
    for up, part_ref in zip(high, parts):
        prefix += jnp.where(up, part_ref[:PER], zero)
        suffix += jnp.where(up, zero, part_ref[PER:])
    give_ref[:PER] = prefix + jnp.where(first, keep_ref[:PER], zero)
    give_ref[PER:] = suffix + jnp.where(first, zero, keep_ref[PER:])
    pre_ref[...] = prefix + jnp.where(first, zero, got_ref[:PER])
    suf_ref[...] = suffix + jnp.where(first, got_ref[PER:], zero)


def join(bits, me, after, keep, got, last, parts):
    half = jax.ShapeDtypeStruct((PER, DH, DH), F32)
    return pl.pallas_call(
        functools.partial(join_kernel, bits),
        out_shape=[jax.ShapeDtypeStruct((HEADS, DH, DH), F32), half, half],
        in_specs=[SMEM] + [VMEM] * (4 + len(parts)),
        out_specs=[VMEM] * 3,
        compiler_params=SMALL,
        name="join_states",
    )(me, after, keep, got, last, *parts)


def swap(value, bit, devices):
    return lax.ppermute(value, "ctx", [(i, i ^ bit) for i in range(devices)])


def on_device(queries, key_vectors, value_rows, cotangent):
    devices = lax.axis_size("ctx")
    length = queries.shape[0]
    factor = 1.0 / math.sqrt(DH * length * devices)
    arrays = (queries, key_vectors, value_rows, cotangent)
    held = tuple(pltpu.with_memory_space_constraint(array, pltpu.HBM) for array in arrays)
    me = jnp.reshape(lax.axis_index("ctx"), (1,))
    own = me & 1
    other = 1 - own
    send = half_states(other, held)
    got = swap(send, 1, devices)
    keep = half_states(own, held)
    total = add_states(keep, got)
    bits = []
    parts = []
    bit = 2
    while bit * 2 < devices:
        part = swap(total, bit, devices)
        bits.append(bit)
        parts.append(part)
        if bit * 4 < devices:
            total = add_states(total, part)
        bit *= 2
    *own_local, own_keep = local_products(own, arrays, total)
    bits.append(bit)
    sent = add_part((me // bit) & 1, total, parts[-1], own_keep)
    last = swap(sent, bit, devices)
    *other_local, other_keep = local_products(other, arrays, sent)
    give, prefix, suffix = join(tuple(bits), me, other_keep, keep, got, last, parts)
    taken = swap(give, 1, devices)
    outs = half_outputs(factor, own, arrays, prefix, suffix, own_local)
    return tuple(half_outputs(factor, other, arrays, taken[:PER], taken[PER:], other_local, tuple(outs)))


def solution(mesh):
    spec = P(("grp", "ctx"), None)
    return jax.shard_map(
        on_device, mesh=mesh, in_specs=(spec,) * 4, out_specs=(spec,) * 4, check_vma=False
    )
```

time: 48.8 us -> 35.9 us (0.74)
  waiting for transfers between devices: 16.8 us -> 8.08 us
  local copies, waits for them, and re-layouts: 4.93 us -> 0.03 us
  Pallas kernels: 13.7 us -> 18 us
  other arithmetic: 3.69 us -> 0 us
    pallas_call x0 -> x5, Pallas kernels: none -> 9.71 us  [the longest x2 9.56 us: local_products(): pl.pallas_call(local_kernel, out_shape=[jax.ShapeDtypeStruct((PER, length...]
    ppermute x4, waiting for transfers between devices: 16.8 us -> 8.08 us  [swap(): return lax.ppermute(value, 'ctx', [(i, i ^ bit) for i in range(devices)])]
    pallas_call x2, Pallas kernels: 12.5 us -> 4.31 us  [half_outputs(): pl.pallas_call(functools.partial(final_kernel, factor), out_shape=[out] *...]
    unnamed x20 -> x8, local copies, waits for them, and re-layouts: 4.91 us -> 0.01 us
    add x3 -> x0, other arithmetic: 3 us -> none  [the longest x1 1.16 us: on_device(): own_suffix = suffix + jnp.where(first, got[per:], 0.0)]
    pallas_call x2, Pallas kernels: 1.21 us -> 4 us  [half_states(): pl.pallas_call(states_kernel, out_shape=jax.ShapeDtypeStruct((HEADS, DH,...]
    select_n x1 -> x0, other arithmetic: 0.67 us -> none  [on_device(): part = swap(jnp.where(high, total[per:], total[:per]), bit, devices)]
  transfers between devices with their start and end apart: 4 -> 4, of which waited for: 3 -> 4; matrix products, arithmetic and copies ran while one was open for 0% -> 0% of each run, Pallas kernels for 14% -> 38%
where the time goes in v2:
time: 35.9 us; the launch traced here: 35.8 us
  Pallas kernels  18 us (50%)
  starting transfers between devices  8.93 us (25%)
  waiting for transfers between devices  8.08 us (23%)
  between operations  0.7 us (2%)
    pallas_call x2, Pallas kernels, local_products(): pl.pallas_call(local_kernel, out_shape=[jax.ShapeDtypeStruct((PER, length...  9.56 us
    ppermute x4, starting transfers between devices, swap(): return lax.ppermute(value, 'ctx', [(i, i ^ bit) for i in range(devices)])  8.93 us
    ppermute x4, waiting for transfers between devices, swap(): return lax.ppermute(value, 'ctx', [(i, i ^ bit) for i in range(devices)])  8.08 us
    pallas_call x2, Pallas kernels, half_outputs(): pl.pallas_call(functools.partial(final_kernel, factor), out_shape=[out] *...  4.31 us
    pallas_call x2, Pallas kernels, half_states(): pl.pallas_call(states_kernel, out_shape=jax.ShapeDtypeStruct((HEADS, DH,...  4 us
  transfers between devices with their start and end apart: 4, of which 4 were waited for; matrix products, arithmetic and copies ran while one was open for 0% of the time, Pallas kernels for 38%

profile of v2, /device:TPU:0, one launch (start us, length us, event | category | flops | bytes accessed | tf_op | source)
XLA Modules:
  0.0 35.8 jit_solution(7598359041162198820)
XLA Ops:
  0.6 1.9 %half_states.3 = f32[4,128,128]{2,1,0:T(8,128)S(1)} custom-call(s32[1]{0:T(128)S(6)} %sub.7.half_ref, bf16[1024,512]{1,0:T(8,128)(2,1)} %q_ref.7, bf16[1024,512]{1,0:T(8,128)(2,1)} %k_ref.7, bf16[1024,512]{1,0:T(8,128)(2,1)} %v_ref.7, bf16[1024,512]{1,0:T(8,128)(2,1)} %d_ref.7), custom_call_target="tpu_custom_call" | custom-call | flops 134217728 | bytes 2097152 | tf_op jit(solution)/shard_map/half_states/pallas_call | solution.py:63
  2.6 3.0 %collective-permute-start = (f32[4,128,128]{2,1,0:T(8,128)S(1)}, f32[4,128,128]{2,1,0:T(8,128)S(1)}, u32[]{:S(2)}, u32[]{:S(2)}) collective-permute-start(f32[4,128,128]{2,1,0:T(8,128)S(1)} %half_states.3), channel_id=1, source_target_pairs={{0,4},{4,0},{8,12},{12,8},{16,20},{20,16},{24,28},{28,24},{1,5},{5... | collective-permute-start | bytes 786440 | tf_op jit(solution)/shard_map/ppermute | solution.py:246
  5.6 0.0 copy-start
  5.6 0.0 copy-start.1
  5.6 0.0 copy-start.2
  5.6 0.0 copy-start.3
  5.6 2.1 %half_states.2.left_ref.keep_ref = f32[4,128,128]{2,1,0:T(8,128)S(1)} custom-call(s32[1]{0:T(128)S(6)} %and.12.half_ref, bf16[1024,512]{1,0:T(8,128)(2,1)} %q_ref.7, bf16[1024,512]{1,0:T(8,128)(2,1)} %k_ref.7, bf16[1024,512]{1,0:T(8,128)(2,1)} %v_ref.7, bf16[1024,512]{1,0:T(8,128)(2,1)} %d_ref.7), custom_call_target="tpu_custom_call" | custom-call | flops 134217728 | bytes 2097152 | tf_op jit(solution)/shard_map/half_states/pallas_call | solution.py:63
  7.7 4.2 %collective-permute-done.right_ref.got_ref = f32[4,128,128]{2,1,0:T(8,128)S(1)} collective-permute-done((f32[4,128,128]{2,1,0:T(8,128)S(1)}, f32[4,128,128]{2,1,0:T(8,128)S(1)}, u32[]{:S(2)}, u32[]{:S(2)}) %collective-permute-start) | collective-permute-done | bytes 262176 | tf_op jit(solution)/shard_map/ppermute | solution.py:246
  11.9 1.9 %collective-permute-start.1 = (f32[4,128,128]{2,1,0:T(8,128)S(1)}, f32[4,128,128]{2,1,0:T(8,128)S(1)}, u32[]{:S(2)}, u32[]{:S(2)}) collective-permute-start(f32[4,128,128]{2,1,0:T(8,128)S(1)} %add_states.1.after_ref.left_ref), channel_id=1, source_target_pairs={{0,8},{4,12},{8,0},{12,4},{16,24},{20,28},{24,16},{28,20},{1,9},{5... | collective-permute-start | bytes 786440 | tf_op jit(solution)/shard_map/ppermute | solution.py:246
  13.8 0.0 copy-done
  13.8 0.0 copy-done.1
  13.8 0.0 copy-done.2
  13.8 0.0 copy-done.3
  13.8 4.8 %local_products.2 = (f32[2,1024,128]{2,1,0:T(8,128)S(1)}, f32[2,1024,128]{2,1,0:T(8,128)S(1)}, f32[2,1024,128]{2,1,0:T(8,128)S(1)}, f32[2,1024,128]{2,1,0:T(8,128)S(1)}, f32[4,128,128]{2,1,0:T(8,128)S(1)}) custom-call(s32[1]{0:T(128)S(6)} %and.12.half_ref, f32[4,128,128]{2,1,0:T(8,128)S(1)} %add_states.1.after_ref.left_ref, bf16[1024,512]{1,0:T(8,128)(2,1)S(1)} %copy-done, ...), custom_call_target="tpu_custom_call" | custom-call | flops 1073741824 | bytes 4194304 | tf_op jit(solution)/shard_map/local_products/pallas_call | solution.py:122
  18.6 0.8 %collective-permute-done.1.right_ref.refs_0_ = f32[4,128,128]{2,1,0:T(8,128)S(1)} collective-permute-done((f32[4,128,128]{2,1,0:T(8,128)S(1)}, f32[4,128,128]{2,1,0:T(8,128)S(1)}, u32[]{:S(2)}, u32[]{:S(2)}) %collective-permute-start.1) | collective-permute-done | bytes 262176 | tf_op jit(solution)/shard_map/ppermute | solution.py:246
  19.5 2.6 %collective-permute-start.2 = (f32[2,128,128]{2,1,0:T(8,128)S(1)}, f32[2,128,128]{2,1,0:T(8,128)S(1)}, u32[]{:S(2)}, u32[]{:S(2)}) collective-permute-start(f32[2,128,128]{2,1,0:T(8,128)S(1)} %add_part.1.after_ref), channel_id=1, source_target_pairs={{0,16},{4,20},{8,24},{12,28},{16,0},{20,4},{24,8},{28,12},{1,17},{... | collective-permute-start | bytes 393224 | tf_op jit(solution)/shard_map/ppermute | solution.py:246
  22.1 4.8 %local_products.3 = (f32[2,1024,128]{2,1,0:T(8,128)S(1)}, f32[2,1024,128]{2,1,0:T(8,128)S(1)}, f32[2,1024,128]{2,1,0:T(8,128)S(1)}, f32[2,1024,128]{2,1,0:T(8,128)S(1)}, f32[4,128,128]{2,1,0:T(8,128)S(1)}) custom-call(s32[1]{0:T(128)S(6)} %sub.7.half_ref, f32[2,128,128]{2,1,0:T(8,128)S(1)} %add_part.1.after_ref, bf16[1024,512]{1,0:T(8,128)(2,1)S(1)} %copy-done, ...), custom_call_target="tpu_custom_call" | custom-call | flops 1073741824 | bytes 4194304 | tf_op jit(solution)/shard_map/local_products/pallas_call | solution.py:122
  26.8 0.2 collective-permute-done.2.last_ref
  27.0 0.1 join_states.1
  27.1 1.4 %collective-permute-start.3 = (f32[4,128,128]{2,1,0:T(8,128)S(1)}, f32[4,128,128]{2,1,0:T(8,128)S(1)}, u32[]{:S(2)}, u32[]{:S(2)}) collective-permute-start(f32[4,128,128]{2,1,0:T(8,128)S(1)} %get-tuple-element.23), channel_id=1, source_target_pairs={{0,4},{4,0},{8,12},{12,8},{16,20},{20,16},{24,28},{28,24},{1,5},{5... | collective-permute-start | bytes 786440 | tf_op jit(solution)/shard_map/ppermute | solution.py:246
  28.6 2.1 %half_outputs.2 = (bf16[1024,512]{1,0:T(8,128)(2,1)}, bf16[1024,512]{1,0:T(8,128)(2,1)}, bf16[1024,512]{1,0:T(8,128)(2,1)}, bf16[1024,512]{1,0:T(8,128)(2,1)}) custom-call(s32[1]{0:T(128)S(6)} %and.12.half_ref, bf16[1024,512]{1,0:T(8,128)(2,1)S(1)} %copy-done, bf16[1024,512]{1,0:T(8,128)(2,1)S(1)} %copy-done.1, bf16[1024,512]{1,0:T(8,128)(2,1)S(1)} %copy-done.2, ...), custom_call_target="tpu_custom_call" | custom-call | flops 536870912 | bytes 4194304 | tf_op jit(solution)/shard_map/half_outputs/pallas_call | solution.py:166
  30.7 2.9 %collective-permute-done.3 = f32[4,128,128]{2,1,0:T(8,128)S(1)} collective-permute-done((f32[4,128,128]{2,1,0:T(8,128)S(1)}, f32[4,128,128]{2,1,0:T(8,128)S(1)}, u32[]{:S(2)}, u32[]{:S(2)}) %collective-permute-start.3) | collective-permute-done | bytes 262176 | tf_op jit(solution)/shard_map/ppermute | solution.py:246
  33.6 2.2 %half_outputs.3 = (bf16[1024,512]{1,0:T(8,128)(2,1)}, bf16[1024,512]{1,0:T(8,128)(2,1)}, bf16[1024,512]{1,0:T(8,128)(2,1)}, bf16[1024,512]{1,0:T(8,128)(2,1)}) custom-call(s32[1]{0:T(128)S(6)} %sub.7.half_ref, bf16[1024,512]{1,0:T(8,128)(2,1)S(1)} %copy-done, ...), custom_call_target="tpu_custom_call", output_to_operand_aliasing={{0}: (11, {}), {1}: (12, {}), {2}: (13, {}), {3}: (14, {})} | custom-call | flops 536870912 | bytes 4194304 | tf_op jit(solution)/shard_map/half_outputs/pallas_call | solution.py:166
  (3 shorter events, 0.1 us)
Async XLA Ops:
  2.6 9.3 %collective-permute-start = (f32[4,128,128]{2,1,0:T(8,128)S(1)}, f32[4,128,128]{2,1,0:T(8,128)S(1)}, u32[]{:S(2)}, u32[]{:S(2)}) collective-permute-start(f32[4,128,128]{2,1,0:T(8,128)S(1)} %half_states.3), channel_id=1, source_target_pairs={{0,4},{4,0},{8,12},{12,8},{16,20},{20,16},{24,28},{28,24},{1,5},{5... | collective-permute-start | bytes 786440 | tf_op jit(solution)/shard_map/ppermute | solution.py:246
  5.6 8.2 %copy-start = (bf16[1024,512]{1,0:T(8,128)(2,1)S(1)}, bf16[1024,512]{1,0:T(8,128)(2,1)}, u32[]{:S(2)}) copy-start(bf16[1024,512]{1,0:T(8,128)(2,1)} %q_ref.7) | copy-start | bytes 3145732
  5.6 8.2 %copy-start.1 = (bf16[1024,512]{1,0:T(8,128)(2,1)S(1)}, bf16[1024,512]{1,0:T(8,128)(2,1)}, u32[]{:S(2)}) copy-start(bf16[1024,512]{1,0:T(8,128)(2,1)} %k_ref.7) | copy-start | bytes 3145732
  5.6 8.2 %copy-start.2 = (bf16[1024,512]{1,0:T(8,128)(2,1)S(1)}, bf16[1024,512]{1,0:T(8,128)(2,1)}, u32[]{:S(2)}) copy-start(bf16[1024,512]{1,0:T(8,128)(2,1)} %v_ref.7) | copy-start | bytes 3145732
  5.6 8.2 %copy-start.3 = (bf16[1024,512]{1,0:T(8,128)(2,1)S(1)}, bf16[1024,512]{1,0:T(8,128)(2,1)}, u32[]{:S(2)}) copy-start(bf16[1024,512]{1,0:T(8,128)(2,1)} %d_ref.7) | copy-start | bytes 3145732
  11.9 7.6 %collective-permute-start.1 = (f32[4,128,128]{2,1,0:T(8,128)S(1)}, f32[4,128,128]{2,1,0:T(8,128)S(1)}, u32[]{:S(2)}, u32[]{:S(2)}) collective-permute-start(f32[4,128,128]{2,1,0:T(8,128)S(1)} %add_states.1.after_ref.left_ref), channel_id=1, source_target_pairs={{0,8},{4,12},{8,0},{12,4},{16,24},{20,28},{24,16},{28,20},{1,9},{5... | collective-permute-start | bytes 786440 | tf_op jit(solution)/shard_map/ppermute | solution.py:246
  19.5 7.5 %collective-permute-start.2 = (f32[2,128,128]{2,1,0:T(8,128)S(1)}, f32[2,128,128]{2,1,0:T(8,128)S(1)}, u32[]{:S(2)}, u32[]{:S(2)}) collective-permute-start(f32[2,128,128]{2,1,0:T(8,128)S(1)} %add_part.1.after_ref), channel_id=1, source_target_pairs={{0,16},{4,20},{8,24},{12,28},{16,0},{20,4},{24,8},{28,12},{1,17},{... | collective-permute-start | bytes 393224 | tf_op jit(solution)/shard_map/ppermute | solution.py:246
  27.1 6.4 %collective-permute-start.3 = (f32[4,128,128]{2,1,0:T(8,128)S(1)}, f32[4,128,128]{2,1,0:T(8,128)S(1)}, u32[]{:S(2)}, u32[]{:S(2)}) collective-permute-start(f32[4,128,128]{2,1,0:T(8,128)S(1)} %get-tuple-element.23), channel_id=1, source_target_pairs={{0,4},{4,0},{8,12},{12,8},{16,20},{20,16},{24,28},{28,24},{1,5},{5... | collective-permute-start | bytes 786440 | tf_op jit(solution)/shard_map/ppermute | solution.py:246

commit v3 on v1

v3 whole, which is shorter than its diff:
```python
import functools
import math

import jax
import jax.numpy as jnp
from jax import lax
from jax.experimental import pallas as pl
from jax.experimental.pallas import tpu as pltpu
from jax.sharding import PartitionSpec as P

DH = 128
HEADS = 4
QUAD = 4
EARLY = ()
ORDER = (1, 2, 3)
CHUNK = 256
F32 = jnp.float32
BF16 = jnp.bfloat16
MIB = 2**20
VMEM = pl.BlockSpec(memory_space=pltpu.VMEM)
SMEM = pl.BlockSpec(memory_space=pltpu.SMEM)
HBM = pl.BlockSpec(memory_space=pltpu.HBM)


def mm(left, right):
    return lax.dot_general(left, right, (((1,), (0,)), ((), ())), preferred_element_type=F32)


def mm_first(left, right):
    return lax.dot_general(left, right, (((0,), (0,)), ((), ())), preferred_element_type=F32)


def mm_last(left, right):
    return lax.dot_general(left, right, (((1,), (1,)), ((), ())), preferred_element_type=F32)


def split(state):
    hi = state.astype(BF16)
    return hi, (state - hi.astype(F32)).astype(BF16)


def head_columns(me_ref, k):
    return pl.ds(pl.multiple_of((lax.rem(me_ref[0], QUAD) ^ k) * DH, DH), DH)


def params(mib):
    return pltpu.CompilerParams(vmem_limit_bytes=mib * MIB)


def states_kernel(ks, me_ref, q_hbm, k_hbm, v_hbm, d_hbm, *refs):
    outs, (q_ref, k_ref, v_ref, d_ref, sems) = refs[: len(ks)], refs[len(ks) :]
    pairs = ((k_hbm, k_ref), (v_hbm, v_ref), (q_hbm, q_ref), (d_hbm, d_ref))
    copies = [
        [
            pltpu.make_async_copy(source.at[:, head_columns(me_ref, k)], target.at[n], sems.at[n, i])
            for i, (source, target) in enumerate(pairs)
        ]
        for n, k in enumerate(ks)
    ]
    for group in copies:
        for copy in group:
            copy.start()
    for n in range(len(ks)):
        for copy in copies[n][:2]:
            copy.wait()
        outs[n][0] = mm_first(k_ref[n], v_ref[n])
        for copy in copies[n][2:]:
            copy.wait()
        outs[n][1] = mm_first(q_ref[n], d_ref[n])


def head_states(ks, me, arrays):
    length = arrays[0].shape[0]
    return pl.pallas_call(
        functools.partial(states_kernel, ks),
        out_shape=[jax.ShapeDtypeStruct((2, DH, DH), F32)] * len(ks),
        in_specs=[SMEM] + [HBM] * 4,
        out_specs=[VMEM] * len(ks),
        scratch_shapes=[pltpu.VMEM((len(ks), length, DH), BF16)] * 4 + [pltpu.SemaphoreType.DMA((len(ks), 4))],
        compiler_params=params(16),
        cost_estimate=pl.CostEstimate(
            flops=4 * len(ks) * length * DH * DH, bytes_accessed=8 * len(ks) * length * DH, transcendentals=0
        ),
        name="head_states",
    )(me, *arrays)


def local_kernel(which, me_ref, after_ref, q_ref, k_ref, v_ref, d_ref, att_ref, gq_ref, gk_ref, gv_ref, sub_ref, keep_ref):
    chunks = q_ref.shape[0] // CHUNK
    rows = lax.broadcasted_iota(jnp.int32, (CHUNK, CHUNK), 0)
    cols = lax.broadcasted_iota(jnp.int32, (CHUNK, CHUNK), 1)
    lower = rows >= cols
    upper = rows <= cols
    columns = head_columns(me_ref, which)
    state = jnp.zeros((DH, DH), F32)
    grads = []
    for c in range(chunks):
        at = slice(c * CHUNK, (c + 1) * CHUNK)
        q, k, v, d = q_ref[at, columns], k_ref[at, columns], v_ref[at, columns], d_ref[at, columns]
        weights = jnp.where(lower, mm_last(q, k), 0.0).astype(BF16)
        back = jnp.where(lower, mm_last(d, v), 0.0).astype(BF16)
        weights_t = jnp.where(upper, mm_last(k, q), 0.0).astype(BF16)
        back_t = jnp.where(upper, mm_last(v, d), 0.0).astype(BF16)
        att_ref[at, :] = mm(weights, v)
        gq_ref[at, :] = mm(back, k)
        gk_ref[at, :] = mm(back_t, q)
        gv_ref[at, :] = mm(weights_t, d)
        sub_ref[c, 0] = state
        state = state + mm_first(k, v)
        grads.append(mm_first(q, d))
    keep_ref[0] = state
    state = jnp.zeros((DH, DH), F32)
    for c in reversed(range(chunks)):
        sub_ref[c, 1] = state
        state = state + grads[c]
    keep_ref[1] = state


def local_products(which, me, arrays, after):
    length = arrays[0].shape[0]
    chunks = length // CHUNK
    *products, keep = pl.pallas_call(
        functools.partial(local_kernel, which),
        out_shape=[jax.ShapeDtypeStruct((length, DH), F32)] * 4
        + [jax.ShapeDtypeStruct((chunks, 2, DH, DH), F32), jax.ShapeDtypeStruct((2, DH, DH), F32)],
        in_specs=[SMEM] + [VMEM] * 5,
        out_specs=[VMEM] * 6,
        compiler_params=params(16),
        cost_estimate=pl.CostEstimate(
            flops=16 * length * CHUNK * DH, bytes_accessed=8 * length * DH, transcendentals=0
        ),
        name="local_products",
    )(me, after, *arrays)
    return products, keep


def final_kernel(factor, which, count, earlier, last, me_ref, q_ref, k_ref, v_ref, d_ref, *refs):
    given, refs = refs[:count], refs[count:]
    (att_ref, gq_ref, gk_ref, gv_ref, sub_ref), refs = refs[:5], refs[5:]
    staged, refs = refs[: len(earlier)], refs[len(earlier) :]
    columns = head_columns(me_ref, which)
    copies = []
    if last is None:
        (stage,) = refs
    else:
        *outs, stage, sems = refs[-6:]
    for row, (k, source) in enumerate(zip(earlier, staged)):
        for i in range(4):
            copies.append(pltpu.make_async_copy(source.at[i], outs[i].at[:, head_columns(me_ref, k)], sems.at[row, i]))
    for copy in copies:
        copy.start()
    chunks = q_ref.shape[0] // CHUNK
    prefix, suffix = given[0][0], given[0][1]
    if count == 2 and given[1].shape[0] == 1:
        high = lax.rem(lax.div(me_ref[0], QUAD), 2) == 1
        zero = jnp.zeros((DH, DH), F32)
        prefix += jnp.where(high, given[1][0], zero)
        suffix += jnp.where(high, zero, given[1][0])
    elif count == 2:
        prefix += given[1][0]
        suffix += given[1][1]
    states = [split(prefix + sub_ref[c, 0]) for c in range(chunks)]
    grads = [split(suffix + sub_ref[c, 1]) for c in range(chunks)]
    work = (
        (q_ref, states, mm, att_ref),
        (d_ref, states, mm_last, gq_ref),
        (v_ref, grads, mm_last, gk_ref),
        (k_ref, grads, mm, gv_ref),
    )
    for i, (source, parts, product, local) in enumerate(work):
        for c, (hi, lo) in enumerate(parts):
            at = slice(c * CHUNK, (c + 1) * CHUNK)
            rows = source[at, columns]
            value = local[at, :] + product(rows, hi) + product(rows, lo)
            stage[i, at, :] = (factor * value).astype(BF16)
        if last is not None:
            copy = pltpu.make_async_copy(stage.at[i], outs[i].at[:, columns], sems.at[len(earlier), i])
            copy.start()
            copies.append(copy)
    for copy in copies:
        copy.wait()


def head_outputs(factor, which, me, arrays, given, local, staged=(), outs=None):
    length, columns = arrays[0].shape
    staging = (4, length, DH)
    earlier = tuple(k for k, _ in staged)
    inputs = [me, *arrays, *given, *local, *(value for _, value in staged)]
    in_specs = [SMEM] + [VMEM] * (len(inputs) - 1)
    if outs is None:
        out_shape, out_specs = [jax.ShapeDtypeStruct(staging, BF16)], [VMEM]
        scratch, aliases = [], {}
    else:
        out_shape, out_specs = [jax.ShapeDtypeStruct((length, columns), BF16)] * 4, [HBM] * 4
        scratch = [pltpu.VMEM(staging, BF16), pltpu.SemaphoreType.DMA((len(earlier) + 1, 4))]
        aliases = {len(inputs) + i: i for i in range(len(outs))}
        in_specs += [HBM] * len(outs)
    return pl.pallas_call(
        functools.partial(final_kernel, factor, which, len(given), earlier, None if outs is None else bool(outs)),
        out_shape=out_shape,
        in_specs=in_specs,
        out_specs=out_specs,
        scratch_shapes=scratch,
        input_output_aliases=aliases,
        compiler_params=params(16),
        cost_estimate=pl.CostEstimate(
            flops=16 * length * DH * DH, bytes_accessed=8 * length * DH, transcendentals=0
        ),
        name="head_outputs",
    )(*inputs, *(outs or ()))


def total_kernel(me_ref, after_ref, *refs):
    pieces, out_ref = refs[:-1], refs[-1]
    total = pieces[0][...]
    for piece in pieces[1:]:
        total += piece[...]
    out_ref[...] = total


def part_kernel(bit, me_ref, after_ref, *refs):
    pieces, out_ref = refs[:-1], refs[-1]
    at = pl.ds(lax.rem(lax.div(me_ref[0], bit), 2), 1)
    total = pieces[0][at]
    for piece in pieces[1:]:
        total += piece[at]
    out_ref[...] = total


def combine(kernel, states, me, after, pieces, name):
    return pl.pallas_call(
        kernel,
        out_shape=jax.ShapeDtypeStruct((states, DH, DH), F32),
        in_specs=[SMEM] + [VMEM] * (1 + len(pieces)),
        out_specs=VMEM,
        compiler_params=params(4),
        name=name,
    )(me, after, *pieces)


def parts_kernel(me_ref, after_ref, *refs):
    pieces, outs = refs[:QUAD], refs[QUAD:]
    rank = lax.rem(me_ref[0], QUAD)
    zero = jnp.zeros((DH, DH), F32)
    for k, out in enumerate(outs):
        prefix, suffix = zero, zero
        for j, piece in enumerate(pieces):
            if j != k:
                before = (rank ^ j) < (rank ^ k)
                prefix += jnp.where(before, piece[0], zero)
                suffix += jnp.where(before, zero, piece[1])
        out[0] = prefix
        out[1] = suffix


def quad_parts(me, after, pieces):
    return pl.pallas_call(
        parts_kernel,
        out_shape=[jax.ShapeDtypeStruct((2, DH, DH), F32)] * QUAD,
        in_specs=[SMEM] + [VMEM] * (1 + QUAD),
        out_specs=[VMEM] * QUAD,
        compiler_params=params(4),
        name="quad_parts",
    )(me, after, *pieces)


def base_kernel(bits, me_ref, last_ref, *refs):
    parts, out_ref = refs[:-1], refs[-1]
    high = [lax.rem(lax.div(me_ref[0], bit), 2) == 1 for bit in bits]
    zero = jnp.zeros((DH, DH), F32)
    prefix = jnp.where(high[-1], last_ref[0], zero)
    suffix = jnp.where(high[-1], zero, last_ref[0])
    for up, part in zip(high, parts):
        prefix += jnp.where(up, part[0], zero)
        suffix += jnp.where(up, zero, part[1])
    out_ref[0] = prefix
    out_ref[1] = suffix


def quad_base(bits, me, last, parts):
    return pl.pallas_call(
        functools.partial(base_kernel, bits),
        out_shape=jax.ShapeDtypeStruct((2, DH, DH), F32),
        in_specs=[SMEM] + [VMEM] * (1 + len(parts)),
        out_specs=VMEM,
        compiler_params=params(4),
        name="quad_base",
    )(me, last, *parts)


def whole_kernel(me_ref, after_ref, base_ref, *refs):
    half = len(refs) // 2
    for part_ref, out_ref in zip(refs[:half], refs[half:]):
        if base_ref.shape[0] == 1:
            high = lax.rem(lax.div(me_ref[0], QUAD), 2) == 1
            zero = jnp.zeros((DH, DH), F32)
            out_ref[0] = part_ref[0] + jnp.where(high, base_ref[0], zero)
            out_ref[1] = part_ref[1] + jnp.where(high, zero, base_ref[0])
        else:
            out_ref[...] = part_ref[...] + base_ref[...]


def whole_states(me, after, base, parts):
    return pl.pallas_call(
        whole_kernel,
        out_shape=[jax.ShapeDtypeStruct((2, DH, DH), F32)] * len(parts),
        in_specs=[SMEM] + [VMEM] * (2 + len(parts)),
        out_specs=[VMEM] * len(parts),
        compiler_params=params(4),
        name="whole_states",
    )(me, after, base, *parts)


def swap(value, bit):
    return lax.ppermute(value, "ctx", [(i, i ^ bit) for i in range(lax.axis_size("ctx"))])


def on_device(queries, key_vectors, value_rows, cotangent):
    devices = lax.axis_size("ctx")
    factor = 1.0 / math.sqrt(DH * queries.shape[0] * devices)
    arrays = (queries, key_vectors, value_rows, cotangent)
    held = tuple(pltpu.with_memory_space_constraint(array, pltpu.HBM) for array in arrays)
    me = jnp.reshape(lax.axis_index("ctx"), (1,))
    local = [None] * QUAD
    send1, send2 = head_states((1, 2), me, held)
    got1 = swap(send1, 1)
    got2 = swap(send2, 2)
    (send3,) = head_states((3,), me, held)
    got3 = swap(send3, 3)
    local[0], keep = local_products(0, me, arrays, send3)
    local[1], after = local_products(1, me, arrays, keep)
    local[2], after = local_products(2, me, arrays, after)
    pieces = (keep, got1, got2, got3)
    known = pieces
    bits = []
    parts = []
    bit = QUAD
    while bit * 2 < devices:
        total = combine(total_kernel, 2, me, after, known, "sum_states")
        part = swap(total, bit)
        bits.append(bit)
        parts.append(part)
        known = (total, part)
        bit *= 2
    bits.append(bit)
    chosen = combine(functools.partial(part_kernel, bit), 1, me, after, known, "pick_state")
    base = swap(chosen, bit)
    mine = quad_parts(me, chosen, pieces)
    early = {k: swap(mine[k], k) for k in EARLY}
    local[3], after = local_products(3, me, arrays, mine[0])
    if parts:
        base = quad_base(tuple(bits), me, base, parts)
    late = [k for k in range(1, QUAD) if k not in EARLY]
    given = {0: (mine[0], base)}
    if late:
        for k, whole in zip(late, whole_states(me, after, base, [mine[k] for k in late])):
            given[k] = (swap(whole, k),)
    for k in EARLY:
        given[k] = (early[k], swap(base, k))
    outs = head_outputs(factor, 0, me, arrays, given[0], local[0], outs=())
    staged = [(k, head_outputs(factor, k, me, arrays, given[k], local[k])[0]) for k in ORDER[:2]]
    k = ORDER[2]
    return tuple(head_outputs(factor, k, me, arrays, given[k], local[k], staged, outs))


def solution(mesh):
    spec = P(("grp", "ctx"), None)
    return jax.shard_map(
        on_device, mesh=mesh, in_specs=(spec,) * 4, out_specs=(spec,) * 4, check_vma=False
    )
```

time: 48.8 us -> 30.9 us (0.63)
  waiting for transfers between devices: 16.8 us -> 4.64 us
  local copies, waits for them, and re-layouts: 4.93 us -> 0.01 us
  other arithmetic: 3.69 us -> 0 us
  starting transfers between devices: 8.61 us -> 11.1 us
  Pallas kernels: 13.7 us -> 14.3 us
    ppermute x4 -> x7, waiting for transfers between devices: 16.8 us -> 4.64 us  [swap(): lax.ppermute(value, 'ctx', [(i, i ^ bit) for i in range(lax.axis_size('ct...]
    unnamed x20 -> x8, local copies, waits for them, and re-layouts: 4.91 us -> 0.01 us
    add x3 -> x0, other arithmetic: 3 us -> none  [the longest x1 1.16 us: on_device(): own_suffix = suffix + jnp.where(first, got[per:], 0.0)]
    ppermute x4 -> x7, starting transfers between devices: 8.61 us -> 11.1 us  [swap(): lax.ppermute(value, 'ctx', [(i, i ^ bit) for i in range(lax.axis_size('ct...]
    select_n x1 -> x0, other arithmetic: 0.67 us -> none  [on_device(): part = swap(jnp.where(high, total[per:], total[:per]), bit, devices)]
    pallas_call x4 -> x13, Pallas kernels: 13.7 us -> 14.3 us  [the longest x4 5.62 us: local_products(): pl.pallas_call(functools.partial(local_kernel, which), out_shape=[jax.Sha...]
  transfers between devices with their start and end apart: 4 -> 7, of which waited for: 3 -> 4; matrix products, arithmetic and copies ran while one was open for 0% -> 0% of each run, Pallas kernels for 14% -> 33%
where the time goes in v3:
time: 30.9 us; the launch traced here: 30.7 us
  Pallas kernels  14.3 us (46%)
  starting transfers between devices  11.1 us (36%)
  waiting for transfers between devices  4.64 us (15%)
  between operations  0.76 us (2%)
    ppermute x7, starting transfers between devices, swap(): lax.ppermute(value, 'ctx', [(i, i ^ bit) for i in range(lax.axis_size('ct...  11.1 us
    pallas_call x4, Pallas kernels, local_products(): pl.pallas_call(functools.partial(local_kernel, which), out_shape=[jax.Sha...  5.62 us
    pallas_call x4, Pallas kernels, head_outputs(): pl.pallas_call(functools.partial(final_kernel, factor, which, len(given),...  4.69 us
    ppermute x7, waiting for transfers between devices, swap(): lax.ppermute(value, 'ctx', [(i, i ^ bit) for i in range(lax.axis_size('ct...  4.64 us
    pallas_call x2, Pallas kernels, head_states(): pl.pallas_call(functools.partial(states_kernel, ks), out_shape=[jax.Shape...  3.82 us
  transfers between devices with their start and end apart: 7, of which 4 were waited for; matrix products, arithmetic and copies ran while one was open for 0% of the time, Pallas kernels for 33%

profile of v3, /device:TPU:0, one launch (start us, length us, event | category | flops | bytes accessed | tf_op | source)
XLA Modules:
  0.0 30.7 jit_solution(14879526383522314543)
XLA Ops:
  0.6 2.2 %head_states.3 = (f32[2,128,128]{2,1,0:T(8,128)S(1)}, f32[2,128,128]{2,1,0:T(8,128)S(1)}) custom-call(s32[1]{0:T(128)} %bitcast.me_ref, bf16[1024,512]{1,0:T(8,128)(2,1)} %q_ref.15, bf16[1024,512]{1,0:T(8,128)(2,1)} %k_ref.15, bf16[1024,512]{1,0:T(8,128)(2,1)} %v_ref.15, bf16[1024,512]{1,0:T(8,128)(2,1)} %d_ref.15), custom_call_target="tpu_custom_call" | custom-call | flops 134217728 | bytes 2097152 | tf_op jit(solution)/shard_map/head_states/pallas_call | solution.py:74
  2.8 3.0 %collective-permute-start = (f32[2,128,128]{2,1,0:T(8,128)S(1)}, f32[2,128,128]{2,1,0:T(8,128)S(1)}, u32[]{:S(2)}, u32[]{:S(2)}) collective-permute-start(f32[2,128,128]{2,1,0:T(8,128)S(1)} %get-tuple-element.44), channel_id=1, source_target_pairs={{0,4},{4,0},{8,12},{12,8},{16,20},{20,16},{24,28},{28,24},{1,5},{5... | collective-permute-start | bytes 393224 | tf_op jit(solution)/shard_map/ppermute | solution.py:315
  5.9 1.6 %collective-permute-start.1 = (f32[2,128,128]{2,1,0:T(8,128)S(1)}, f32[2,128,128]{2,1,0:T(8,128)S(1)}, u32[]{:S(2)}, u32[]{:S(2)}) collective-permute-start(f32[2,128,128]{2,1,0:T(8,128)S(1)} %get-tuple-element.45), channel_id=1, source_target_pairs={{0,8},{4,12},{8,0},{12,4},{16,24},{20,28},{24,16},{28,20},{1,9},{5... | collective-permute-start | bytes 393224 | tf_op jit(solution)/shard_map/ppermute | solution.py:315
  7.5 1.6 %head_states.2.after_ref = f32[2,128,128]{2,1,0:T(8,128)S(1)} custom-call(s32[1]{0:T(128)} %bitcast.me_ref, bf16[1024,512]{1,0:T(8,128)(2,1)} %q_ref.15, bf16[1024,512]{1,0:T(8,128)(2,1)} %k_ref.15, bf16[1024,512]{1,0:T(8,128)(2,1)} %v_ref.15, bf16[1024,512]{1,0:T(8,128)(2,1)} %d_ref.15), custom_call_target="tpu_custom_call" | custom-call | flops 67108864 | bytes 1048576 | tf_op jit(solution)/shard_map/head_states/pallas_call | solution.py:74
  9.1 0.2 collective-permute-start.2
  9.4 1.4 %local_products.4 = (f32[1024,128]{1,0:T(8,128)S(1)}, f32[1024,128]{1,0:T(8,128)S(1)}, f32[1024,128]{1,0:T(8,128)S(1)}, f32[1024,128]{1,0:T(8,128)S(1)}, f32[4,2...) custom-call(s32[1]{0:T(128)} %bitcast.me_ref, f32[2,128,128]{2,1,0:T(8,128)S(1)} %head_states.2.after_ref, ...), custom_call_target="tpu_custom_call" | custom-call | flops 536870912 | bytes 1048576 | tf_op jit(solution)/shard_map/local_products/pallas_call | solution.py:122
  10.8 1.4 %local_products.5 = (f32[1024,128]{1,0:T(8,128)S(1)}, f32[1024,128]{1,0:T(8,128)S(1)}, f32[1024,128]{1,0:T(8,128)S(1)}, f32[1024,128]{1,0:T(8,128)S(1)}, f32[4,2...) custom-call(s32[1]{0:T(128)} %bitcast.me_ref, f32[2,128,128]{2,1,0:T(8,128)S(1)} %get-tuple-element.41.after_ref.refs_0_, ...), custom_call_target="tpu_custom_call" | custom-call | flops 536870912 | bytes 1048576 | tf_op jit(solution)/shard_map/local_products/pallas_call | solution.py:122
  12.2 1.4 %local_products.6 = (f32[1024,128]{1,0:T(8,128)S(1)}, f32[1024,128]{1,0:T(8,128)S(1)}, f32[1024,128]{1,0:T(8,128)S(1)}, f32[1024,128]{1,0:T(8,128)S(1)}, f32[4,2...) custom-call(s32[1]{0:T(128)} %bitcast.me_ref, f32[2,128,128]{2,1,0:T(8,128)S(1)} %get-tuple-element.42.after_ref, ...), custom_call_target="tpu_custom_call" | custom-call | flops 536870912 | bytes 1048576 | tf_op jit(solution)/shard_map/local_products/pallas_call | solution.py:122
  13.6 0.0 collective-permute-done.refs_1_
  13.6 0.0 collective-permute-done.1.refs_2_
  13.6 1.4 %collective-permute-done.2.refs_3_ = f32[2,128,128]{2,1,0:T(8,128)S(1)} collective-permute-done((f32[2,128,128]{2,1,0:T(8,128)S(1)}, f32[2,128,128]{2,1,0:T(8,128)S(1)}, u32[]{:S(2)}, u32[]{:S(2)}) %collective-permute-start.2) | collective-permute-done | bytes 131104 | tf_op jit(solution)/shard_map/ppermute | solution.py:315
  15.1 2.7 %collective-permute-start.3 = (f32[1,128,128]{2,1,0:T(8,128)S(1)}, f32[1,128,128]{2,1,0:T(8,128)S(1)}, u32[]{:S(2)}, u32[]{:S(2)}) collective-permute-start(f32[1,128,128]{2,1,0:T(8,128)S(1)} %pick_state.1.after_ref), channel_id=1, source_target_pairs={{0,16},{4,20},{8,24},{12,28},{16,0},{20,4},{24,8},{28,12},{1,17},{... | collective-permute-start | bytes 196616 | tf_op jit(solution)/shard_map/ppermute | solution.py:315
  17.7 0.1 quad_parts.1
  17.8 1.4 %local_products.7 = (f32[1024,128]{1,0:T(8,128)S(1)}, f32[1024,128]{1,0:T(8,128)S(1)}, f32[1024,128]{1,0:T(8,128)S(1)}, f32[1024,128]{1,0:T(8,128)S(1)}, f32[4,2...) custom-call(s32[1]{0:T(128)} %bitcast.me_ref, f32[2,128,128]{2,1,0:T(8,128)S(1)} %get-tuple-element.46.after_ref.refs_0_, ...), custom_call_target="tpu_custom_call" | custom-call | flops 536870912 | bytes 1048576 | tf_op jit(solution)/shard_map/local_products/pallas_call | solution.py:122
  19.2 1.8 %collective-permute-done.3.base_ref.refs_1_ = f32[1,128,128]{2,1,0:T(8,128)S(1)} collective-permute-done((f32[1,128,128]{2,1,0:T(8,128)S(1)}, f32[1,128,128]{2,1,0:T(8,128)S(1)}, u32[]{:S(2)}, u32[]{:S(2)}) %collective-permute-start.3) | collective-permute-done | bytes 65568 | tf_op jit(solution)/shard_map/ppermute | solution.py:315
  21.1 0.1 collective-permute-start.5
  21.1 1.2 %collective-permute-start.6 = (f32[2,128,128]{2,1,0:T(8,128)S(1)}, f32[2,128,128]{2,1,0:T(8,128)S(1)}, u32[]{:S(2)}, u32[]{:S(2)}) collective-permute-start(f32[2,128,128]{2,1,0:T(8,128)S(1)} %get-tuple-element.63), channel_id=1, source_target_pairs={{0,8},{4,12},{8,0},{12,4},{16,24},{20,28},{24,16},{28,20},{1,9},{5... | collective-permute-start | bytes 393224 | tf_op jit(solution)/shard_map/ppermute | solution.py:315
  22.3 2.3 %collective-permute-start.4 = (f32[2,128,128]{2,1,0:T(8,128)S(1)}, f32[2,128,128]{2,1,0:T(8,128)S(1)}, u32[]{:S(2)}, u32[]{:S(2)}) collective-permute-start(f32[2,128,128]{2,1,0:T(8,128)S(1)} %get-tuple-element.51), channel_id=1, source_target_pairs={{0,12},{4,8},{8,4},{12,0},{16,28},{20,24},{24,20},{28,16},{1,13},{... | collective-permute-start | bytes 393224 | tf_op jit(solution)/shard_map/ppermute | solution.py:315
  24.6 1.5 %head_outputs.6 = (bf16[1024,512]{1,0:T(8,128)(2,1)}, bf16[1024,512]{1,0:T(8,128)(2,1)}, bf16[1024,512]{1,0:T(8,128)(2,1)}, bf16[1024,512]{1,0:T(8,128)(2,1)}) custom-call(s32[1]{0:T(128)} %bitcast.me_ref, bf16[1024,512]{1,0:T(8,128)(2,1)S(1)} %copy-done, bf16[1024,512]{1,0:T(8,128)(2,1)S(1)} %copy-done.1, bf16[1024,512]{1,0:T(8,128)(2,1)S(1)} %copy-done.2, ...), custom_call_target="tpu_custom_call" | custom-call | flops 268435456 | bytes 1048576 | tf_op jit(solution)/shard_map/head_outputs/pallas_call | solution.py:198
  26.1 0.1 collective-permute-done.5.refs_0_
  26.1 0.7 %head_outputs.4.refs_6_ = bf16[4,1024,128]{2,1,0:T(8,128)(2,1)S(1)} custom-call(s32[1]{0:T(128)} %bitcast.me_ref, bf16[1024,512]{1,0:T(8,128)(2,1)S(1)} %copy-done, bf16[1024,512]{1,0:T(8,128)(2,1)S(1)} %copy-done.1, bf16[1024,512]{1,0:T(8,128)(2,1)S(1)} %copy-done.2, bf16[1024,512]{1,0:T(8,128)(2,1)S(1)} %copy-done.3, ...), custom_call_target="tpu_custom_call" | custom-call | flops 268435456 | bytes 1048576 | tf_op jit(solution)/shard_map/head_outputs/pallas_call | solution.py:198
  26.9 0.7 %head_outputs.5.refs_7_ = bf16[4,1024,128]{2,1,0:T(8,128)(2,1)S(1)} custom-call(s32[1]{0:T(128)} %bitcast.me_ref, bf16[1024,512]{1,0:T(8,128)(2,1)S(1)} %copy-done, bf16[1024,512]{1,0:T(8,128)(2,1)S(1)} %copy-done.1, bf16[1024,512]{1,0:T(8,128)(2,1)S(1)} %copy-done.2, bf16[1024,512]{1,0:T(8,128)(2,1)S(1)} %copy-done.3, ...), custom_call_target="tpu_custom_call" | custom-call | flops 268435456 | bytes 1048576 | tf_op jit(solution)/shard_map/head_outputs/pallas_call | solution.py:198
  27.6 1.4 %collective-permute-done.4.refs_0_ = f32[2,128,128]{2,1,0:T(8,128)S(1)} collective-permute-done((f32[2,128,128]{2,1,0:T(8,128)S(1)}, f32[2,128,128]{2,1,0:T(8,128)S(1)}, u32[]{:S(2)}, u32[]{:S(2)}) %collective-permute-start.4) | collective-permute-done | bytes 131104 | tf_op jit(solution)/shard_map/ppermute | solution.py:315
  29.0 1.8 %head_outputs.7 = (bf16[1024,512]{1,0:T(8,128)(2,1)}, bf16[1024,512]{1,0:T(8,128)(2,1)}, bf16[1024,512]{1,0:T(8,128)(2,1)}, bf16[1024,512]{1,0:T(8,128)(2,1)}) custom-call(s32[1]{0:T(128)} %bitcast.me_ref, bf16[1024,512]{1,0:T(8,128)(2,1)S(1)} %copy-done, ...), custom_call_target="tpu_custom_call", output_to_operand_aliasing={{0}: (13, {}), {1}: (14, {}), {2}: (15, {}), {3}: (16, {})} | custom-call | flops 268435456 | bytes 1048576 | tf_op jit(solution)/shard_map/head_outputs/pallas_call | solution.py:198
  (11 shorter events, 0.1 us)
Async XLA Ops:
  2.8 10.7 %collective-permute-start = (f32[2,128,128]{2,1,0:T(8,128)S(1)}, f32[2,128,128]{2,1,0:T(8,128)S(1)}, u32[]{:S(2)}, u32[]{:S(2)}) collective-permute-start(f32[2,128,128]{2,1,0:T(8,128)S(1)} %get-tuple-element.44), channel_id=1, source_target_pairs={{0,4},{4,0},{8,12},{12,8},{16,20},{20,16},{24,28},{28,24},{1,5},{5... | collective-permute-start | bytes 393224 | tf_op jit(solution)/shard_map/ppermute | solution.py:315
  5.9 3.5 %copy-start = (bf16[1024,512]{1,0:T(8,128)(2,1)S(1)}, bf16[1024,512]{1,0:T(8,128)(2,1)}, u32[]{:S(2)}) copy-start(bf16[1024,512]{1,0:T(8,128)(2,1)} %q_ref.15) | copy-start | bytes 3145732
  5.9 3.5 %copy-start.1 = (bf16[1024,512]{1,0:T(8,128)(2,1)S(1)}, bf16[1024,512]{1,0:T(8,128)(2,1)}, u32[]{:S(2)}) copy-start(bf16[1024,512]{1,0:T(8,128)(2,1)} %k_ref.15) | copy-start | bytes 3145732
  5.9 3.5 %copy-start.2 = (bf16[1024,512]{1,0:T(8,128)(2,1)S(1)}, bf16[1024,512]{1,0:T(8,128)(2,1)}, u32[]{:S(2)}) copy-start(bf16[1024,512]{1,0:T(8,128)(2,1)} %v_ref.15) | copy-start | bytes 3145732
  5.9 3.5 %copy-start.3 = (bf16[1024,512]{1,0:T(8,128)(2,1)S(1)}, bf16[1024,512]{1,0:T(8,128)(2,1)}, u32[]{:S(2)}) copy-start(bf16[1024,512]{1,0:T(8,128)(2,1)} %d_ref.15) | copy-start | bytes 3145732
  5.9 7.7 %collective-permute-start.1 = (f32[2,128,128]{2,1,0:T(8,128)S(1)}, f32[2,128,128]{2,1,0:T(8,128)S(1)}, u32[]{:S(2)}, u32[]{:S(2)}) collective-permute-start(f32[2,128,128]{2,1,0:T(8,128)S(1)} %get-tuple-element.45), channel_id=1, source_target_pairs={{0,8},{4,12},{8,0},{12,4},{16,24},{20,28},{24,16},{28,20},{1,9},{5... | collective-permute-start | bytes 393224 | tf_op jit(solution)/shard_map/ppermute | solution.py:315
  9.1 5.9 %collective-permute-start.2 = (f32[2,128,128]{2,1,0:T(8,128)S(1)}, f32[2,128,128]{2,1,0:T(8,128)S(1)}, u32[]{:S(2)}, u32[]{:S(2)}) collective-permute-start(f32[2,128,128]{2,1,0:T(8,128)S(1)} %head_states.2.after_ref), channel_id=1, source_target_pairs={{0,12},{4,8},{8,4},{12,0},{16,28},{20,24},{24,20},{28,16},{1,13},{... | collective-permute-start | bytes 393224 | tf_op jit(solution)/shard_map/ppermute | solution.py:315
  15.1 5.9 %collective-permute-start.3 = (f32[1,128,128]{2,1,0:T(8,128)S(1)}, f32[1,128,128]{2,1,0:T(8,128)S(1)}, u32[]{:S(2)}, u32[]{:S(2)}) collective-permute-start(f32[1,128,128]{2,1,0:T(8,128)S(1)} %pick_state.1.after_ref), channel_id=1, source_target_pairs={{0,16},{4,20},{8,24},{12,28},{16,0},{20,4},{24,8},{28,12},{1,17},{... | collective-permute-start | bytes 196616 | tf_op jit(solution)/shard_map/ppermute | solution.py:315
  21.1 5.1 %collective-permute-start.5 = (f32[2,128,128]{2,1,0:T(8,128)S(1)}, f32[2,128,128]{2,1,0:T(8,128)S(1)}, u32[]{:S(2)}, u32[]{:S(2)}) collective-permute-start(f32[2,128,128]{2,1,0:T(8,128)S(1)} %get-tuple-element.57), channel_id=1, source_target_pairs={{0,4},{4,0},{8,12},{12,8},{16,20},{20,16},{24,28},{28,24},{1,5},{5... | collective-permute-start | bytes 393224 | tf_op jit(solution)/shard_map/ppermute | solution.py:315
  21.1 5.7 %collective-permute-start.6 = (f32[2,128,128]{2,1,0:T(8,128)S(1)}, f32[2,128,128]{2,1,0:T(8,128)S(1)}, u32[]{:S(2)}, u32[]{:S(2)}) collective-permute-start(f32[2,128,128]{2,1,0:T(8,128)S(1)} %get-tuple-element.63), channel_id=1, source_target_pairs={{0,8},{4,12},{8,0},{12,4},{16,24},{20,28},{24,16},{28,20},{1,9},{5... | collective-permute-start | bytes 393224 | tf_op jit(solution)/shard_map/ppermute | solution.py:315
  22.3 6.6 %collective-permute-start.4 = (f32[2,128,128]{2,1,0:T(8,128)S(1)}, f32[2,128,128]{2,1,0:T(8,128)S(1)}, u32[]{:S(2)}, u32[]{:S(2)}) collective-permute-start(f32[2,128,128]{2,1,0:T(8,128)S(1)} %get-tuple-element.51), channel_id=1, source_target_pairs={{0,12},{4,8},{8,4},{12,0},{16,28},{20,24},{24,20},{28,16},{1,13},{... | collective-permute-start | bytes 393224 | tf_op jit(solution)/shard_map/ppermute | solution.py:315

commit v4 on v3

--- a/solution.py
+++ b/solution.py
@@ -12,7 +12,7 @@
 HEADS = 4
 QUAD = 4
 EARLY = ()
-ORDER = (1, 2, 3)
+ORDER = (3, 1, 2)
 CHUNK = 256
 F32 = jnp.float32
 BF16 = jnp.bfloat16
@@ -47,91 +47,129 @@
     return pltpu.CompilerParams(vmem_limit_bytes=mib * MIB)
 
 
-def states_kernel(ks, me_ref, q_hbm, k_hbm, v_hbm, d_hbm, *refs):
-    outs, (q_ref, k_ref, v_ref, d_ref, sems) = refs[: len(ks)], refs[len(ks) :]
-    pairs = ((k_hbm, k_ref), (v_hbm, v_ref), (q_hbm, q_ref), (d_hbm, d_ref))
-    copies = [
-        [
-            pltpu.make_async_copy(source.at[:, head_columns(me_ref, k)], target.at[n], sems.at[n, i])
-            for i, (source, target) in enumerate(pairs)
-        ]
-        for n, k in enumerate(ks)
+def sub_states(left, right, axis, sub_ref, total_ref):
+    chunks = left.shape[0] // CHUNK
+    state = jnp.zeros((DH, DH), F32)
+    for c in range(chunks) if axis == 0 else reversed(range(chunks)):
+        at = slice(c * CHUNK, (c + 1) * CHUNK)
+        sub_ref[c, axis] = state
+        state = state + mm_first(left[at], right[at])
+    total_ref[axis] = state
+
+
+def states_kernel(ks, extra, me_ref, q_hbm, k_hbm, v_hbm, d_hbm, *refs):
+    held_ref, sems = refs[-2:]
+    pairs = (k_hbm, v_hbm, q_hbm, d_hbm)
+    every = ks + extra
+
+    def copy(n, i):
+        target = held_ref.at[n, i] if n < len(ks) else refs[2 * len(ks)].at[n - len(ks), i]
+        return pltpu.make_async_copy(pairs[i].at[:, head_columns(me_ref, every[n])], target, sems.at[n, i])
+
+    copies = [[copy(n, i) for i in range(4)] for n in range(len(every))]
+    for group in copies:
+        for item in group:
+            item.start()
+    for axis in range(2):
+        for n in range(len(ks)):
+            copies[n][2 * axis].wait()
+            copies[n][2 * axis + 1].wait()
+            sub_states(held_ref[n, 2 * axis], held_ref[n, 2 * axis + 1], axis, refs[2 * n + 1], refs[2 * n])
+    for group in copies[len(ks) :]:
+        for item in group:
+            item.wait()
+
+
+def state_shapes(length):
+    return [
+        jax.ShapeDtypeStruct((2, DH, DH), F32),
+        jax.ShapeDtypeStruct((length // CHUNK, 2, DH, DH), F32),
     ]
-    for group in copies:
-        for copy in group:
-            copy.start()
-    for n in range(len(ks)):
-        for copy in copies[n][:2]:
-            copy.wait()
-        outs[n][0] = mm_first(k_ref[n], v_ref[n])
-        for copy in copies[n][2:]:
-            copy.wait()
-        outs[n][1] = mm_first(q_ref[n], d_ref[n])
-
-
-def head_states(ks, me, arrays):
+
+
+def head_states(ks, extra, me, arrays):
     length = arrays[0].shape[0]
-    return pl.pallas_call(
-        functools.partial(states_kernel, ks),
-        out_shape=[jax.ShapeDtypeStruct((2, DH, DH), F32)] * len(ks),
+    every = len(ks) + len(extra)
+    held = [jax.ShapeDtypeStruct((len(extra), 4, length, DH), BF16)] if extra else []
+    return pl.pallas_call(
+        functools.partial(states_kernel, ks, extra),
+        out_shape=state_shapes(length) * len(ks) + held,
         in_specs=[SMEM] + [HBM] * 4,
-        out_specs=[VMEM] * len(ks),
-        scratch_shapes=[pltpu.VMEM((len(ks), length, DH), BF16)] * 4 + [pltpu.SemaphoreType.DMA((len(ks), 4))],
+        out_specs=[VMEM] * (2 * len(ks) + len(held)),
+        scratch_shapes=[pltpu.VMEM((len(ks), 4, length, DH), BF16), pltpu.SemaphoreType.DMA((every, 4))],
         compiler_params=params(16),
         cost_estimate=pl.CostEstimate(
-            flops=4 * len(ks) * length * DH * DH, bytes_accessed=8 * len(ks) * length * DH, transcendentals=0
+            flops=4 * len(ks) * length * DH * DH, bytes_accessed=8 * every * length * DH, transcendentals=0
         ),
         name="head_states",
     )(me, *arrays)
 
 
-def local_kernel(which, me_ref, after_ref, q_ref, k_ref, v_ref, d_ref, att_ref, gq_ref, gk_ref, gv_ref, sub_ref, keep_ref):
-    chunks = q_ref.shape[0] // CHUNK
+def held_kernel(held_ref, *refs):
+    for n in range(held_ref.shape[0]):
+        for axis in range(2):
+            sub_states(held_ref[n, 2 * axis], held_ref[n, 2 * axis + 1], axis, refs[2 * n + 1], refs[2 * n])
+
+
+def held_states(held):
+    count, _, length, _ = held.shape
+    return pl.pallas_call(
+        held_kernel,
+        out_shape=state_shapes(length) * count,
+        in_specs=[VMEM],
+        out_specs=[VMEM] * (2 * count),
+        compiler_params=params(8),
+        cost_estimate=pl.CostEstimate(
+            flops=4 * count * length * DH * DH, bytes_accessed=8 * count * length * DH, transcendentals=0
+        ),
+        name="held_states",
+    )(held)
+
+
+def local_kernel(ks, me_ref, after_ref, q_ref, k_ref, v_ref, d_ref, *refs):
+    length = q_ref.shape[0]
     rows = lax.broadcasted_iota(jnp.int32, (CHUNK, CHUNK), 0)
     cols = lax.broadcasted_iota(jnp.int32, (CHUNK, CHUNK), 1)
     lower = rows >= cols
     upper = rows <= cols
-    columns = head_columns(me_ref, which)
-    state = jnp.zeros((DH, DH), F32)
-    grads = []
-    for c in range(chunks):
-        at = slice(c * CHUNK, (c + 1) * CHUNK)
-        q, k, v, d = q_ref[at, columns], k_ref[at, columns], v_ref[at, columns], d_ref[at, columns]
-        weights = jnp.where(lower, mm_last(q, k), 0.0).astype(BF16)
-        back = jnp.where(lower, mm_last(d, v), 0.0).astype(BF16)
-        weights_t = jnp.where(upper, mm_last(k, q), 0.0).astype(BF16)
-        back_t = jnp.where(upper, mm_last(v, d), 0.0).astype(BF16)
-        att_ref[at, :] = mm(weights, v)
-        gq_ref[at, :] = mm(back, k)
-        gk_ref[at, :] = mm(back_t, q)
-        gv_ref[at, :] = mm(weights_t, d)
-        sub_ref[c, 0] = state
-        state = state + mm_first(k, v)
-        grads.append(mm_first(q, d))
-    keep_ref[0] = state
-    state = jnp.zeros((DH, DH), F32)
-    for c in reversed(range(chunks)):
-        sub_ref[c, 1] = state
-        state = state + grads[c]
-    keep_ref[1] = state
-
-
-def local_products(which, me, arrays, after):
+    for n, which in enumerate(ks):
+        att_ref, gq_ref, gk_ref, gv_ref = refs[4 * n : 4 * n + 4]
+        columns = head_columns(me_ref, which)
+        for c in range(length // CHUNK):
+            at = slice(c * CHUNK, (c + 1) * CHUNK)
+            q, k, v, d = q_ref[at, columns], k_ref[at, columns], v_ref[at, columns], d_ref[at, columns]
+            weights = jnp.where(lower, mm_last(q, k), 0.0).astype(BF16)
+            back = jnp.where(lower, mm_last(d, v), 0.0).astype(BF16)
+            weights_t = jnp.where(upper, mm_last(k, q), 0.0).astype(BF16)
+            back_t = jnp.where(upper, mm_last(v, d), 0.0).astype(BF16)
+            att_ref[at, :] = mm(weights, v)
+            gq_ref[at, :] = mm(back, k)
+            gk_ref[at, :] = mm(back_t, q)
+            gv_ref[at, :] = mm(weights_t, d)
+        if which == 0:
+            total_ref, sub_ref = refs[-3:-1]
+            sub_states(k_ref[:, columns], v_ref[:, columns], 0, sub_ref, total_ref)
+            sub_states(q_ref[:, columns], d_ref[:, columns], 1, sub_ref, total_ref)
+    refs[-1][...] = jnp.zeros_like(refs[-1])
+
+
+def local_products(ks, me, arrays, after):
     length = arrays[0].shape[0]
-    chunks = length // CHUNK
-    *products, keep = pl.pallas_call(
-        functools.partial(local_kernel, which),
-        out_shape=[jax.ShapeDtypeStruct((length, DH), F32)] * 4
-        + [jax.ShapeDtypeStruct((chunks, 2, DH, DH), F32), jax.ShapeDtypeStruct((2, DH, DH), F32)],
+    states = state_shapes(length) if 0 in ks else []
+    results = pl.pallas_call(
+        functools.partial(local_kernel, ks),
+        out_shape=[jax.ShapeDtypeStruct((length, DH), F32)] * (4 * len(ks))
+        + states
+        + [jax.ShapeDtypeStruct((8, DH), F32)],
         in_specs=[SMEM] + [VMEM] * 5,
-        out_specs=[VMEM] * 6,
+        out_specs=[VMEM] * (4 * len(ks) + len(states) + 1),
         compiler_params=params(16),
         cost_estimate=pl.CostEstimate(
-            flops=16 * length * CHUNK * DH, bytes_accessed=8 * length * DH, transcendentals=0
+            flops=16 * len(ks) * length * CHUNK * DH, bytes_accessed=8 * len(ks) * length * DH, transcendentals=0
         ),
         name="local_products",
     )(me, after, *arrays)
-    return products, keep
+    return [results[4 * n : 4 * n + 4] for n in range(len(ks))], results[4 * len(ks) : -1], results[-1]
 
 
 def final_kernel(factor, which, count, earlier, last, me_ref, q_ref, k_ref, v_ref, d_ref, *refs):
@@ -322,14 +360,14 @@
     held = tuple(pltpu.with_memory_space_constraint(array, pltpu.HBM) for array in arrays)
     me = jnp.reshape(lax.axis_index("ctx"), (1,))
     local = [None] * QUAD
-    send1, send2 = head_states((1, 2), me, held)
+    subs = [None] * QUAD
+    send1, subs[1], send2, subs[2], held3 = head_states((1, 2), (3,), me, held)
+    send3, subs[3] = held_states(held3)
+    got3 = swap(send3, 3)
+    got2 = swap(send2, 2)
     got1 = swap(send1, 1)
-    got2 = swap(send2, 2)
-    (send3,) = head_states((3,), me, held)
-    got3 = swap(send3, 3)
-    local[0], keep = local_products(0, me, arrays, send3)
-    local[1], after = local_products(1, me, arrays, keep)
-    local[2], after = local_products(2, me, arrays, after)
+    (local[0], local[1],), (keep, subs[0]), after = local_products((0, 1), me, arrays, send3)
+    (local[2],), _, after = local_products((2,), me, arrays, after)
     pieces = (keep, got1, got2, got3)
     known = pieces
     bits = []
@@ -347,7 +385,7 @@
     base = swap(chosen, bit)
     mine = quad_parts(me, chosen, pieces)
     early = {k: swap(mine[k], k) for k in EARLY}
-    local[3], after = local_products(3, me, arrays, mine[0])
+    (local[3],), _, after = local_products((3,), me, arrays, mine[0])
     if parts:
         base = quad_base(tuple(bits), me, base, parts)
     late = [k for k in range(1, QUAD) if k not in EARLY]
@@ -357,10 +395,10 @@
             given[k] = (swap(whole, k),)
     for k in EARLY:
         given[k] = (early[k], swap(base, k))
-    outs = head_outputs(factor, 0, me, arrays, given[0], local[0], outs=())
-    staged = [(k, head_outputs(factor, k, me, arrays, given[k], local[k])[0]) for k in ORDER[:2]]
+    outs = head_outputs(factor, 0, me, arrays, given[0], [*local[0], subs[0]], outs=())
+    staged = [(k, head_outputs(factor, k, me, arrays, given[k], [*local[k], subs[k]])[0]) for k in ORDER[:2]]
     k = ORDER[2]
-    return tuple(head_outputs(factor, k, me, arrays, given[k], local[k], staged, outs))
+    return tuple(head_outputs(factor, k, me, arrays, given[k], [*local[k], subs[k]], staged, outs))
 
 
 def solution(mesh):

time: 30.9 us -> 29.5 us (0.955)
  Pallas kernels: 14.3 us -> 12.7 us
    pallas_call x6 -> x5, Pallas kernels: 9.44 us -> 7.84 us  [the longest x3 5.03 us: local_products(): pl.pallas_call(functools.partial(local_kernel, ks), out_shape=[jax.ShapeD...]
  transfers between devices with their start and end apart: 7 -> 7, of which waited for: 4 -> 5; matrix products, arithmetic and copies ran while one was open for 0% -> 0% of each run, Pallas kernels for 33% -> 29%
where the time goes in v4:
time: 29.5 us; the launch traced here: 29.3 us
  Pallas kernels  12.7 us (43%)
  starting transfers between devices  10.9 us (37%)
  waiting for transfers between devices  4.93 us (17%)
  between operations  0.8 us (3%)
    ppermute x7, starting transfers between devices, swap(): lax.ppermute(value, 'ctx', [(i, i ^ bit) for i in range(lax.axis_size('ct...  10.9 us
    pallas_call x3, Pallas kernels, local_products(): pl.pallas_call(functools.partial(local_kernel, ks), out_shape=[jax.ShapeD...  5.03 us
    ppermute x7, waiting for transfers between devices, swap(): lax.ppermute(value, 'ctx', [(i, i ^ bit) for i in range(lax.axis_size('ct...  4.93 us
    pallas_call x4, Pallas kernels, head_outputs(): pl.pallas_call(functools.partial(final_kernel, factor, which, len(given),...  4.72 us
    pallas_call x1, Pallas kernels, head_states(): pl.pallas_call(functools.partial(states_kernel, ks, extra), out_shape=sta...  2.47 us
  transfers between devices with their start and end apart: 7, of which 5 were waited for; matrix products, arithmetic and copies ran while one was open for 0% of the time, Pallas kernels for 29%

profile of v4, /device:TPU:0, one launch (start us, length us, event | category | flops | bytes accessed | tf_op | source)
XLA Modules:
  0.0 29.3 jit_solution(4922250894071650281)
XLA Ops:
  0.7 2.5 %head_states.1 = (f32[2,128,128]{2,1,0:T(8,128)S(1)}, f32[4,2,128,128]{3,2,1,0:T(8,128)S(1)}, f32[2,128,128]{2,1,0:T(8,128)S(1)}, f32[4,2,128,128]{3,2,1,0:T(8,128)S(1)}, bf16[1,4,1024,128]{3,2,1,0:T(8,128)(2,1)S(1)}) custom-call(s32[1]{0:T(128)} %bitcast.me_ref, bf16[1024,512]{1,0:T(8,128)(2,1)} %q_ref.13, bf16[1024,512]{1,0:T(8,128)(2,1)} %k_ref.13, ...), custom_call_target="tpu_custom_call" | custom-call | flops 134217728 | bytes 3145728 | tf_op jit(solution)/shard_map/head_states/pallas_call | solution.py:94
  3.1 0.0 copy-start
  3.2 3.0 %collective-permute-start = (f32[2,128,128]{2,1,0:T(8,128)S(1)}, f32[2,128,128]{2,1,0:T(8,128)S(1)}, u32[]{:S(2)}, u32[]{:S(2)}) collective-permute-start(f32[2,128,128]{2,1,0:T(8,128)S(1)} %get-tuple-element.48), channel_id=1, source_target_pairs={{0,4},{4,0},{8,12},{12,8},{16,20},{20,16},{24,28},{28,24},{1,5},{5... | collective-permute-start | bytes 393224 | tf_op jit(solution)/shard_map/ppermute | solution.py:353
  6.2 1.6 %collective-permute-start.1 = (f32[2,128,128]{2,1,0:T(8,128)S(1)}, f32[2,128,128]{2,1,0:T(8,128)S(1)}, u32[]{:S(2)}, u32[]{:S(2)}) collective-permute-start(f32[2,128,128]{2,1,0:T(8,128)S(1)} %get-tuple-element.49), channel_id=1, source_target_pairs={{0,8},{4,12},{8,0},{12,4},{16,24},{20,28},{24,16},{28,20},{1,9},{5... | collective-permute-start | bytes 393224 | tf_op jit(solution)/shard_map/ppermute | solution.py:353
  7.7 0.3 %held_states.1 = (f32[2,128,128]{2,1,0:T(8,128)S(1)}, f32[4,2,128,128]{3,2,1,0:T(8,128)S(1)}) custom-call(bf16[1,4,1024,128]{3,2,1,0:T(8,128)(2,1)S(1)} %get-tuple-element.43.held_ref), custom_call_target="tpu_custom_call" | custom-call | flops 67108864 | bytes 1048576 | tf_op jit(solution)/shard_map/held_states/pallas_call | solution.py:116
  8.1 0.1 collective-permute-start.2
  8.2 2.5 %local_products.3 = (f32[1024,128]{1,0:T(8,128)S(1)}, f32[1024,128]{1,0:T(8,128)S(1)}, f32[1024,128]{1,0:T(8,128)S(1)}, f32[1024,128]{1,0:T(8,128)S(1)}, f32[102...) custom-call(s32[1]{0:T(128)} %bitcast.me_ref, ...), custom_call_target="tpu_custom_call" | custom-call | flops 1073741824 | bytes 2097152 | tf_op jit(solution)/shard_map/local_products/pallas_call | solution.py:159
  10.7 1.3 %local_products.4 = (f32[1024,128]{1,0:T(8,128)S(1)}, f32[1024,128]{1,0:T(8,128)S(1)}, f32[1024,128]{1,0:T(8,128)S(1)}, f32[1024,128]{1,0:T(8,128)S(1)}, f32[8,128]{1,0:T(8,128)S(1)}) custom-call(s32[1]{0:T(128)} %bitcast.me_ref, f32[8,128]{1,0:T(8,128)S(1)} %get-tuple-element.45.after_ref, bf16[1024,512]{1,0:T(8,128)(2,1)S(1)} %copy-done, ...), custom_call_target="tpu_custom_call" | custom-call | flops 536870912 | bytes 1048576 | tf_op jit(solution)/shard_map/local_products/pallas_call | solution.py:159
  12.0 0.3 collective-permute-done.1.refs_2_
  12.3 1.7 %collective-permute-done.2.refs_3_ = f32[2,128,128]{2,1,0:T(8,128)S(1)} collective-permute-done((f32[2,128,128]{2,1,0:T(8,128)S(1)}, f32[2,128,128]{2,1,0:T(8,128)S(1)}, u32[]{:S(2)}, u32[]{:S(2)}) %collective-permute-start.2) | collective-permute-done | bytes 131104 | tf_op jit(solution)/shard_map/ppermute | solution.py:353
  14.0 2.7 %collective-permute-start.3 = (f32[1,128,128]{2,1,0:T(8,128)S(1)}, f32[1,128,128]{2,1,0:T(8,128)S(1)}, u32[]{:S(2)}, u32[]{:S(2)}) collective-permute-start(f32[1,128,128]{2,1,0:T(8,128)S(1)} %pick_state.1.after_ref), channel_id=1, source_target_pairs={{0,16},{4,20},{8,24},{12,28},{16,0},{20,4},{24,8},{28,12},{1,17},{... | collective-permute-start | bytes 196616 | tf_op jit(solution)/shard_map/ppermute | solution.py:353
  16.7 0.1 quad_parts.1
  16.8 1.3 %local_products.5 = (f32[1024,128]{1,0:T(8,128)S(1)}, f32[1024,128]{1,0:T(8,128)S(1)}, f32[1024,128]{1,0:T(8,128)S(1)}, f32[1024,128]{1,0:T(8,128)S(1)}, f32[8,128]{1,0:T(8,128)S(1)}) custom-call(s32[1]{0:T(128)} %bitcast.me_ref, f32[2,128,128]{2,1,0:T(8,128)S(1)} %get-tuple-element.50.after_ref.refs_0_, bf16[1024,512]{1,0:T(8,128)(2,1)S(1)} %copy-done, ...), custom_call_target="tpu_custom_call" | custom-call | flops 536870912 | bytes 1048576 | tf_op jit(solution)/shard_map/local_products/pallas_call | solution.py:159
  18.1 1.2 %collective-permute-done.3.base_ref.refs_1_ = f32[1,128,128]{2,1,0:T(8,128)S(1)} collective-permute-done((f32[1,128,128]{2,1,0:T(8,128)S(1)}, f32[1,128,128]{2,1,0:T(8,128)S(1)}, u32[]{:S(2)}, u32[]{:S(2)}) %collective-permute-start.3) | collective-permute-done | bytes 65568 | tf_op jit(solution)/shard_map/ppermute | solution.py:353
  19.3 2.5 %collective-permute-start.5 = (f32[2,128,128]{2,1,0:T(8,128)S(1)}, f32[2,128,128]{2,1,0:T(8,128)S(1)}, u32[]{:S(2)}, u32[]{:S(2)}) collective-permute-start(f32[2,128,128]{2,1,0:T(8,128)S(1)} %get-tuple-element.61), channel_id=1, source_target_pairs={{0,12},{4,8},{8,4},{12,0},{16,28},{20,24},{24,20},{28,16},{1,13},{... | collective-permute-start | bytes 393224 | tf_op jit(solution)/shard_map/ppermute | solution.py:353
  21.8 0.5 %collective-permute-start.6 = (f32[2,128,128]{2,1,0:T(8,128)S(1)}, f32[2,128,128]{2,1,0:T(8,128)S(1)}, u32[]{:S(2)}, u32[]{:S(2)}) collective-permute-start(f32[2,128,128]{2,1,0:T(8,128)S(1)} %get-tuple-element.67), channel_id=1, source_target_pairs={{0,4},{4,0},{8,12},{12,8},{16,20},{20,16},{24,28},{28,24},{1,5},{5... | collective-permute-start | bytes 393224 | tf_op jit(solution)/shard_map/ppermute | solution.py:353
  22.3 0.6 %collective-permute-start.4 = (f32[2,128,128]{2,1,0:T(8,128)S(1)}, f32[2,128,128]{2,1,0:T(8,128)S(1)}, u32[]{:S(2)}, u32[]{:S(2)}) collective-permute-start(f32[2,128,128]{2,1,0:T(8,128)S(1)} %get-tuple-element.55), channel_id=1, source_target_pairs={{0,8},{4,12},{8,0},{12,4},{16,24},{20,28},{24,16},{28,20},{1,9},{5... | collective-permute-start | bytes 393224 | tf_op jit(solution)/shard_map/ppermute | solution.py:353
  22.9 1.5 %head_outputs.6 = (bf16[1024,512]{1,0:T(8,128)(2,1)}, bf16[1024,512]{1,0:T(8,128)(2,1)}, bf16[1024,512]{1,0:T(8,128)(2,1)}, bf16[1024,512]{1,0:T(8,128)(2,1)}) custom-call(s32[1]{0:T(128)} %bitcast.me_ref, bf16[1024,512]{1,0:T(8,128)(2,1)S(1)} %copy-done, bf16[1024,512]{1,0:T(8,128)(2,1)S(1)} %copy-done.1, bf16[1024,512]{1,0:T(8,128)(2,1)S(1)} %copy-done.2, ...), custom_call_target="tpu_custom_call" | custom-call | flops 268435456 | bytes 1048576 | tf_op jit(solution)/shard_map/head_outputs/pallas_call | solution.py:236
  24.3 1.0 %collective-permute-done.5.refs_0_ = f32[2,128,128]{2,1,0:T(8,128)S(1)} collective-permute-done((f32[2,128,128]{2,1,0:T(8,128)S(1)}, f32[2,128,128]{2,1,0:T(8,128)S(1)}, u32[]{:S(2)}, u32[]{:S(2)}) %collective-permute-start.5) | collective-permute-done | bytes 131104 | tf_op jit(solution)/shard_map/ppermute | solution.py:353
  25.4 0.7 %head_outputs.4.refs_6_ = bf16[4,1024,128]{2,1,0:T(8,128)(2,1)S(1)} custom-call(s32[1]{0:T(128)} %bitcast.me_ref, bf16[1024,512]{1,0:T(8,128)(2,1)S(1)} %copy-done, bf16[1024,512]{1,0:T(8,128)(2,1)S(1)} %copy-done.1, bf16[1024,512]{1,0:T(8,128)(2,1)S(1)} %copy-done.2, bf16[1024,512]{1,0:T(8,128)(2,1)S(1)} %copy-done.3, ...), custom_call_target="tpu_custom_call" | custom-call | flops 268435456 | bytes 1048576 | tf_op jit(solution)/shard_map/head_outputs/pallas_call | solution.py:236
  26.1 0.7 %collective-permute-done.6.refs_0_ = f32[2,128,128]{2,1,0:T(8,128)S(1)} collective-permute-done((f32[2,128,128]{2,1,0:T(8,128)S(1)}, f32[2,128,128]{2,1,0:T(8,128)S(1)}, u32[]{:S(2)}, u32[]{:S(2)}) %collective-permute-start.6) | collective-permute-done | bytes 131104 | tf_op jit(solution)/shard_map/ppermute | solution.py:353
  26.8 0.7 %head_outputs.5.refs_7_ = bf16[4,1024,128]{2,1,0:T(8,128)(2,1)S(1)} custom-call(s32[1]{0:T(128)} %bitcast.me_ref, bf16[1024,512]{1,0:T(8,128)(2,1)S(1)} %copy-done, bf16[1024,512]{1,0:T(8,128)(2,1)S(1)} %copy-done.1, bf16[1024,512]{1,0:T(8,128)(2,1)S(1)} %copy-done.2, bf16[1024,512]{1,0:T(8,128)(2,1)S(1)} %copy-done.3, ...), custom_call_target="tpu_custom_call" | custom-call | flops 268435456 | bytes 1048576 | tf_op jit(solution)/shard_map/head_outputs/pallas_call | solution.py:236
  27.5 0.0 collective-permute-done.4.refs_0_
  27.5 1.8 %head_outputs.7 = (bf16[1024,512]{1,0:T(8,128)(2,1)}, bf16[1024,512]{1,0:T(8,128)(2,1)}, bf16[1024,512]{1,0:T(8,128)(2,1)}, bf16[1024,512]{1,0:T(8,128)(2,1)}) custom-call(s32[1]{0:T(128)} %bitcast.me_ref, bf16[1024,512]{1,0:T(8,128)(2,1)S(1)} %copy-done, ...), custom_call_target="tpu_custom_call", output_to_operand_aliasing={{0}: (13, {}), {1}: (14, {}), {2}: (15, {}), {3}: (16, {})} | custom-call | flops 268435456 | bytes 1048576 | tf_op jit(solution)/shard_map/head_outputs/pallas_call | solution.py:236
  (10 shorter events, 0.1 us)
Async XLA Ops:
  0.6 7.5 %copy-start.1 = (bf16[1024,512]{1,0:T(8,128)(2,1)S(1)}, bf16[1024,512]{1,0:T(8,128)(2,1)}, u32[]{:S(2)}) copy-start(bf16[1024,512]{1,0:T(8,128)(2,1)} %k_ref.13) | copy-start | bytes 3145732
  0.6 7.5 %copy-start.2 = (bf16[1024,512]{1,0:T(8,128)(2,1)S(1)}, bf16[1024,512]{1,0:T(8,128)(2,1)}, u32[]{:S(2)}) copy-start(bf16[1024,512]{1,0:T(8,128)(2,1)} %v_ref.13) | copy-start | bytes 3145732
  0.7 7.5 %copy-start.3 = (bf16[1024,512]{1,0:T(8,128)(2,1)S(1)}, bf16[1024,512]{1,0:T(8,128)(2,1)}, u32[]{:S(2)}) copy-start(bf16[1024,512]{1,0:T(8,128)(2,1)} %d_ref.13) | copy-start | bytes 3145732
  3.1 5.0 %copy-start = (bf16[1024,512]{1,0:T(8,128)(2,1)S(1)}, bf16[1024,512]{1,0:T(8,128)(2,1)}, u32[]{:S(2)}) copy-start(bf16[1024,512]{1,0:T(8,128)(2,1)} %q_ref.13) | copy-start | bytes 3145732
  3.2 8.8 %collective-permute-start = (f32[2,128,128]{2,1,0:T(8,128)S(1)}, f32[2,128,128]{2,1,0:T(8,128)S(1)}, u32[]{:S(2)}, u32[]{:S(2)}) collective-permute-start(f32[2,128,128]{2,1,0:T(8,128)S(1)} %get-tuple-element.48), channel_id=1, source_target_pairs={{0,4},{4,0},{8,12},{12,8},{16,20},{20,16},{24,28},{28,24},{1,5},{5... | collective-permute-start | bytes 393224 | tf_op jit(solution)/shard_map/ppermute | solution.py:353
  6.2 6.1 %collective-permute-start.1 = (f32[2,128,128]{2,1,0:T(8,128)S(1)}, f32[2,128,128]{2,1,0:T(8,128)S(1)}, u32[]{:S(2)}, u32[]{:S(2)}) collective-permute-start(f32[2,128,128]{2,1,0:T(8,128)S(1)} %get-tuple-element.49), channel_id=1, source_target_pairs={{0,8},{4,12},{8,0},{12,4},{16,24},{20,28},{24,16},{28,20},{1,9},{5... | collective-permute-start | bytes 393224 | tf_op jit(solution)/shard_map/ppermute | solution.py:353
  8.1 5.9 %collective-permute-start.2 = (f32[2,128,128]{2,1,0:T(8,128)S(1)}, f32[2,128,128]{2,1,0:T(8,128)S(1)}, u32[]{:S(2)}, u32[]{:S(2)}) collective-permute-start(f32[2,128,128]{2,1,0:T(8,128)S(1)} %get-tuple-element.44.after_ref), channel_id=1, source_target_pairs={{0,12},{4,8},{8,4},{12,0},{16,28},{20,24},{24,20},{28,16},{1,13},{... | collective-permute-start | bytes 393224 | tf_op jit(solution)/shard_map/ppermute | solution.py:353
  14.0 5.2 %collective-permute-start.3 = (f32[1,128,128]{2,1,0:T(8,128)S(1)}, f32[1,128,128]{2,1,0:T(8,128)S(1)}, u32[]{:S(2)}, u32[]{:S(2)}) collective-permute-start(f32[1,128,128]{2,1,0:T(8,128)S(1)} %pick_state.1.after_ref), channel_id=1, source_target_pairs={{0,16},{4,20},{8,24},{12,28},{16,0},{20,4},{24,8},{28,12},{1,17},{... | collective-permute-start | bytes 196616 | tf_op jit(solution)/shard_map/ppermute | solution.py:353
  19.3 6.1 %collective-permute-start.5 = (f32[2,128,128]{2,1,0:T(8,128)S(1)}, f32[2,128,128]{2,1,0:T(8,128)S(1)}, u32[]{:S(2)}, u32[]{:S(2)}) collective-permute-start(f32[2,128,128]{2,1,0:T(8,128)S(1)} %get-tuple-element.61), channel_id=1, source_target_pairs={{0,12},{4,8},{8,4},{12,0},{16,28},{20,24},{24,20},{28,16},{1,13},{... | collective-permute-start | bytes 393224 | tf_op jit(solution)/shard_map/ppermute | solution.py:353
  21.8 5.0 %collective-permute-start.6 = (f32[2,128,128]{2,1,0:T(8,128)S(1)}, f32[2,128,128]{2,1,0:T(8,128)S(1)}, u32[]{:S(2)}, u32[]{:S(2)}) collective-permute-start(f32[2,128,128]{2,1,0:T(8,128)S(1)} %get-tuple-element.67), channel_id=1, source_target_pairs={{0,4},{4,0},{8,12},{12,8},{16,20},{20,16},{24,28},{28,24},{1,5},{5... | collective-permute-start | bytes 393224 | tf_op jit(solution)/shard_map/ppermute | solution.py:353
  22.3 5.2 %collective-permute-start.4 = (f32[2,128,128]{2,1,0:T(8,128)S(1)}, f32[2,128,128]{2,1,0:T(8,128)S(1)}, u32[]{:S(2)}, u32[]{:S(2)}) collective-permute-start(f32[2,128,128]{2,1,0:T(8,128)S(1)} %get-tuple-element.55), channel_id=1, source_target_pairs={{0,8},{4,12},{8,0},{12,4},{16,24},{20,28},{24,16},{28,20},{1,9},{5... | collective-permute-start | bytes 393224 | tf_op jit(solution)/shard_map/ppermute | solution.py:353

commit v5 on v4

--- a/solution.py
+++ b/solution.py
@@ -11,6 +11,7 @@
 DH = 128
 HEADS = 4
 QUAD = 4
+PARTNERS = (0, 3, 2, 1)
 EARLY = ()
 ORDER = (3, 1, 2)
 CHUNK = 256
@@ -40,7 +41,7 @@
 
 
 def head_columns(me_ref, k):
-    return pl.ds(pl.multiple_of((lax.rem(me_ref[0], QUAD) ^ k) * DH, DH), DH)
+    return pl.ds(pl.multiple_of((lax.rem(me_ref[0], QUAD) ^ PARTNERS[k]) * DH, DH), DH)
 
 
 def params(mib):
@@ -284,7 +285,7 @@
         prefix, suffix = zero, zero
         for j, piece in enumerate(pieces):
             if j != k:
-                before = (rank ^ j) < (rank ^ k)
+                before = (rank ^ PARTNERS[j]) < (rank ^ PARTNERS[k])
                 prefix += jnp.where(before, piece[0], zero)
                 suffix += jnp.where(before, zero, piece[1])
         out[0] = prefix
@@ -363,9 +364,9 @@
     subs = [None] * QUAD
     send1, subs[1], send2, subs[2], held3 = head_states((1, 2), (3,), me, held)
     send3, subs[3] = held_states(held3)
-    got3 = swap(send3, 3)
-    got2 = swap(send2, 2)
-    got1 = swap(send1, 1)
+    got3 = swap(send3, PARTNERS[3])
+    got2 = swap(send2, PARTNERS[2])
+    got1 = swap(send1, PARTNERS[1])
     (local[0], local[1],), (keep, subs[0]), after = local_products((0, 1), me, arrays, send3)
     (local[2],), _, after = local_products((2,), me, arrays, after)
     pieces = (keep, got1, got2, got3)
@@ -384,7 +385,7 @@
     chosen = combine(functools.partial(part_kernel, bit), 1, me, after, known, "pick_state")
     base = swap(chosen, bit)
     mine = quad_parts(me, chosen, pieces)
-    early = {k: swap(mine[k], k) for k in EARLY}
+    early = {k: swap(mine[k], PARTNERS[k]) for k in EARLY}
     (local[3],), _, after = local_products((3,), me, arrays, mine[0])
     if parts:
         base = quad_base(tuple(bits), me, base, parts)
@@ -392,9 +393,9 @@
     given = {0: (mine[0], base)}
     if late:
         for k, whole in zip(late, whole_states(me, after, base, [mine[k] for k in late])):
-            given[k] = (swap(whole, k),)
+            given[k] = (swap(whole, PARTNERS[k]),)
     for k in EARLY:
-        given[k] = (early[k], swap(base, k))
+        given[k] = (early[k], swap(base, PARTNERS[k]))
     outs = head_outputs(factor, 0, me, arrays, given[0], [*local[0], subs[0]], outs=())
     staged = [(k, head_outputs(factor, k, me, arrays, given[k], [*local[k], subs[k]])[0]) for k in ORDER[:2]]
     k = ORDER[2]

time: 29.5 us -> 29.3 us (level)
  transfers between devices with their start and end apart: 7 -> 7, of which waited for: 5 -> 4; matrix products, arithmetic and copies ran while one was open for 0% -> 0% of each run, Pallas kernels for 29% -> 29%
where the time goes in v5:
time: 29.3 us; the launch traced here: 29.2 us
  Pallas kernels  12.7 us (43%)
  starting transfers between devices  11 us (38%)
  waiting for transfers between devices  4.67 us (16%)
  between operations  0.77 us (3%)
    ppermute x7, starting transfers between devices, swap(): lax.ppermute(value, 'ctx', [(i, i ^ bit) for i in range(lax.axis_size('ct...  11 us
    pallas_call x3, Pallas kernels, local_products(): pl.pallas_call(functools.partial(local_kernel, ks), out_shape=[jax.ShapeD...  5.03 us
    pallas_call x4, Pallas kernels, head_outputs(): pl.pallas_call(functools.partial(final_kernel, factor, which, len(given),...  4.74 us
    ppermute x7, waiting for transfers between devices, swap(): lax.ppermute(value, 'ctx', [(i, i ^ bit) for i in range(lax.axis_size('ct...  4.67 us
    pallas_call x1, Pallas kernels, head_states(): pl.pallas_call(functools.partial(states_kernel, ks, extra), out_shape=sta...  2.47 us
  transfers between devices with their start and end apart: 7, of which 4 were waited for; matrix products, arithmetic and copies ran while one was open for 0% of the time, Pallas kernels for 29%

profile of v5, /device:TPU:0, one launch (start us, length us, event | category | flops | bytes accessed | tf_op | source)
XLA Modules:
  0.0 29.2 jit_solution(10411912857369475325)
XLA Ops:
  0.7 2.5 %head_states.1 = (f32[2,128,128]{2,1,0:T(8,128)S(1)}, f32[4,2,128,128]{3,2,1,0:T(8,128)S(1)}, f32[2,128,128]{2,1,0:T(8,128)S(1)}, f32[4,2,128,128]{3,2,1,0:T(8,128)S(1)}, bf16[1,4,1024,128]{3,2,1,0:T(8,128)(2,1)S(1)}) custom-call(s32[1]{0:T(128)} %bitcast.me_ref, bf16[1024,512]{1,0:T(8,128)(2,1)} %q_ref.13, bf16[1024,512]{1,0:T(8,128)(2,1)} %k_ref.13, ...), custom_call_target="tpu_custom_call" | custom-call | flops 134217728 | bytes 3145728 | tf_op jit(solution)/shard_map/head_states/pallas_call | solution.py:95
  3.1 0.0 copy-start
  3.2 4.0 %collective-permute-start = (f32[2,128,128]{2,1,0:T(8,128)S(1)}, f32[2,128,128]{2,1,0:T(8,128)S(1)}, u32[]{:S(2)}, u32[]{:S(2)}) collective-permute-start(f32[2,128,128]{2,1,0:T(8,128)S(1)} %get-tuple-element.48), channel_id=1, source_target_pairs={{0,12},{4,8},{8,4},{12,0},{16,28},{20,24},{24,20},{28,16},{1,13},{... | collective-permute-start | bytes 393224 | tf_op jit(solution)/shard_map/ppermute | solution.py:354
  7.2 0.4 %collective-permute-start.1 = (f32[2,128,128]{2,1,0:T(8,128)S(1)}, f32[2,128,128]{2,1,0:T(8,128)S(1)}, u32[]{:S(2)}, u32[]{:S(2)}) collective-permute-start(f32[2,128,128]{2,1,0:T(8,128)S(1)} %get-tuple-element.49), channel_id=1, source_target_pairs={{0,8},{4,12},{8,0},{12,4},{16,24},{20,28},{24,16},{28,20},{1,9},{5... | collective-permute-start | bytes 393224 | tf_op jit(solution)/shard_map/ppermute | solution.py:354
  7.6 0.3 %held_states.1 = (f32[2,128,128]{2,1,0:T(8,128)S(1)}, f32[4,2,128,128]{3,2,1,0:T(8,128)S(1)}) custom-call(bf16[1,4,1024,128]{3,2,1,0:T(8,128)(2,1)S(1)} %get-tuple-element.43.held_ref), custom_call_target="tpu_custom_call" | custom-call | flops 67108864 | bytes 1048576 | tf_op jit(solution)/shard_map/held_states/pallas_call | solution.py:117
  8.0 0.3 collective-permute-start.2
  8.2 2.5 %local_products.3 = (f32[1024,128]{1,0:T(8,128)S(1)}, f32[1024,128]{1,0:T(8,128)S(1)}, f32[1024,128]{1,0:T(8,128)S(1)}, f32[1024,128]{1,0:T(8,128)S(1)}, f32[102...) custom-call(s32[1]{0:T(128)} %bitcast.me_ref, ...), custom_call_target="tpu_custom_call" | custom-call | flops 1073741824 | bytes 2097152 | tf_op jit(solution)/shard_map/local_products/pallas_call | solution.py:160
  10.7 1.3 %local_products.4 = (f32[1024,128]{1,0:T(8,128)S(1)}, f32[1024,128]{1,0:T(8,128)S(1)}, f32[1024,128]{1,0:T(8,128)S(1)}, f32[1024,128]{1,0:T(8,128)S(1)}, f32[8,128]{1,0:T(8,128)S(1)}) custom-call(s32[1]{0:T(128)} %bitcast.me_ref, f32[8,128]{1,0:T(8,128)S(1)} %get-tuple-element.45.after_ref, bf16[1024,512]{1,0:T(8,128)(2,1)S(1)} %copy-done, ...), custom_call_target="tpu_custom_call" | custom-call | flops 536870912 | bytes 1048576 | tf_op jit(solution)/shard_map/local_products/pallas_call | solution.py:160
  12.0 0.0 collective-permute-done.refs_1_
  12.0 1.6 %collective-permute-done.1.refs_2_ = f32[2,128,128]{2,1,0:T(8,128)S(1)} collective-permute-done((f32[2,128,128]{2,1,0:T(8,128)S(1)}, f32[2,128,128]{2,1,0:T(8,128)S(1)}, u32[]{:S(2)}, u32[]{:S(2)}) %collective-permute-start.1) | collective-permute-done | bytes 131104 | tf_op jit(solution)/shard_map/ppermute | solution.py:354
  13.6 0.0 collective-permute-done.2.refs_3_
  13.7 2.7 %collective-permute-start.3 = (f32[1,128,128]{2,1,0:T(8,128)S(1)}, f32[1,128,128]{2,1,0:T(8,128)S(1)}, u32[]{:S(2)}, u32[]{:S(2)}) collective-permute-start(f32[1,128,128]{2,1,0:T(8,128)S(1)} %pick_state.1.after_ref), channel_id=1, source_target_pairs={{0,16},{4,20},{8,24},{12,28},{16,0},{20,4},{24,8},{28,12},{1,17},{... | collective-permute-start | bytes 196616 | tf_op jit(solution)/shard_map/ppermute | solution.py:354
  16.4 0.1 quad_parts.1
  16.5 1.3 %local_products.5 = (f32[1024,128]{1,0:T(8,128)S(1)}, f32[1024,128]{1,0:T(8,128)S(1)}, f32[1024,128]{1,0:T(8,128)S(1)}, f32[1024,128]{1,0:T(8,128)S(1)}, f32[8,128]{1,0:T(8,128)S(1)}) custom-call(s32[1]{0:T(128)} %bitcast.me_ref, f32[2,128,128]{2,1,0:T(8,128)S(1)} %get-tuple-element.50.after_ref.refs_0_, bf16[1024,512]{1,0:T(8,128)(2,1)S(1)} %copy-done, ...), custom_call_target="tpu_custom_call" | custom-call | flops 536870912 | bytes 1048576 | tf_op jit(solution)/shard_map/local_products/pallas_call | solution.py:160
  17.8 1.2 %collective-permute-done.3.base_ref.refs_1_ = f32[1,128,128]{2,1,0:T(8,128)S(1)} collective-permute-done((f32[1,128,128]{2,1,0:T(8,128)S(1)}, f32[1,128,128]{2,1,0:T(8,128)S(1)}, u32[]{:S(2)}, u32[]{:S(2)}) %collective-permute-start.3) | collective-permute-done | bytes 65568 | tf_op jit(solution)/shard_map/ppermute | solution.py:354
  19.0 1.8 %collective-permute-start.5 = (f32[2,128,128]{2,1,0:T(8,128)S(1)}, f32[2,128,128]{2,1,0:T(8,128)S(1)}, u32[]{:S(2)}, u32[]{:S(2)}) collective-permute-start(f32[2,128,128]{2,1,0:T(8,128)S(1)} %get-tuple-element.61), channel_id=1, source_target_pairs={{0,4},{4,0},{8,12},{12,8},{16,20},{20,16},{24,28},{28,24},{1,5},{5... | collective-permute-start | bytes 393224 | tf_op jit(solution)/shard_map/ppermute | solution.py:354
  20.8 1.4 %collective-permute-start.6 = (f32[2,128,128]{2,1,0:T(8,128)S(1)}, f32[2,128,128]{2,1,0:T(8,128)S(1)}, u32[]{:S(2)}, u32[]{:S(2)}) collective-permute-start(f32[2,128,128]{2,1,0:T(8,128)S(1)} %get-tuple-element.67), channel_id=1, source_target_pairs={{0,12},{4,8},{8,4},{12,0},{16,28},{20,24},{24,20},{28,16},{1,13},{... | collective-permute-start | bytes 393224 | tf_op jit(solution)/shard_map/ppermute | solution.py:354
  22.1 0.4 %collective-permute-start.4 = (f32[2,128,128]{2,1,0:T(8,128)S(1)}, f32[2,128,128]{2,1,0:T(8,128)S(1)}, u32[]{:S(2)}, u32[]{:S(2)}) collective-permute-start(f32[2,128,128]{2,1,0:T(8,128)S(1)} %get-tuple-element.55), channel_id=1, source_target_pairs={{0,8},{4,12},{8,0},{12,4},{16,24},{20,28},{24,16},{28,20},{1,9},{5... | collective-permute-start | bytes 393224 | tf_op jit(solution)/shard_map/ppermute | solution.py:354
  22.5 1.5 %head_outputs.6 = (bf16[1024,512]{1,0:T(8,128)(2,1)}, bf16[1024,512]{1,0:T(8,128)(2,1)}, bf16[1024,512]{1,0:T(8,128)(2,1)}, bf16[1024,512]{1,0:T(8,128)(2,1)}) custom-call(s32[1]{0:T(128)} %bitcast.me_ref, bf16[1024,512]{1,0:T(8,128)(2,1)S(1)} %copy-done, bf16[1024,512]{1,0:T(8,128)(2,1)S(1)} %copy-done.1, bf16[1024,512]{1,0:T(8,128)(2,1)S(1)} %copy-done.2, ...), custom_call_target="tpu_custom_call" | custom-call | flops 268435456 | bytes 1048576 | tf_op jit(solution)/shard_map/head_outputs/pallas_call | solution.py:237
  24.0 1.1 %collective-permute-done.5.refs_0_ = f32[2,128,128]{2,1,0:T(8,128)S(1)} collective-permute-done((f32[2,128,128]{2,1,0:T(8,128)S(1)}, f32[2,128,128]{2,1,0:T(8,128)S(1)}, u32[]{:S(2)}, u32[]{:S(2)}) %collective-permute-start.5) | collective-permute-done | bytes 131104 | tf_op jit(solution)/shard_map/ppermute | solution.py:354
  25.1 0.7 %head_outputs.4.refs_6_ = bf16[4,1024,128]{2,1,0:T(8,128)(2,1)S(1)} custom-call(s32[1]{0:T(128)} %bitcast.me_ref, bf16[1024,512]{1,0:T(8,128)(2,1)S(1)} %copy-done, bf16[1024,512]{1,0:T(8,128)(2,1)S(1)} %copy-done.1, bf16[1024,512]{1,0:T(8,128)(2,1)S(1)} %copy-done.2, bf16[1024,512]{1,0:T(8,128)(2,1)S(1)} %copy-done.3, ...), custom_call_target="tpu_custom_call" | custom-call | flops 268435456 | bytes 1048576 | tf_op jit(solution)/shard_map/head_outputs/pallas_call | solution.py:237
  25.9 0.8 %collective-permute-done.6.refs_0_ = f32[2,128,128]{2,1,0:T(8,128)S(1)} collective-permute-done((f32[2,128,128]{2,1,0:T(8,128)S(1)}, f32[2,128,128]{2,1,0:T(8,128)S(1)}, u32[]{:S(2)}, u32[]{:S(2)}) %collective-permute-start.6) | collective-permute-done | bytes 131104 | tf_op jit(solution)/shard_map/ppermute | solution.py:354
  26.6 0.7 %head_outputs.5.refs_7_ = bf16[4,1024,128]{2,1,0:T(8,128)(2,1)S(1)} custom-call(s32[1]{0:T(128)} %bitcast.me_ref, bf16[1024,512]{1,0:T(8,128)(2,1)S(1)} %copy-done, bf16[1024,512]{1,0:T(8,128)(2,1)S(1)} %copy-done.1, bf16[1024,512]{1,0:T(8,128)(2,1)S(1)} %copy-done.2, bf16[1024,512]{1,0:T(8,128)(2,1)S(1)} %copy-done.3, ...), custom_call_target="tpu_custom_call" | custom-call | flops 268435456 | bytes 1048576 | tf_op jit(solution)/shard_map/head_outputs/pallas_call | solution.py:237
  27.4 1.8 %head_outputs.7 = (bf16[1024,512]{1,0:T(8,128)(2,1)}, bf16[1024,512]{1,0:T(8,128)(2,1)}, bf16[1024,512]{1,0:T(8,128)(2,1)}, bf16[1024,512]{1,0:T(8,128)(2,1)}) custom-call(s32[1]{0:T(128)} %bitcast.me_ref, bf16[1024,512]{1,0:T(8,128)(2,1)S(1)} %copy-done, ...), custom_call_target="tpu_custom_call", output_to_operand_aliasing={{0}: (13, {}), {1}: (14, {}), {2}: (15, {}), {3}: (16, {})} | custom-call | flops 268435456 | bytes 1048576 | tf_op jit(solution)/shard_map/head_outputs/pallas_call | solution.py:237
  (10 shorter events, 0.1 us)
Async XLA Ops:
  0.6 7.6 %copy-start.1 = (bf16[1024,512]{1,0:T(8,128)(2,1)S(1)}, bf16[1024,512]{1,0:T(8,128)(2,1)}, u32[]{:S(2)}) copy-start(bf16[1024,512]{1,0:T(8,128)(2,1)} %k_ref.13) | copy-start | bytes 3145732
  0.6 7.6 %copy-start.2 = (bf16[1024,512]{1,0:T(8,128)(2,1)S(1)}, bf16[1024,512]{1,0:T(8,128)(2,1)}, u32[]{:S(2)}) copy-start(bf16[1024,512]{1,0:T(8,128)(2,1)} %v_ref.13) | copy-start | bytes 3145732
  0.7 7.6 %copy-start.3 = (bf16[1024,512]{1,0:T(8,128)(2,1)S(1)}, bf16[1024,512]{1,0:T(8,128)(2,1)}, u32[]{:S(2)}) copy-start(bf16[1024,512]{1,0:T(8,128)(2,1)} %d_ref.13) | copy-start | bytes 3145732
  3.1 5.1 %copy-start = (bf16[1024,512]{1,0:T(8,128)(2,1)S(1)}, bf16[1024,512]{1,0:T(8,128)(2,1)}, u32[]{:S(2)}) copy-start(bf16[1024,512]{1,0:T(8,128)(2,1)} %q_ref.13) | copy-start | bytes 3145732
  3.2 8.9 %collective-permute-start = (f32[2,128,128]{2,1,0:T(8,128)S(1)}, f32[2,128,128]{2,1,0:T(8,128)S(1)}, u32[]{:S(2)}, u32[]{:S(2)}) collective-permute-start(f32[2,128,128]{2,1,0:T(8,128)S(1)} %get-tuple-element.48), channel_id=1, source_target_pairs={{0,12},{4,8},{8,4},{12,0},{16,28},{20,24},{24,20},{28,16},{1,13},{... | collective-permute-start | bytes 393224 | tf_op jit(solution)/shard_map/ppermute | solution.py:354
  7.2 6.5 %collective-permute-start.1 = (f32[2,128,128]{2,1,0:T(8,128)S(1)}, f32[2,128,128]{2,1,0:T(8,128)S(1)}, u32[]{:S(2)}, u32[]{:S(2)}) collective-permute-start(f32[2,128,128]{2,1,0:T(8,128)S(1)} %get-tuple-element.49), channel_id=1, source_target_pairs={{0,8},{4,12},{8,0},{12,4},{16,24},{20,28},{24,16},{28,20},{1,9},{5... | collective-permute-start | bytes 393224 | tf_op jit(solution)/shard_map/ppermute | solution.py:354
  8.0 5.7 %collective-permute-start.2 = (f32[2,128,128]{2,1,0:T(8,128)S(1)}, f32[2,128,128]{2,1,0:T(8,128)S(1)}, u32[]{:S(2)}, u32[]{:S(2)}) collective-permute-start(f32[2,128,128]{2,1,0:T(8,128)S(1)} %get-tuple-element.44.after_ref), channel_id=1, source_target_pairs={{0,4},{4,0},{8,12},{12,8},{16,20},{20,16},{24,28},{28,24},{1,5},{5... | collective-permute-start | bytes 393224 | tf_op jit(solution)/shard_map/ppermute | solution.py:354
  13.7 5.3 %collective-permute-start.3 = (f32[1,128,128]{2,1,0:T(8,128)S(1)}, f32[1,128,128]{2,1,0:T(8,128)S(1)}, u32[]{:S(2)}, u32[]{:S(2)}) collective-permute-start(f32[1,128,128]{2,1,0:T(8,128)S(1)} %pick_state.1.after_ref), channel_id=1, source_target_pairs={{0,16},{4,20},{8,24},{12,28},{16,0},{20,4},{24,8},{28,12},{1,17},{... | collective-permute-start | bytes 196616 | tf_op jit(solution)/shard_map/ppermute | solution.py:354
  19.0 6.1 %collective-permute-start.5 = (f32[2,128,128]{2,1,0:T(8,128)S(1)}, f32[2,128,128]{2,1,0:T(8,128)S(1)}, u32[]{:S(2)}, u32[]{:S(2)}) collective-permute-start(f32[2,128,128]{2,1,0:T(8,128)S(1)} %get-tuple-element.61), channel_id=1, source_target_pairs={{0,4},{4,0},{8,12},{12,8},{16,20},{20,16},{24,28},{28,24},{1,5},{5... | collective-permute-start | bytes 393224 | tf_op jit(solution)/shard_map/ppermute | solution.py:354
  20.8 5.9 %collective-permute-start.6 = (f32[2,128,128]{2,1,0:T(8,128)S(1)}, f32[2,128,128]{2,1,0:T(8,128)S(1)}, u32[]{:S(2)}, u32[]{:S(2)}) collective-permute-start(f32[2,128,128]{2,1,0:T(8,128)S(1)} %get-tuple-element.67), channel_id=1, source_target_pairs={{0,12},{4,8},{8,4},{12,0},{16,28},{20,24},{24,20},{28,16},{1,13},{... | collective-permute-start | bytes 393224 | tf_op jit(solution)/shard_map/ppermute | solution.py:354
  22.1 5.2 %collective-permute-start.4 = (f32[2,128,128]{2,1,0:T(8,128)S(1)}, f32[2,128,128]{2,1,0:T(8,128)S(1)}, u32[]{:S(2)}, u32[]{:S(2)}) collective-permute-start(f32[2,128,128]{2,1,0:T(8,128)S(1)} %get-tuple-element.55), channel_id=1, source_target_pairs={{0,8},{4,12},{8,0},{12,4},{16,24},{20,28},{24,16},{28,20},{1,9},{5... | collective-permute-start | bytes 393224 | tf_op jit(solution)/shard_map/ppermute | solution.py:354

commit v6 on v5

--- a/solution.py
+++ b/solution.py
@@ -68,7 +68,11 @@
         return pltpu.make_async_copy(pairs[i].at[:, head_columns(me_ref, every[n])], target, sems.at[n, i])
 
     copies = [[copy(n, i) for i in range(4)] for n in range(len(every))]
-    for group in copies:
+    for axis in range(2):
+        for group in copies[: len(ks)]:
+            group[2 * axis].start()
+            group[2 * axis + 1].start()
+    for group in copies[len(ks) :]:
         for item in group:
             item.start()
     for axis in range(2):

time: 29.3 us -> 29.3 us (level)
  no operation moved by 1% of the time
where the time goes in v6:
time: 29.3 us; the launch traced here: 29.1 us
  Pallas kernels  12.7 us (43%)
  starting transfers between devices  11 us (38%)
  waiting for transfers between devices  4.67 us (16%)
  between operations  0.77 us (3%)
    ppermute x7, starting transfers between devices, swap(): lax.ppermute(value, 'ctx', [(i, i ^ bit) for i in range(lax.axis_size('ct...  11 us
    pallas_call x3, Pallas kernels, local_products(): pl.pallas_call(functools.partial(local_kernel, ks), out_shape=[jax.ShapeD...  5.03 us
    pallas_call x4, Pallas kernels, head_outputs(): pl.pallas_call(functools.partial(final_kernel, factor, which, len(given),...  4.74 us
    ppermute x7, waiting for transfers between devices, swap(): lax.ppermute(value, 'ctx', [(i, i ^ bit) for i in range(lax.axis_size('ct...  4.67 us
    pallas_call x1, Pallas kernels, head_states(): pl.pallas_call(functools.partial(states_kernel, ks, extra), out_shape=sta...  2.4 us
  transfers between devices with their start and end apart: 7, of which 4 were waited for; matrix products, arithmetic and copies ran while one was open for 0% of the time, Pallas kernels for 29%

profile of v6, /device:TPU:0, one launch (start us, length us, event | category | flops | bytes accessed | tf_op | source)
XLA Modules:
  0.0 29.1 jit_solution(11762243884116231379)
XLA Ops:
  0.7 2.4 %head_states.1 = (f32[2,128,128]{2,1,0:T(8,128)S(1)}, f32[4,2,128,128]{3,2,1,0:T(8,128)S(1)}, f32[2,128,128]{2,1,0:T(8,128)S(1)}, f32[4,2,128,128]{3,2,1,0:T(8,128)S(1)}, bf16[1,4,1024,128]{3,2,1,0:T(8,128)(2,1)S(1)}) custom-call(s32[1]{0:T(128)} %bitcast.me_ref, bf16[1024,512]{1,0:T(8,128)(2,1)} %q_ref.13, bf16[1024,512]{1,0:T(8,128)(2,1)} %k_ref.13, ...), custom_call_target="tpu_custom_call" | custom-call | flops 134217728 | bytes 3145728 | tf_op jit(solution)/shard_map/head_states/pallas_call | solution.py:99
  3.1 0.0 copy-start
  3.1 4.0 %collective-permute-start = (f32[2,128,128]{2,1,0:T(8,128)S(1)}, f32[2,128,128]{2,1,0:T(8,128)S(1)}, u32[]{:S(2)}, u32[]{:S(2)}) collective-permute-start(f32[2,128,128]{2,1,0:T(8,128)S(1)} %get-tuple-element.48), channel_id=1, source_target_pairs={{0,12},{4,8},{8,4},{12,0},{16,28},{20,24},{24,20},{28,16},{1,13},{... | collective-permute-start | bytes 393224 | tf_op jit(solution)/shard_map/ppermute | solution.py:358
  7.1 0.4 %collective-permute-start.1 = (f32[2,128,128]{2,1,0:T(8,128)S(1)}, f32[2,128,128]{2,1,0:T(8,128)S(1)}, u32[]{:S(2)}, u32[]{:S(2)}) collective-permute-start(f32[2,128,128]{2,1,0:T(8,128)S(1)} %get-tuple-element.49), channel_id=1, source_target_pairs={{0,8},{4,12},{8,0},{12,4},{16,24},{20,28},{24,16},{28,20},{1,9},{5... | collective-permute-start | bytes 393224 | tf_op jit(solution)/shard_map/ppermute | solution.py:358
  7.6 0.3 %held_states.1 = (f32[2,128,128]{2,1,0:T(8,128)S(1)}, f32[4,2,128,128]{3,2,1,0:T(8,128)S(1)}) custom-call(bf16[1,4,1024,128]{3,2,1,0:T(8,128)(2,1)S(1)} %get-tuple-element.43.held_ref), custom_call_target="tpu_custom_call" | custom-call | flops 67108864 | bytes 1048576 | tf_op jit(solution)/shard_map/held_states/pallas_call | solution.py:121
  7.9 0.3 collective-permute-start.2
  8.2 2.5 %local_products.3 = (f32[1024,128]{1,0:T(8,128)S(1)}, f32[1024,128]{1,0:T(8,128)S(1)}, f32[1024,128]{1,0:T(8,128)S(1)}, f32[1024,128]{1,0:T(8,128)S(1)}, f32[102...) custom-call(s32[1]{0:T(128)} %bitcast.me_ref, ...), custom_call_target="tpu_custom_call" | custom-call | flops 1073741824 | bytes 2097152 | tf_op jit(solution)/shard_map/local_products/pallas_call | solution.py:164
  10.7 1.3 %local_products.4 = (f32[1024,128]{1,0:T(8,128)S(1)}, f32[1024,128]{1,0:T(8,128)S(1)}, f32[1024,128]{1,0:T(8,128)S(1)}, f32[1024,128]{1,0:T(8,128)S(1)}, f32[8,128]{1,0:T(8,128)S(1)}) custom-call(s32[1]{0:T(128)} %bitcast.me_ref, f32[8,128]{1,0:T(8,128)S(1)} %get-tuple-element.45.after_ref, bf16[1024,512]{1,0:T(8,128)(2,1)S(1)} %copy-done, ...), custom_call_target="tpu_custom_call" | custom-call | flops 536870912 | bytes 1048576 | tf_op jit(solution)/shard_map/local_products/pallas_call | solution.py:164
  11.9 0.0 collective-permute-done.refs_1_
  12.0 1.6 %collective-permute-done.1.refs_2_ = f32[2,128,128]{2,1,0:T(8,128)S(1)} collective-permute-done((f32[2,128,128]{2,1,0:T(8,128)S(1)}, f32[2,128,128]{2,1,0:T(8,128)S(1)}, u32[]{:S(2)}, u32[]{:S(2)}) %collective-permute-start.1) | collective-permute-done | bytes 131104 | tf_op jit(solution)/shard_map/ppermute | solution.py:358
  13.6 2.7 %collective-permute-start.3 = (f32[1,128,128]{2,1,0:T(8,128)S(1)}, f32[1,128,128]{2,1,0:T(8,128)S(1)}, u32[]{:S(2)}, u32[]{:S(2)}) collective-permute-start(f32[1,128,128]{2,1,0:T(8,128)S(1)} %pick_state.1.after_ref), channel_id=1, source_target_pairs={{0,16},{4,20},{8,24},{12,28},{16,0},{20,4},{24,8},{28,12},{1,17},{... | collective-permute-start | bytes 196616 | tf_op jit(solution)/shard_map/ppermute | solution.py:358
  16.3 0.1 quad_parts.1
  16.4 1.3 %local_products.5 = (f32[1024,128]{1,0:T(8,128)S(1)}, f32[1024,128]{1,0:T(8,128)S(1)}, f32[1024,128]{1,0:T(8,128)S(1)}, f32[1024,128]{1,0:T(8,128)S(1)}, f32[8,128]{1,0:T(8,128)S(1)}) custom-call(s32[1]{0:T(128)} %bitcast.me_ref, f32[2,128,128]{2,1,0:T(8,128)S(1)} %get-tuple-element.50.after_ref.refs_0_, bf16[1024,512]{1,0:T(8,128)(2,1)S(1)} %copy-done, ...), custom_call_target="tpu_custom_call" | custom-call | flops 536870912 | bytes 1048576 | tf_op jit(solution)/shard_map/local_products/pallas_call | solution.py:164
  17.7 1.2 %collective-permute-done.3.base_ref.refs_1_ = f32[1,128,128]{2,1,0:T(8,128)S(1)} collective-permute-done((f32[1,128,128]{2,1,0:T(8,128)S(1)}, f32[1,128,128]{2,1,0:T(8,128)S(1)}, u32[]{:S(2)}, u32[]{:S(2)}) %collective-permute-start.3) | collective-permute-done | bytes 65568 | tf_op jit(solution)/shard_map/ppermute | solution.py:358
  18.9 1.8 %collective-permute-start.5 = (f32[2,128,128]{2,1,0:T(8,128)S(1)}, f32[2,128,128]{2,1,0:T(8,128)S(1)}, u32[]{:S(2)}, u32[]{:S(2)}) collective-permute-start(f32[2,128,128]{2,1,0:T(8,128)S(1)} %get-tuple-element.61), channel_id=1, source_target_pairs={{0,4},{4,0},{8,12},{12,8},{16,20},{20,16},{24,28},{28,24},{1,5},{5... | collective-permute-start | bytes 393224 | tf_op jit(solution)/shard_map/ppermute | solution.py:358
  20.7 1.4 %collective-permute-start.6 = (f32[2,128,128]{2,1,0:T(8,128)S(1)}, f32[2,128,128]{2,1,0:T(8,128)S(1)}, u32[]{:S(2)}, u32[]{:S(2)}) collective-permute-start(f32[2,128,128]{2,1,0:T(8,128)S(1)} %get-tuple-element.67), channel_id=1, source_target_pairs={{0,12},{4,8},{8,4},{12,0},{16,28},{20,24},{24,20},{28,16},{1,13},{... | collective-permute-start | bytes 393224 | tf_op jit(solution)/shard_map/ppermute | solution.py:358
  22.1 0.4 %collective-permute-start.4 = (f32[2,128,128]{2,1,0:T(8,128)S(1)}, f32[2,128,128]{2,1,0:T(8,128)S(1)}, u32[]{:S(2)}, u32[]{:S(2)}) collective-permute-start(f32[2,128,128]{2,1,0:T(8,128)S(1)} %get-tuple-element.55), channel_id=1, source_target_pairs={{0,8},{4,12},{8,0},{12,4},{16,24},{20,28},{24,16},{28,20},{1,9},{5... | collective-permute-start | bytes 393224 | tf_op jit(solution)/shard_map/ppermute | solution.py:358
  22.5 1.5 %head_outputs.6 = (bf16[1024,512]{1,0:T(8,128)(2,1)}, bf16[1024,512]{1,0:T(8,128)(2,1)}, bf16[1024,512]{1,0:T(8,128)(2,1)}, bf16[1024,512]{1,0:T(8,128)(2,1)}) custom-call(s32[1]{0:T(128)} %bitcast.me_ref, bf16[1024,512]{1,0:T(8,128)(2,1)S(1)} %copy-done, bf16[1024,512]{1,0:T(8,128)(2,1)S(1)} %copy-done.1, bf16[1024,512]{1,0:T(8,128)(2,1)S(1)} %copy-done.2, ...), custom_call_target="tpu_custom_call" | custom-call | flops 268435456 | bytes 1048576 | tf_op jit(solution)/shard_map/head_outputs/pallas_call | solution.py:241
  23.9 1.1 %collective-permute-done.5.refs_0_ = f32[2,128,128]{2,1,0:T(8,128)S(1)} collective-permute-done((f32[2,128,128]{2,1,0:T(8,128)S(1)}, f32[2,128,128]{2,1,0:T(8,128)S(1)}, u32[]{:S(2)}, u32[]{:S(2)}) %collective-permute-start.5) | collective-permute-done | bytes 131104 | tf_op jit(solution)/shard_map/ppermute | solution.py:358
  25.1 0.7 %head_outputs.4.refs_6_ = bf16[4,1024,128]{2,1,0:T(8,128)(2,1)S(1)} custom-call(s32[1]{0:T(128)} %bitcast.me_ref, bf16[1024,512]{1,0:T(8,128)(2,1)S(1)} %copy-done, bf16[1024,512]{1,0:T(8,128)(2,1)S(1)} %copy-done.1, bf16[1024,512]{1,0:T(8,128)(2,1)S(1)} %copy-done.2, bf16[1024,512]{1,0:T(8,128)(2,1)S(1)} %copy-done.3, ...), custom_call_target="tpu_custom_call" | custom-call | flops 268435456 | bytes 1048576 | tf_op jit(solution)/shard_map/head_outputs/pallas_call | solution.py:241
  25.8 0.8 %collective-permute-done.6.refs_0_ = f32[2,128,128]{2,1,0:T(8,128)S(1)} collective-permute-done((f32[2,128,128]{2,1,0:T(8,128)S(1)}, f32[2,128,128]{2,1,0:T(8,128)S(1)}, u32[]{:S(2)}, u32[]{:S(2)}) %collective-permute-start.6) | collective-permute-done | bytes 131104 | tf_op jit(solution)/shard_map/ppermute | solution.py:358
  26.6 0.7 %head_outputs.5.refs_7_ = bf16[4,1024,128]{2,1,0:T(8,128)(2,1)S(1)} custom-call(s32[1]{0:T(128)} %bitcast.me_ref, bf16[1024,512]{1,0:T(8,128)(2,1)S(1)} %copy-done, bf16[1024,512]{1,0:T(8,128)(2,1)S(1)} %copy-done.1, bf16[1024,512]{1,0:T(8,128)(2,1)S(1)} %copy-done.2, bf16[1024,512]{1,0:T(8,128)(2,1)S(1)} %copy-done.3, ...), custom_call_target="tpu_custom_call" | custom-call | flops 268435456 | bytes 1048576 | tf_op jit(solution)/shard_map/head_outputs/pallas_call | solution.py:241
  27.3 0.0 collective-permute-done.4.refs_0_
  27.3 1.8 %head_outputs.7 = (bf16[1024,512]{1,0:T(8,128)(2,1)}, bf16[1024,512]{1,0:T(8,128)(2,1)}, bf16[1024,512]{1,0:T(8,128)(2,1)}, bf16[1024,512]{1,0:T(8,128)(2,1)}) custom-call(s32[1]{0:T(128)} %bitcast.me_ref, bf16[1024,512]{1,0:T(8,128)(2,1)S(1)} %copy-done, ...), custom_call_target="tpu_custom_call", output_to_operand_aliasing={{0}: (13, {}), {1}: (14, {}), {2}: (15, {}), {3}: (16, {})} | custom-call | flops 268435456 | bytes 1048576 | tf_op jit(solution)/shard_map/head_outputs/pallas_call | solution.py:241
  (10 shorter events, 0.1 us)
Async XLA Ops:
  0.6 7.5 %copy-start.1 = (bf16[1024,512]{1,0:T(8,128)(2,1)S(1)}, bf16[1024,512]{1,0:T(8,128)(2,1)}, u32[]{:S(2)}) copy-start(bf16[1024,512]{1,0:T(8,128)(2,1)} %k_ref.13) | copy-start | bytes 3145732
  0.6 7.5 %copy-start.2 = (bf16[1024,512]{1,0:T(8,128)(2,1)S(1)}, bf16[1024,512]{1,0:T(8,128)(2,1)}, u32[]{:S(2)}) copy-start(bf16[1024,512]{1,0:T(8,128)(2,1)} %v_ref.13) | copy-start | bytes 3145732
  0.7 7.5 %copy-start.3 = (bf16[1024,512]{1,0:T(8,128)(2,1)S(1)}, bf16[1024,512]{1,0:T(8,128)(2,1)}, u32[]{:S(2)}) copy-start(bf16[1024,512]{1,0:T(8,128)(2,1)} %d_ref.13) | copy-start | bytes 3145732
  3.1 5.1 %copy-start = (bf16[1024,512]{1,0:T(8,128)(2,1)S(1)}, bf16[1024,512]{1,0:T(8,128)(2,1)}, u32[]{:S(2)}) copy-start(bf16[1024,512]{1,0:T(8,128)(2,1)} %q_ref.13) | copy-start | bytes 3145732
  3.1 8.9 %collective-permute-start = (f32[2,128,128]{2,1,0:T(8,128)S(1)}, f32[2,128,128]{2,1,0:T(8,128)S(1)}, u32[]{:S(2)}, u32[]{:S(2)}) collective-permute-start(f32[2,128,128]{2,1,0:T(8,128)S(1)} %get-tuple-element.48), channel_id=1, source_target_pairs={{0,12},{4,8},{8,4},{12,0},{16,28},{20,24},{24,20},{28,16},{1,13},{... | collective-permute-start | bytes 393224 | tf_op jit(solution)/shard_map/ppermute | solution.py:358
  7.1 6.5 %collective-permute-start.1 = (f32[2,128,128]{2,1,0:T(8,128)S(1)}, f32[2,128,128]{2,1,0:T(8,128)S(1)}, u32[]{:S(2)}, u32[]{:S(2)}) collective-permute-start(f32[2,128,128]{2,1,0:T(8,128)S(1)} %get-tuple-element.49), channel_id=1, source_target_pairs={{0,8},{4,12},{8,0},{12,4},{16,24},{20,28},{24,16},{28,20},{1,9},{5... | collective-permute-start | bytes 393224 | tf_op jit(solution)/shard_map/ppermute | solution.py:358
  7.9 5.7 %collective-permute-start.2 = (f32[2,128,128]{2,1,0:T(8,128)S(1)}, f32[2,128,128]{2,1,0:T(8,128)S(1)}, u32[]{:S(2)}, u32[]{:S(2)}) collective-permute-start(f32[2,128,128]{2,1,0:T(8,128)S(1)} %get-tuple-element.44.after_ref), channel_id=1, source_target_pairs={{0,4},{4,0},{8,12},{12,8},{16,20},{20,16},{24,28},{28,24},{1,5},{5... | collective-permute-start | bytes 393224 | tf_op jit(solution)/shard_map/ppermute | solution.py:358
  13.6 5.3 %collective-permute-start.3 = (f32[1,128,128]{2,1,0:T(8,128)S(1)}, f32[1,128,128]{2,1,0:T(8,128)S(1)}, u32[]{:S(2)}, u32[]{:S(2)}) collective-permute-start(f32[1,128,128]{2,1,0:T(8,128)S(1)} %pick_state.1.after_ref), channel_id=1, source_target_pairs={{0,16},{4,20},{8,24},{12,28},{16,0},{20,4},{24,8},{28,12},{1,17},{... | collective-permute-start | bytes 196616 | tf_op jit(solution)/shard_map/ppermute | solution.py:358
  18.9 6.2 %collective-permute-start.5 = (f32[2,128,128]{2,1,0:T(8,128)S(1)}, f32[2,128,128]{2,1,0:T(8,128)S(1)}, u32[]{:S(2)}, u32[]{:S(2)}) collective-permute-start(f32[2,128,128]{2,1,0:T(8,128)S(1)} %get-tuple-element.61), channel_id=1, source_target_pairs={{0,4},{4,0},{8,12},{12,8},{16,20},{20,16},{24,28},{28,24},{1,5},{5... | collective-permute-start | bytes 393224 | tf_op jit(solution)/shard_map/ppermute | solution.py:358
  20.7 5.9 %collective-permute-start.6 = (f32[2,128,128]{2,1,0:T(8,128)S(1)}, f32[2,128,128]{2,1,0:T(8,128)S(1)}, u32[]{:S(2)}, u32[]{:S(2)}) collective-permute-start(f32[2,128,128]{2,1,0:T(8,128)S(1)} %get-tuple-element.67), channel_id=1, source_target_pairs={{0,12},{4,8},{8,4},{12,0},{16,28},{20,24},{24,20},{28,16},{1,13},{... | collective-permute-start | bytes 393224 | tf_op jit(solution)/shard_map/ppermute | solution.py:358
  22.1 5.2 %collective-permute-start.4 = (f32[2,128,128]{2,1,0:T(8,128)S(1)}, f32[2,128,128]{2,1,0:T(8,128)S(1)}, u32[]{:S(2)}, u32[]{:S(2)}) collective-permute-start(f32[2,128,128]{2,1,0:T(8,128)S(1)} %get-tuple-element.55), channel_id=1, source_target_pairs={{0,8},{4,12},{8,0},{12,4},{16,24},{20,28},{24,16},{28,20},{1,9},{5... | collective-permute-start | bytes 393224 | tf_op jit(solution)/shard_map/ppermute | solution.py:358

commit v7 on v6

--- a/solution.py
+++ b/solution.py
@@ -216,10 +216,14 @@
             rows = source[at, columns]
             value = local[at, :] + product(rows, hi) + product(rows, lo)
             stage[i, at, :] = (factor * value).astype(BF16)
-        if last is not None:
-            copy = pltpu.make_async_copy(stage.at[i], outs[i].at[:, columns], sems.at[len(earlier), i])
-            copy.start()
-            copies.append(copy)
+            if last is not None and (c + 1) % (chunks // 2) == 0:
+                half = (c + 1) // (chunks // 2) - 1
+                part = slice(half * (chunks // 2) * CHUNK, (c + 1) * CHUNK)
+                copy = pltpu.make_async_copy(
+                    stage.at[i, part], outs[i].at[part, columns], sems.at[len(earlier) + half, i]
+                )
+                copy.start()
+                copies.append(copy)
     for copy in copies:
         copy.wait()
 
@@ -235,7 +239,7 @@
         scratch, aliases = [], {}
     else:
         out_shape, out_specs = [jax.ShapeDtypeStruct((length, columns), BF16)] * 4, [HBM] * 4
-        scratch = [pltpu.VMEM(staging, BF16), pltpu.SemaphoreType.DMA((len(earlier) + 1, 4))]
+        scratch = [pltpu.VMEM(staging, BF16), pltpu.SemaphoreType.DMA((len(earlier) + 2, 4))]
         aliases = {len(inputs) + i: i for i in range(len(outs))}
         in_specs += [HBM] * len(outs)
     return pl.pallas_call(

time: 29.3 us -> 29.4 us (level)
  no operation moved by 1% of the time
where the time goes in v7:
time: 29.4 us; the launch traced here: 29.2 us
  Pallas kernels  12.8 us (44%)
  starting transfers between devices  11 us (37%)
  waiting for transfers between devices  4.68 us (16%)
  between operations  0.77 us (3%)
    ppermute x7, starting transfers between devices, swap(): lax.ppermute(value, 'ctx', [(i, i ^ bit) for i in range(lax.axis_size('ct...  11 us
    pallas_call x3, Pallas kernels, local_products(): pl.pallas_call(functools.partial(local_kernel, ks), out_shape=[jax.ShapeD...  5.03 us
    pallas_call x4, Pallas kernels, head_outputs(): pl.pallas_call(functools.partial(final_kernel, factor, which, len(given),...  4.84 us
    ppermute x7, waiting for transfers between devices, swap(): lax.ppermute(value, 'ctx', [(i, i ^ bit) for i in range(lax.axis_size('ct...  4.68 us
    pallas_call x1, Pallas kernels, head_states(): pl.pallas_call(functools.partial(states_kernel, ks, extra), out_shape=sta...  2.4 us
  transfers between devices with their start and end apart: 7, of which 4 were waited for; matrix products, arithmetic and copies ran while one was open for 0% of the time, Pallas kernels for 29%

profile of v7, /device:TPU:0, one launch (start us, length us, event | category | flops | bytes accessed | tf_op | source)
XLA Modules:
  0.0 29.2 jit_solution(15274485637151906530)
XLA Ops:
  0.7 2.4 %head_states.1 = (f32[2,128,128]{2,1,0:T(8,128)S(1)}, f32[4,2,128,128]{3,2,1,0:T(8,128)S(1)}, f32[2,128,128]{2,1,0:T(8,128)S(1)}, f32[4,2,128,128]{3,2,1,0:T(8,128)S(1)}, bf16[1,4,1024,128]{3,2,1,0:T(8,128)(2,1)S(1)}) custom-call(s32[1]{0:T(128)} %bitcast.me_ref, bf16[1024,512]{1,0:T(8,128)(2,1)} %q_ref.13, bf16[1024,512]{1,0:T(8,128)(2,1)} %k_ref.13, ...), custom_call_target="tpu_custom_call" | custom-call | flops 134217728 | bytes 3145728 | tf_op jit(solution)/shard_map/head_states/pallas_call | solution.py:99
  3.1 0.0 copy-start
  3.1 4.0 %collective-permute-start = (f32[2,128,128]{2,1,0:T(8,128)S(1)}, f32[2,128,128]{2,1,0:T(8,128)S(1)}, u32[]{:S(2)}, u32[]{:S(2)}) collective-permute-start(f32[2,128,128]{2,1,0:T(8,128)S(1)} %get-tuple-element.48), channel_id=1, source_target_pairs={{0,12},{4,8},{8,4},{12,0},{16,28},{20,24},{24,20},{28,16},{1,13},{... | collective-permute-start | bytes 393224 | tf_op jit(solution)/shard_map/ppermute | solution.py:362
  7.1 0.4 %collective-permute-start.1 = (f32[2,128,128]{2,1,0:T(8,128)S(1)}, f32[2,128,128]{2,1,0:T(8,128)S(1)}, u32[]{:S(2)}, u32[]{:S(2)}) collective-permute-start(f32[2,128,128]{2,1,0:T(8,128)S(1)} %get-tuple-element.49), channel_id=1, source_target_pairs={{0,8},{4,12},{8,0},{12,4},{16,24},{20,28},{24,16},{28,20},{1,9},{5... | collective-permute-start | bytes 393224 | tf_op jit(solution)/shard_map/ppermute | solution.py:362
  7.6 0.3 %held_states.1 = (f32[2,128,128]{2,1,0:T(8,128)S(1)}, f32[4,2,128,128]{3,2,1,0:T(8,128)S(1)}) custom-call(bf16[1,4,1024,128]{3,2,1,0:T(8,128)(2,1)S(1)} %get-tuple-element.43.held_ref), custom_call_target="tpu_custom_call" | custom-call | flops 67108864 | bytes 1048576 | tf_op jit(solution)/shard_map/held_states/pallas_call | solution.py:121
  7.9 0.3 collective-permute-start.2
  8.2 2.5 %local_products.3 = (f32[1024,128]{1,0:T(8,128)S(1)}, f32[1024,128]{1,0:T(8,128)S(1)}, f32[1024,128]{1,0:T(8,128)S(1)}, f32[1024,128]{1,0:T(8,128)S(1)}, f32[102...) custom-call(s32[1]{0:T(128)} %bitcast.me_ref, ...), custom_call_target="tpu_custom_call" | custom-call | flops 1073741824 | bytes 2097152 | tf_op jit(solution)/shard_map/local_products/pallas_call | solution.py:164
  10.7 1.3 %local_products.4 = (f32[1024,128]{1,0:T(8,128)S(1)}, f32[1024,128]{1,0:T(8,128)S(1)}, f32[1024,128]{1,0:T(8,128)S(1)}, f32[1024,128]{1,0:T(8,128)S(1)}, f32[8,128]{1,0:T(8,128)S(1)}) custom-call(s32[1]{0:T(128)} %bitcast.me_ref, f32[8,128]{1,0:T(8,128)S(1)} %get-tuple-element.45.after_ref, bf16[1024,512]{1,0:T(8,128)(2,1)S(1)} %copy-done, ...), custom_call_target="tpu_custom_call" | custom-call | flops 536870912 | bytes 1048576 | tf_op jit(solution)/shard_map/local_products/pallas_call | solution.py:164
  11.9 0.0 collective-permute-done.refs_1_
  12.0 1.6 %collective-permute-done.1.refs_2_ = f32[2,128,128]{2,1,0:T(8,128)S(1)} collective-permute-done((f32[2,128,128]{2,1,0:T(8,128)S(1)}, f32[2,128,128]{2,1,0:T(8,128)S(1)}, u32[]{:S(2)}, u32[]{:S(2)}) %collective-permute-start.1) | collective-permute-done | bytes 131104 | tf_op jit(solution)/shard_map/ppermute | solution.py:362
  13.6 2.7 %collective-permute-start.3 = (f32[1,128,128]{2,1,0:T(8,128)S(1)}, f32[1,128,128]{2,1,0:T(8,128)S(1)}, u32[]{:S(2)}, u32[]{:S(2)}) collective-permute-start(f32[1,128,128]{2,1,0:T(8,128)S(1)} %pick_state.1.after_ref), channel_id=1, source_target_pairs={{0,16},{4,20},{8,24},{12,28},{16,0},{20,4},{24,8},{28,12},{1,17},{... | collective-permute-start | bytes 196616 | tf_op jit(solution)/shard_map/ppermute | solution.py:362
  16.3 0.1 quad_parts.1
  16.4 1.3 %local_products.5 = (f32[1024,128]{1,0:T(8,128)S(1)}, f32[1024,128]{1,0:T(8,128)S(1)}, f32[1024,128]{1,0:T(8,128)S(1)}, f32[1024,128]{1,0:T(8,128)S(1)}, f32[8,128]{1,0:T(8,128)S(1)}) custom-call(s32[1]{0:T(128)} %bitcast.me_ref, f32[2,128,128]{2,1,0:T(8,128)S(1)} %get-tuple-element.50.after_ref.refs_0_, bf16[1024,512]{1,0:T(8,128)(2,1)S(1)} %copy-done, ...), custom_call_target="tpu_custom_call" | custom-call | flops 536870912 | bytes 1048576 | tf_op jit(solution)/shard_map/local_products/pallas_call | solution.py:164
  17.7 1.2 %collective-permute-done.3.base_ref.refs_1_ = f32[1,128,128]{2,1,0:T(8,128)S(1)} collective-permute-done((f32[1,128,128]{2,1,0:T(8,128)S(1)}, f32[1,128,128]{2,1,0:T(8,128)S(1)}, u32[]{:S(2)}, u32[]{:S(2)}) %collective-permute-start.3) | collective-permute-done | bytes 65568 | tf_op jit(solution)/shard_map/ppermute | solution.py:362
  18.9 1.8 %collective-permute-start.5 = (f32[2,128,128]{2,1,0:T(8,128)S(1)}, f32[2,128,128]{2,1,0:T(8,128)S(1)}, u32[]{:S(2)}, u32[]{:S(2)}) collective-permute-start(f32[2,128,128]{2,1,0:T(8,128)S(1)} %get-tuple-element.61), channel_id=1, source_target_pairs={{0,4},{4,0},{8,12},{12,8},{16,20},{20,16},{24,28},{28,24},{1,5},{5... | collective-permute-start | bytes 393224 | tf_op jit(solution)/shard_map/ppermute | solution.py:362
  20.7 1.4 %collective-permute-start.6 = (f32[2,128,128]{2,1,0:T(8,128)S(1)}, f32[2,128,128]{2,1,0:T(8,128)S(1)}, u32[]{:S(2)}, u32[]{:S(2)}) collective-permute-start(f32[2,128,128]{2,1,0:T(8,128)S(1)} %get-tuple-element.67), channel_id=1, source_target_pairs={{0,12},{4,8},{8,4},{12,0},{16,28},{20,24},{24,20},{28,16},{1,13},{... | collective-permute-start | bytes 393224 | tf_op jit(solution)/shard_map/ppermute | solution.py:362
  22.1 0.4 %collective-permute-start.4 = (f32[2,128,128]{2,1,0:T(8,128)S(1)}, f32[2,128,128]{2,1,0:T(8,128)S(1)}, u32[]{:S(2)}, u32[]{:S(2)}) collective-permute-start(f32[2,128,128]{2,1,0:T(8,128)S(1)} %get-tuple-element.55), channel_id=1, source_target_pairs={{0,8},{4,12},{8,0},{12,4},{16,24},{20,28},{24,16},{28,20},{1,9},{5... | collective-permute-start | bytes 393224 | tf_op jit(solution)/shard_map/ppermute | solution.py:362
  22.5 1.5 %head_outputs.6 = (bf16[1024,512]{1,0:T(8,128)(2,1)}, bf16[1024,512]{1,0:T(8,128)(2,1)}, bf16[1024,512]{1,0:T(8,128)(2,1)}, bf16[1024,512]{1,0:T(8,128)(2,1)}) custom-call(s32[1]{0:T(128)} %bitcast.me_ref, bf16[1024,512]{1,0:T(8,128)(2,1)S(1)} %copy-done, bf16[1024,512]{1,0:T(8,128)(2,1)S(1)} %copy-done.1, bf16[1024,512]{1,0:T(8,128)(2,1)S(1)} %copy-done.2, ...), custom_call_target="tpu_custom_call" | custom-call | flops 268435456 | bytes 1048576 | tf_op jit(solution)/shard_map/head_outputs/pallas_call | solution.py:245
  23.9 1.1 %collective-permute-done.5.refs_0_ = f32[2,128,128]{2,1,0:T(8,128)S(1)} collective-permute-done((f32[2,128,128]{2,1,0:T(8,128)S(1)}, f32[2,128,128]{2,1,0:T(8,128)S(1)}, u32[]{:S(2)}, u32[]{:S(2)}) %collective-permute-start.5) | collective-permute-done | bytes 131104 | tf_op jit(solution)/shard_map/ppermute | solution.py:362
  25.1 0.7 %head_outputs.4.refs_6_ = bf16[4,1024,128]{2,1,0:T(8,128)(2,1)S(1)} custom-call(s32[1]{0:T(128)} %bitcast.me_ref, bf16[1024,512]{1,0:T(8,128)(2,1)S(1)} %copy-done, bf16[1024,512]{1,0:T(8,128)(2,1)S(1)} %copy-done.1, bf16[1024,512]{1,0:T(8,128)(2,1)S(1)} %copy-done.2, bf16[1024,512]{1,0:T(8,128)(2,1)S(1)} %copy-done.3, ...), custom_call_target="tpu_custom_call" | custom-call | flops 268435456 | bytes 1048576 | tf_op jit(solution)/shard_map/head_outputs/pallas_call | solution.py:245
  25.8 0.8 %collective-permute-done.6.refs_0_ = f32[2,128,128]{2,1,0:T(8,128)S(1)} collective-permute-done((f32[2,128,128]{2,1,0:T(8,128)S(1)}, f32[2,128,128]{2,1,0:T(8,128)S(1)}, u32[]{:S(2)}, u32[]{:S(2)}) %collective-permute-start.6) | collective-permute-done | bytes 131104 | tf_op jit(solution)/shard_map/ppermute | solution.py:362
  26.6 0.7 %head_outputs.5.refs_7_ = bf16[4,1024,128]{2,1,0:T(8,128)(2,1)S(1)} custom-call(s32[1]{0:T(128)} %bitcast.me_ref, bf16[1024,512]{1,0:T(8,128)(2,1)S(1)} %copy-done, bf16[1024,512]{1,0:T(8,128)(2,1)S(1)} %copy-done.1, bf16[1024,512]{1,0:T(8,128)(2,1)S(1)} %copy-done.2, bf16[1024,512]{1,0:T(8,128)(2,1)S(1)} %copy-done.3, ...), custom_call_target="tpu_custom_call" | custom-call | flops 268435456 | bytes 1048576 | tf_op jit(solution)/shard_map/head_outputs/pallas_call | solution.py:245
  27.3 0.0 collective-permute-done.4.refs_0_
  27.3 1.9 %head_outputs.7 = (bf16[1024,512]{1,0:T(8,128)(2,1)}, bf16[1024,512]{1,0:T(8,128)(2,1)}, bf16[1024,512]{1,0:T(8,128)(2,1)}, bf16[1024,512]{1,0:T(8,128)(2,1)}) custom-call(s32[1]{0:T(128)} %bitcast.me_ref, bf16[1024,512]{1,0:T(8,128)(2,1)S(1)} %copy-done, ...), custom_call_target="tpu_custom_call", output_to_operand_aliasing={{0}: (13, {}), {1}: (14, {}), {2}: (15, {}), {3}: (16, {})} | custom-call | flops 268435456 | bytes 1048576 | tf_op jit(solution)/shard_map/head_outputs/pallas_call | solution.py:245
  (10 shorter events, 0.1 us)
Async XLA Ops:
  0.6 7.5 %copy-start.1 = (bf16[1024,512]{1,0:T(8,128)(2,1)S(1)}, bf16[1024,512]{1,0:T(8,128)(2,1)}, u32[]{:S(2)}) copy-start(bf16[1024,512]{1,0:T(8,128)(2,1)} %k_ref.13) | copy-start | bytes 3145732
  0.6 7.5 %copy-start.2 = (bf16[1024,512]{1,0:T(8,128)(2,1)S(1)}, bf16[1024,512]{1,0:T(8,128)(2,1)}, u32[]{:S(2)}) copy-start(bf16[1024,512]{1,0:T(8,128)(2,1)} %v_ref.13) | copy-start | bytes 3145732
  0.7 7.5 %copy-start.3 = (bf16[1024,512]{1,0:T(8,128)(2,1)S(1)}, bf16[1024,512]{1,0:T(8,128)(2,1)}, u32[]{:S(2)}) copy-start(bf16[1024,512]{1,0:T(8,128)(2,1)} %d_ref.13) | copy-start | bytes 3145732
  3.1 5.1 %copy-start = (bf16[1024,512]{1,0:T(8,128)(2,1)S(1)}, bf16[1024,512]{1,0:T(8,128)(2,1)}, u32[]{:S(2)}) copy-start(bf16[1024,512]{1,0:T(8,128)(2,1)} %q_ref.13) | copy-start | bytes 3145732
  3.1 8.9 %collective-permute-start = (f32[2,128,128]{2,1,0:T(8,128)S(1)}, f32[2,128,128]{2,1,0:T(8,128)S(1)}, u32[]{:S(2)}, u32[]{:S(2)}) collective-permute-start(f32[2,128,128]{2,1,0:T(8,128)S(1)} %get-tuple-element.48), channel_id=1, source_target_pairs={{0,12},{4,8},{8,4},{12,0},{16,28},{20,24},{24,20},{28,16},{1,13},{... | collective-permute-start | bytes 393224 | tf_op jit(solution)/shard_map/ppermute | solution.py:362
  7.1 6.5 %collective-permute-start.1 = (f32[2,128,128]{2,1,0:T(8,128)S(1)}, f32[2,128,128]{2,1,0:T(8,128)S(1)}, u32[]{:S(2)}, u32[]{:S(2)}) collective-permute-start(f32[2,128,128]{2,1,0:T(8,128)S(1)} %get-tuple-element.49), channel_id=1, source_target_pairs={{0,8},{4,12},{8,0},{12,4},{16,24},{20,28},{24,16},{28,20},{1,9},{5... | collective-permute-start | bytes 393224 | tf_op jit(solution)/shard_map/ppermute | solution.py:362
  7.9 5.7 %collective-permute-start.2 = (f32[2,128,128]{2,1,0:T(8,128)S(1)}, f32[2,128,128]{2,1,0:T(8,128)S(1)}, u32[]{:S(2)}, u32[]{:S(2)}) collective-permute-start(f32[2,128,128]{2,1,0:T(8,128)S(1)} %get-tuple-element.44.after_ref), channel_id=1, source_target_pairs={{0,4},{4,0},{8,12},{12,8},{16,20},{20,16},{24,28},{28,24},{1,5},{5... | collective-permute-start | bytes 393224 | tf_op jit(solution)/shard_map/ppermute | solution.py:362
  13.6 5.3 %collective-permute-start.3 = (f32[1,128,128]{2,1,0:T(8,128)S(1)}, f32[1,128,128]{2,1,0:T(8,128)S(1)}, u32[]{:S(2)}, u32[]{:S(2)}) collective-permute-start(f32[1,128,128]{2,1,0:T(8,128)S(1)} %pick_state.1.after_ref), channel_id=1, source_target_pairs={{0,16},{4,20},{8,24},{12,28},{16,0},{20,4},{24,8},{28,12},{1,17},{... | collective-permute-start | bytes 196616 | tf_op jit(solution)/shard_map/ppermute | solution.py:362
  18.9 6.2 %collective-permute-start.5 = (f32[2,128,128]{2,1,0:T(8,128)S(1)}, f32[2,128,128]{2,1,0:T(8,128)S(1)}, u32[]{:S(2)}, u32[]{:S(2)}) collective-permute-start(f32[2,128,128]{2,1,0:T(8,128)S(1)} %get-tuple-element.61), channel_id=1, source_target_pairs={{0,4},{4,0},{8,12},{12,8},{16,20},{20,16},{24,28},{28,24},{1,5},{5... | collective-permute-start | bytes 393224 | tf_op jit(solution)/shard_map/ppermute | solution.py:362
  20.7 5.9 %collective-permute-start.6 = (f32[2,128,128]{2,1,0:T(8,128)S(1)}, f32[2,128,128]{2,1,0:T(8,128)S(1)}, u32[]{:S(2)}, u32[]{:S(2)}) collective-permute-start(f32[2,128,128]{2,1,0:T(8,128)S(1)} %get-tuple-element.67), channel_id=1, source_target_pairs={{0,12},{4,8},{8,4},{12,0},{16,28},{20,24},{24,20},{28,16},{1,13},{... | collective-permute-start | bytes 393224 | tf_op jit(solution)/shard_map/ppermute | solution.py:362
  22.1 5.2 %collective-permute-start.4 = (f32[2,128,128]{2,1,0:T(8,128)S(1)}, f32[2,128,128]{2,1,0:T(8,128)S(1)}, u32[]{:S(2)}, u32[]{:S(2)}) collective-permute-start(f32[2,128,128]{2,1,0:T(8,128)S(1)} %get-tuple-element.55), channel_id=1, source_target_pairs={{0,8},{4,12},{8,0},{12,4},{16,24},{20,28},{24,16},{28,20},{1,9},{5... | collective-permute-start | bytes 393224 | tf_op jit(solution)/shard_map/ppermute | solution.py:362
